TPU v7x, 32 devices: a whole 2x2x4 slice. The times are simulated.
32 devices in a mesh: grp: 1, gx: 8 (over z, core), gy: 4 (over y, x).
Axes of the slice: x: 2, y: 2, z: 4, core: 2. Of those that a mesh axis runs over, the one named last changes fastest.
Arguments:
- features: bfloat16 [20, 64, 128, 128], P(None, ('grp', 'gx'), 'gy'), may hold values from -6 to 6
- spectral_weight: float32 [2, 20, 20, 8, 128, 64], P(None, None, None, 'gy', 'gx'), may hold values from -6 to 6
- conv_weight: bfloat16 [3, 27, 20, 20], replicated, may hold values from -0.75 to 0.75
- point_weight: bfloat16 [20, 20], replicated, may hold values from -1.25 to 1.25
Outputs:
- layer_output: bfloat16 [20, 64, 128, 128], P(None, ('grp', 'gx'), 'gy')
All inputs are finite; a program needn't handle non-finite values.
Results may differ from a plain program's by a relative error of at most 0.014.
Values may be sent and summed in bfloat16 or wider, within the bound.
No kernel may reach another device: no remote copies, remote signals or barrier semaphores. Data moves between devices by JAX's collectives and lax.ppermute only.
A program may use at most 128 MiB of HBM per device.

v0:
```python
import functools
import math

import jax
import jax.numpy as jnp
import numpy as np
from jax import lax
from jax.experimental import pallas as pl
from jax.experimental.pallas import tpu as pltpu
from jax.sharding import PartitionSpec as P

LANES = 128
BF16 = jnp.bfloat16
F32 = jnp.float32
MIB = 1024 * 1024


def dot(left, right):
    return jnp.dot(left, right, preferred_element_type=F32)


def signed_modes(count):
    position = np.arange(count)
    return np.where(position < count // 2, position, position - count)


def phase(frequency, length):
    index = np.mod(frequency[:, None] * np.arange(length)[None, :], length)
    angle = index.astype(np.float32) * np.float32(2.0 * math.pi / length)
    return (
        np.cos(angle).astype(BF16).astype(np.float32),
        np.sin(angle).astype(BF16).astype(np.float32),
    )


def const(array):
    return np.asarray(array, np.float32).astype(BF16)


class Plan:
    def __init__(self, features, spectral_weight, devices_x, devices_y):
        self.channels, self.cx, self.cy, self.cz = features
        self.dx, self.dy = devices_x, devices_y
        self.kz, self.ky, self.kx = spectral_weight[3:]
        self.gx, self.gy = self.cx * self.dx, self.cy * self.dy
        self.my = self.ky * self.dx
        self.mz = self.kz * self.dy
        self.unit = 2 * self.kz * self.cx
        self.groups = LANES // self.unit
        self.cg = self.channels // self.groups

    def forward_z(self):
        cos, sin = phase(np.arange(self.mz), self.cz)
        table = np.stack([cos, -sin], 0).reshape(2, self.dy, self.kz, self.cz)
        out = np.einsum("pdkz,xw->xzdpkw", table, np.eye(self.cx))
        return const(out.reshape(self.cx * self.cz, self.dy * self.unit))

    def inverse_z(self):
        cos, sin = phase(np.arange(self.mz), self.cz)
        scale = np.where(np.arange(self.mz) == 0, 1.0, 2.0) / float(self.gx * self.gy * self.cz)
        table = np.stack([cos, -sin], 0) * scale[None, :, None]
        table = table.reshape(2, self.dy, self.kz, self.cz)
        out = np.einsum("pdkz,xw->dpkxwz", table, np.eye(self.cx))
        return const(out.reshape(self.dy * self.unit, self.cx * self.cz))

    def regroup(self, outer, inner):
        out = np.einsum("ac,bd,lm->abldcm", np.eye(outer), np.eye(inner), np.eye(self.unit))
        size = outer * inner * self.unit
        return const(out.reshape(size, size))

    def swap(self, sign):
        turn = np.array([[0.0, -sign], [sign, 0.0]])
        half = self.unit // 2
        return const(np.kron(np.eye(self.groups), np.kron(turn, np.eye(half))))

    def forward_y(self):
        cos, sin = phase(signed_modes(self.my), self.gy)
        return const(np.concatenate([cos, sin], 1))

    def inverse_y(self):
        cos, sin = phase(signed_modes(self.my), self.gy)
        return const(np.concatenate([cos.T, sin.T], 1))

    def forward_x(self):
        cos, sin = phase(signed_modes(self.kx), self.gx)
        turn = np.stack([np.stack([cos, -sin]), np.stack([sin, cos])])
        turn = turn.reshape(2, 2, self.kx, self.dx, self.cx)
        out = np.einsum("pqjsx,gh,kl->sgpkxhlqj", turn, np.eye(self.groups), np.eye(self.kz))
        return const(out.reshape(self.dx * LANES, self.groups * self.kz * 2 * self.kx))

    def inverse_x(self):
        cos, sin = phase(signed_modes(self.kx), self.gx)
        turn = np.stack([np.stack([cos, sin]), np.stack([-sin, cos])])
        turn = turn.reshape(2, 2, self.kx, self.dx, self.cx)
        out = np.einsum("pqjsx,gh,kl->gkpjshqlx", turn, np.eye(self.groups), np.eye(self.kz))
        return const(out.reshape(self.groups * self.kz * 2 * self.kx, self.dx * LANES))


VMEM = pl.BlockSpec(memory_space=pltpu.VMEM)
SMEM = pl.BlockSpec(memory_space=pltpu.SMEM)


def call(body, outs, inputs, scratch=(), specs=None, vmem=8, flops=1e9, moved=1e6, **kw):
    return pl.pallas_call(
        body,
        out_shape=outs,
        in_specs=specs or [VMEM] * len(inputs),
        out_specs=kw.pop("out_specs", jax.tree.map(lambda _: VMEM, outs)),
        scratch_shapes=scratch,
        compiler_params=pltpu.CompilerParams(vmem_limit_bytes=vmem * MIB),
        cost_estimate=pl.CostEstimate(
            flops=int(flops), bytes_accessed=int(moved), transcendentals=0
        ),
        **kw,
    )(*inputs)


def z_body(plan, field, table, regroup, out):
    rows = plan.channels * plan.cy
    lhs = jnp.concatenate(
        [field[:, x].reshape(rows, plan.cz) for x in range(plan.cx)], axis=1
    )
    modes = dot(lhs, table[...]).astype(BF16)
    part = plan.cg * plan.cy
    lanes = jnp.concatenate(
        [modes[g * part : (g + 1) * part] for g in range(plan.groups)], axis=1
    )
    result = dot(lanes, regroup[...]).astype(BF16)
    for d in range(plan.dy):
        out[d] = result[:, d * LANES : (d + 1) * LANES].reshape(plan.cg, plan.cy, LANES)


def y_body(plan, line, table, swap, out):
    sources, _, rows, _ = line.shape
    targets = out.shape[0]
    rows_out = out.shape[2]
    columns = []
    for c in range(plan.cg):
        value = jnp.concatenate([line[s, c] for s in range(sources)], axis=0)
        turned = dot(value, swap[...]).astype(BF16)
        columns.append(jnp.concatenate([value, turned], axis=0))
    result = dot(table[...], jnp.concatenate(columns, axis=1)).astype(BF16)
    for d in range(targets):
        for c in range(plan.cg):
            out[d, c] = result[
                d * rows_out : (d + 1) * rows_out, c * LANES : (c + 1) * LANES
            ]


def mix(plan, spec, weight, mixed):
    def step(o, carry):
        for k in range(plan.kz):
            real = jnp.zeros((plan.ky, plan.kx), F32)
            imag = jnp.zeros((plan.ky, plan.kx), F32)
            for i in range(plan.channels):
                wr = weight[0, i, o, k]
                wi = weight[1, i, o, k]
                xr = spec[0, k, i]
                xi = spec[1, k, i]
                real += xr * wr - xi * wi
                imag += xr * wi + xi * wr
            mixed[k, o] = jnp.concatenate([real, imag], axis=1)
        return carry

    lax.fori_loop(0, plan.channels, step, 0)


def x_body(plan, pencil, forward, weight, inverse, out, spec, mixed):
    rows = plan.cg * plan.ky
    kx = plan.kx
    lhs = jnp.concatenate([pencil[s].reshape(rows, LANES) for s in range(plan.dx)], axis=1)
    spectrum = dot(lhs, forward[...])
    for g in range(plan.groups):
        for k in range(plan.kz):
            for p in range(2):
                start = ((g * plan.kz + k) * 2 + p) * kx
                block = spectrum[:, start : start + kx]
                for c in range(plan.cg):
                    spec[p, k, g * plan.cg + c] = block[c * plan.ky : (c + 1) * plan.ky]
    mix(plan, spec, weight, mixed)
    back = jnp.concatenate(
        [
            mixed[k, g * plan.cg : (g + 1) * plan.cg].reshape(rows, 2 * kx).astype(BF16)
            for g in range(plan.groups)
            for k in range(plan.kz)
        ],
        axis=1,
    )
    result = dot(back, inverse[...]).astype(BF16)
    for d in range(plan.dx):
        out[d] = result[:, d * LANES : (d + 1) * LANES].reshape(plan.cg, plan.ky, LANES)


def x_stage_general(plan, pencil, weight):
    groups, cg, ky, kz, kx = plan.groups, plan.cg, plan.ky, plan.kz, plan.kx
    lhs = jnp.transpose(pencil, (1, 2, 0, 3)).reshape(cg * ky, plan.dx * LANES)
    spectrum = dot(lhs, plan.forward_x()).reshape(cg, ky, groups, kz, 2, kx)
    spectrum = jnp.transpose(spectrum, (4, 3, 2, 0, 1, 5)).reshape(2, kz, groups * cg, ky, kx)
    mixed = call(
        functools.partial(mix, plan),
        jax.ShapeDtypeStruct((kz, groups * cg, ky, 2 * kx), F32),
        (spectrum, weight),
        vmem=32,
    )
    back = jnp.transpose(mixed.reshape(kz, groups, cg, ky, 2 * kx), (2, 3, 1, 0, 4))
    back = back.reshape(cg * ky, groups * kz * 2 * kx).astype(BF16)
    back = dot(back, plan.inverse_x()).astype(BF16).reshape(cg, ky, plan.dx, LANES)
    return jnp.transpose(back, (2, 0, 1, 3))


CP = 24


def gelu(value):
    return 0.5 * value * (1.0 + lax.erf(value * (0.5**0.5)))


def pool_tables(plan):
    half = plan.cy // 2
    quarter = half // 2
    rows = np.einsum(
        "cC,yY->ycCY", np.eye(CP)[:, : plan.channels], np.kron(np.eye(quarter), np.ones((1, 2)))
    ).reshape(quarter * CP, plan.channels * half)
    rows = np.concatenate([rows, rows], 1)
    pairs = np.kron(np.eye(plan.cz), np.full((2, 1), 0.125))
    return const(rows), const(pairs)


def pool_body(plan, field, rows_table, pair_table, out):
    half = plan.cy // 2
    quarter = half // 2
    cells = plan.channels * half
    for h in range(2):
        columns = []
        for x in range(plan.cx // 2):
            columns.append(
                jnp.concatenate(
                    [
                        field[:, 2 * x + e, h * half : (h + 1) * half].reshape(cells, plan.cz)
                        for e in range(2)
                    ],
                    axis=0,
                )
            )
        summed = dot(rows_table[...], jnp.concatenate(columns, axis=1))
        blocks = []
        for x in range(plan.cx // 2):
            for j in range(quarter // 2):
                blocks.append(
                    jnp.concatenate(
                        [
                            summed[
                                (2 * j + e) * CP : (2 * j + e + 1) * CP,
                                x * plan.cz : (x + 1) * plan.cz,
                            ]
                            for e in range(2)
                        ],
                        axis=1,
                    )
                )
        block = jnp.concatenate(blocks, axis=0)
        high = block.astype(BF16)
        low = (block - high.astype(F32)).astype(BF16)
        result = dot(high, pair_table[...]) + dot(low, pair_table[...])
        index = 0
        for x in range(plan.cx // 2):
            for j in range(quarter // 2):
                out[x, h * (quarter // 2) + j] = result[index * CP : (index + 1) * CP].astype(BF16)
                index += 1


def conv_body(
    plan, flags, own, y_low, y_high, x_low, x_high, filters, point, spread, pick_o, pick_i, diag,
    fixed, third, lift, volume, partial,
):
    nx = plan.cx // 2
    ny = plan.cy // 4
    wide = ny + 4
    lane = lax.broadcasted_iota(jnp.int32, (CP, LANES), 1)
    z = lane % (LANES // 2)
    lower = lane < LANES // 2
    first_z = z == 0
    last_z = z == LANES // 2 - 1
    zero = jnp.zeros((CP, LANES), F32)

    expanded = dot(dot(pick_o[...], point[...]).astype(BF16), pick_i[...]).astype(BF16)
    wide_cols = expanded.shape[1]
    lift[:, :wide_cols] = expanded * diag[...]
    lift[:, wide_cols:] = fixed[...]

    def tile(x, j):
        if x < 3:
            return x_low[x, j]
        if x >= 3 + nx:
            return x_high[x - 3 - nx, j]
        if j < 2:
            return y_low[x - 3, j]
        if j >= 2 + ny:
            return y_high[x - 3, j - 2 - ny]
        return own[x - 3, j - 2]

    for x in range(nx + 6):
        for j in range(wide):
            volume[x, j] = tile(x, j).astype(F32)

    def layer(number, planes, tiles):
        def multiply(x, carry):
            shifted = {}
            for j in range(tiles[0] - 1, tiles[1] + 1):
                value = volume[x, j]
                versions = (
                    jnp.where(first_z, 0.0, pltpu.roll(value, 1, 1)),
                    value,
                    jnp.where(last_z, 0.0, pltpu.roll(value, LANES - 1, 1)),
                )
                shifted[j] = (versions, [pltpu.roll(v, LANES // 2, 1) for v in versions])
            columns = []
            for j in range(tiles[0], tiles[1]):
                pieces = []
                for e in range(3):
                    pieces.append(jnp.where(lower, shifted[j - 1][1][e], shifted[j][1][e]))
                for e in range(3):
                    pieces.append(shifted[j][0][e])
                for e in range(3):
                    pieces.append(jnp.where(lower, shifted[j][1][e], shifted[j + 1][1][e]))
                columns.append(jnp.concatenate(pieces, axis=0).astype(BF16))
            partial[x, :, : (tiles[1] - tiles[0]) * LANES] = dot(
                filters[number], jnp.concatenate(columns, axis=1)
            )
            return carry

        lax.fori_loop(0, planes, multiply, 0)

        def combine(x, carry):
            margin = (planes - 2 - nx) // 2
            inside = jnp.where(x < margin, flags[0], 1.0) * jnp.where(
                x >= margin + nx, flags[1], 1.0
            )
            for j in range(tiles[0], tiles[1]):
                cols = slice((j - tiles[0]) * LANES, (j - tiles[0] + 1) * LANES)
                total = (
                    partial[x, 0:CP, cols]
                    + partial[x + 1, CP : 2 * CP, cols]
                    + partial[x + 2, 2 * CP : 3 * CP, cols]
                )
                if number < 2:
                    scale = inside
                    if j < 2:
                        scale = scale * flags[2]
                    if j >= 2 + ny:
                        scale = scale * flags[3]
                    total = gelu(total).astype(BF16).astype(F32) * scale
                    volume[x, j] = total
                else:
                    up = dot(total.astype(BF16), spread[...]).astype(BF16)
                    third[x, 2 * (j - 2)] = up[:, : plan.cz]
                    third[x, 2 * (j - 2) + 1] = up[:, plan.cz :]
            return carry

        lax.fori_loop(0, planes - 2, combine, 0)

    layer(0, nx + 6, (1, ny + 3))
    for x in range(nx + 4):
        volume[x, 0] = zero
        volume[x, wide - 1] = zero
    layer(1, nx + 4, (1, ny + 3))
    layer(2, nx + 2, (2, ny + 2))


def final_body(plan, field, third, line, lift, regroup, inverse, out, lanes):
    step = pl.program_id(0)
    half = plan.cy // 2
    part = plan.cg * plan.cy

    @pl.when(step == 0)
    def _():
        gathered = jnp.concatenate(
            [line[s].reshape(part, LANES) for s in range(plan.dy)], axis=1
        )
        result = dot(gathered, regroup[...]).astype(BF16)
        width = plan.dy * plan.unit
        for g in range(plan.groups):
            lanes[g * part : (g + 1) * part] = result[:, g * width : (g + 1) * width]

    cells = plan.channels * half
    columns = []
    for e in range(2):
        for h in range(2):
            cols = third[0, h * (half // 2) : (h + 1) * (half // 2)]
            columns.append(
                jnp.concatenate(
                    [
                        field[:, e, h * half : (h + 1) * half].reshape(cells, plan.cz),
                        cols.astype(F32).reshape(half // 2 * CP, plan.cz).astype(BF16),
                    ],
                    axis=0,
                )
            )
    local = dot(lift[...], jnp.concatenate(columns, axis=1))
    spectral = dot(lanes[...], inverse[...]).reshape(plan.channels, plan.cy, 2 * plan.cz)
    for e in range(2):
        for h in range(2):
            index = e * 2 + h
            total = local[:, index * plan.cz : (index + 1) * plan.cz].reshape(
                plan.channels, half, plan.cz
            ) + spectral[:, h * half : (h + 1) * half, e * plan.cz : (e + 1) * plan.cz]
            out[:, e, h * half : (h + 1) * half] = gelu(total).astype(BF16)


def aligned(rows):
    return rows % 16 == 0


def on_device(features, spectral_weight, conv_weight, point_weight):
    devices_x = lax.axis_size("gx")
    devices_y = lax.axis_size("gy")
    plan = Plan(features.shape, spectral_weight.shape, devices_x, devices_y)
    channels, cx, cy, cz = features.shape
    shape = jax.ShapeDtypeStruct
    cg = plan.cg

    z_spec = call(
        functools.partial(z_body, plan),
        shape((devices_y, cg, cy, LANES), BF16),
        (features, plan.forward_z(), plan.regroup(plan.groups, devices_y)),
    )
    lines = lax.all_to_all(z_spec, "gy", 0, 0, tiled=True)

    rows_table, pair_table = pool_tables(plan)
    coarse = call(
        functools.partial(pool_body, plan),
        shape((cx // 2, cy // 4, CP, cz), BF16),
        (features, rows_table, pair_table),
    )
    up_y = [(i, i + 1) for i in range(devices_y - 1)]
    down_y = [(t, s) for s, t in up_y]
    y_low = lax.ppermute(coarse[:, -2:], "gy", up_y)
    y_high = lax.ppermute(coarse[:, :2], "gy", down_y)
    up_x = [(i, i + 1) for i in range(devices_x - 1)]
    down_x = [(t, s) for s, t in up_x]
    x_low = lax.ppermute(
        jnp.concatenate([y_low[-3:], coarse[-3:], y_high[-3:]], axis=1), "gx", up_x
    )
    x_high = lax.ppermute(
        jnp.concatenate([y_low[:3], coarse[:3], y_high[:3]], axis=1), "gx", down_x
    )
    here_x = lax.axis_index("gx")
    here_y = lax.axis_index("gy")
    flags = jnp.stack(
        [here_x > 0, here_x < devices_x - 1, here_y > 0, here_y < devices_y - 1]
    ).astype(F32)

    filters = jnp.pad(
        conv_weight.reshape(3, 3, 9, channels, channels),
        ((0, 0), (0, 0), (0, 0), (0, CP - channels), (0, CP - channels)),
    )
    filters = jnp.transpose(filters, (0, 1, 3, 2, 4)).reshape(3, 3 * CP, 9 * CP)
    half = cy // 2
    pick_o = const(np.kron(np.eye(channels), np.ones((half, 1))))
    pick_i = const(np.kron(np.eye(channels), np.ones((1, half))))
    diag = const(np.kron(np.ones((channels, channels)), np.eye(half)))
    fixed = const(
        np.einsum(
            "oO,yY->oyYO", np.eye(CP)[:channels], np.kron(np.eye(half // 2), np.ones((2, 1)))
        ).reshape(channels * half, half // 2 * CP)
    )
    spread = const(np.kron(np.eye(cz), np.ones((1, 2))))
    third, lift = call(
        functools.partial(conv_body, plan),
        (
            shape((cx // 2, cy // 2, CP, cz), BF16),
            shape((channels * half, channels * half + half // 2 * CP), BF16),
        ),
        (
            flags, coarse, y_low, y_high, x_low, x_high, filters, jnp.transpose(point_weight),
            spread, pick_o, pick_i, diag, fixed,
        ),
        scratch=[
            pltpu.VMEM((cx // 2 + 6, cy // 4 + 4, CP, LANES), F32),
            pltpu.VMEM((cx // 2 + 6, 3 * CP, (cy // 4 + 2) * LANES), F32),
        ],
        specs=[SMEM] + [VMEM] * 12,
        vmem=16,
        flops=6e9,
        moved=6e6,
    )

    split = aligned(plan.ky)
    y_out = (devices_x, cg, plan.ky) if split else (1, cg, plan.my)
    y_spec = call(
        functools.partial(y_body, plan),
        shape(y_out + (LANES,), BF16),
        (lines, plan.forward_y(), plan.swap(1.0)),
    )
    if not split:
        y_spec = jnp.transpose(y_spec.reshape(cg, devices_x, plan.ky, LANES), (1, 0, 2, 3))
    pencil = lax.all_to_all(y_spec, "gx", 0, 0, tiled=True)

    if split:
        back = call(
            functools.partial(x_body, plan),
            shape((devices_x, cg, plan.ky, LANES), BF16),
            (pencil, plan.forward_x(), spectral_weight, plan.inverse_x()),
            scratch=[
                pltpu.VMEM((2, plan.kz, channels, plan.ky, plan.kx), F32),
                pltpu.VMEM((plan.kz, channels, plan.ky, 2 * plan.kx), F32),
            ],
            vmem=26,
        )
    else:
        back = x_stage_general(plan, pencil, spectral_weight)
    back = lax.all_to_all(back, "gx", 0, 0, tiled=True)
    if not split:
        back = jnp.transpose(back, (1, 0, 2, 3)).reshape(1, cg, plan.my, LANES)
    y_cells = call(
        functools.partial(y_body, plan),
        shape((devices_y, cg, cy, LANES), BF16),
        (back, plan.inverse_y(), plan.swap(-1.0)),
    )
    y_cells = lax.all_to_all(y_cells, "gy", 0, 0, tiled=True)

    full = lambda array: pl.BlockSpec(array.shape, lambda s: (0,) * array.ndim)
    regroup = plan.regroup(devices_y, plan.groups)
    return call(
        functools.partial(final_body, plan),
        shape(features.shape, BF16),
        (features, third, y_cells, lift, regroup, plan.inverse_z()),
        grid=(cx // 2,),
        specs=[
            pl.BlockSpec((channels, 2, cy, cz), lambda s: (0, s, 0, 0)),
            pl.BlockSpec((1, cy // 2, CP, cz), lambda s: (s, 0, 0, 0)),
            full(y_cells),
            full(lift),
            full(regroup),
            pl.BlockSpec((devices_y * plan.unit, 2 * cz), lambda s: (0, s)),
        ],
        out_specs=pl.BlockSpec((channels, 2, cy, cz), lambda s: (0, s, 0, 0)),
        scratch=[pltpu.VMEM((channels * cy, devices_y * plan.unit), BF16)],
        vmem=12,
    )


def solution(mesh):
    in_specs = (P(None, ("grp", "gx"), "gy", None), P(None, None, None, "gy", "gx", None), P(), P())
    out_specs = P(None, ("grp", "gx"), "gy", None)
    return jax.shard_map(
        on_device, mesh=mesh, in_specs=in_specs, out_specs=out_specs, check_vma=False
    )
```

profile of v0, /device:TPU:0, one launch (start us, length us, event | category | flops | bytes accessed | tf_op | source)
XLA Modules:
  0.0 85.2 jit_solution(8659387911341299110)
XLA Ops:
  0.0 1.3 %copy-done.3 = bf16[20,8,32,128]{3,2,1,0:T(8,128)(2,1)S(1)} copy-done((bf16[20,8,32,128]{3,2,1,0:T(8,128)(2,1)S(1)}, bf16[20,8,32,128]{3,2,1,0:T(8,128)(2,1)}, u32[]{:S(2)}) %copy-start.3) | copy-done | bytes 1310744
  1.3 0.9 %copy-done.16 = bf16[192,640]{1,0:T(8,128)(2,1)S(1)} copy-done((bf16[192,640]{1,0:T(8,128)(2,1)S(1)}, bf16[192,640]{1,0:T(8,128)(2,1)}, u32[]{:S(2)}) %copy-start.16) | copy-done | bytes 245784
  2.3 0.8 copy-done.22
  3.1 0.9 %shard_map.199.own = bf16[4,8,24,128]{3,2,1,0:T(8,128)(2,1)S(1)} custom-call(bf16[20,8,32,128]{3,2,1,0:T(8,128)(2,1)S(1)} %copy-done.3, bf16[192,640]{1,0:T(8,128)(2,1)S(1)} %copy-done.16, bf16[256,128]{1,0:T(8,128)(2,1)S(1)} %copy-done.22), custom_call_target="tpu_custom_call" | custom-call | flops 1000000000 | bytes 1000000 | tf_op jit(solution)/shard_map/pallas_call | solution.py:104
  4.0 0.0 copy-start.5
  4.0 0.7 fusion.1
  4.7 4.8 %collective-permute-start = (bf16[4,2,24,128]{3,2,1,0:T(8,128)(2,1)S(1)}, bf16[4,2,24,128]{3,2,1,0:T(8,128)(2,1)S(1)}, u32[]{:S(2)}, u32[]{:S(2)}) collective-permute-start(bf16[4,2,24,128]{3,2,1,0:T(8,128)(2,1)S(1)} %get-tuple-element.12), channel_id=1, source_target_pairs={{0,1},{1,2},{2,3},{4,5},{5,6},{6,7},{8,9},{9,10},{10,11},{12,13},{... | collective-permute-start | bytes 147464 | tf_op jit(solution)/shard_map/ppermute | solution.py:437
  9.6 0.0 copy-start.26
  9.6 0.0 copy-start.24
  9.6 1.4 %collective-permute-start.1 = (bf16[4,2,24,128]{3,2,1,0:T(8,128)(2,1)}, bf16[4,2,24,128]{3,2,1,0:T(8,128)(2,1)S(1)}, u32[]{:S(2)}, u32[]{:S(2)}) collective-permute-start(bf16[4,2,24,128]{3,2,1,0:T(8,128)(2,1)} %get-tuple-element.11), channel_id=1, source_target_pairs={{1,0},{2,1},{3,2},{5,4},{6,5},{7,6},{9,8},{10,9},{11,10},{13,12},{... | collective-permute-start | bytes 147464 | tf_op jit(solution)/shard_map/ppermute | solution.py:438
  11.0 0.0 copy-done.4
  11.0 0.0 copy-done.8
  11.0 0.0 copy-done.14
  11.0 1.5 %shard_map.201 = bf16[4,5,32,128]{3,2,1,0:T(8,128)(2,1)} custom-call(bf16[20,8,32,128]{3,2,1,0:T(8,128)(2,1)S(1)} %copy-done.4, bf16[1024,128]{1,0:T(8,128)(2,1)S(1)} %copy-done.14, bf16[512,512]{1,0:T(8,128)(2,1)S(1)} %copy-done.8), custom_call_target="tpu_custom_call" | custom-call | flops 1000000000 | bytes 1000000 | tf_op jit(solution)/shard_map/pallas_call | solution.py:104
  12.5 4.9 %all-to-all-start = ((bf16[4,5,32,128]{3,2,1,0:T(8,128)(2,1)}), bf16[4,5,32,128]{3,2,1,0:T(8,128)(2,1)}, u32[]{:S(2)}, u32[]{:S(2)}) async-start(bf16[4,5,32,128]{3,2,1,0:T(8,128)(2,1)} %shard_map.201), calls=%async_computation | async-start | bytes 327680 | tf_op jit(solution)/shard_map/all_to_all | solution.py:427
  17.4 0.0 copy-done.5
  17.4 0.8 fusion
  18.1 0.0 copy-done.26
  18.1 1.4 %copy.24 = bf16[3,27,20,20]{3,2,1,0:T(8,128)(2,1)} copy(bf16[3,27,20,20]{1,3,2,0:T(8,128)(2,1)S(1)} %copy-done.26) | data formatting | bytes 129600 | tf_op args[2]
  19.5 0.0 collective-permute-done.y_low
  19.5 0.6 fusion.2
  20.1 2.6 %all-to-all-done.line = bf16[4,5,32,128]{3,2,1,0:T(8,128)(2,1)} async-done(((bf16[4,5,32,128]{3,2,1,0:T(8,128)(2,1)}), bf16[4,5,32,128]{3,2,1,0:T(8,128)(2,1)}, u32[]{:S(2)}, u32[]{:S(2)}) %all-to-all-start) | async-done | bytes 163872 | tf_op jit(solution)/shard_map/all_to_all | solution.py:427
  22.8 0.0 copy-done.24
  22.8 0.8 copy-done.20
  23.6 1.3 %shard_map.202 = bf16[8,5,16,128]{3,2,1,0:T(8,128)(2,1)S(1)} custom-call(bf16[4,5,32,128]{3,2,1,0:T(8,128)(2,1)} %all-to-all-done.line, bf16[128,256]{1,0:T(8,128)(2,1)S(1)} %copy-done.20, bf16[128,128]{1,0:T(8,128)(2,1)S(1)} %copy-done.24), custom_call_target="tpu_custom_call" | custom-call | flops 1000000000 | bytes 1000000 | tf_op jit(solution)/shard_map/pallas_call | solution.py:104
  24.9 0.0 copy-start.11
  24.9 0.6 copy-done.11
  25.5 4.9 %all-to-all-start.1 = ((bf16[8,5,16,128]{3,2,1,0:T(8,128)(2,1)}), bf16[8,5,16,128]{3,2,1,0:T(8,128)(2,1)}, u32[]{:S(2)}, u32[]{:S(2)}) async-start(bf16[8,5,16,128]{3,2,1,0:T(8,128)(2,1)} %copy-done.11), calls=%async_computation.1 | async-start | bytes 327680 | tf_op jit(solution)/shard_map/all_to_all | solution.py:497
  30.4 0.0 collective-permute-done.1.y_high
  30.4 0.6 fusion.3
  31.0 1.6 %pad_maximum_fusion.1 = bf16[3,12,24,128]{3,2,1,0:T(8,128)(2,1)} fusion(bf16[3,2,24,128]{3,2,1,0:T(8,128)(2,1)S(1)} %get-tuple-element.15, bf16[3,8,24,128]{3,2,1,0:T(8,128)(2,1)} %get-tuple-element.9, bf16[3,2,24,128]{3,2,1,0:T(8,128)(2,1)} %get-tuple-element.13), kind=kLoop, calls=%fused_computation.2 | loop fusion | flops 221184 | bytes 442368 | tf_op jit(solution)/shard_map/concatenate | solution.py:445
  32.7 1.3 %collective-permute-start.3 = (bf16[3,12,24,128]{3,2,1,0:T(8,128)(2,1)}, bf16[3,12,24,128]{3,2,1,0:T(8,128)(2,1)}, u32[]{:S(2)}, u32[]{:S(2)}) collective-permute-start(bf16[3,12,24,128]{3,2,1,0:T(8,128)(2,1)} %pad_maximum_fusion.1), channel_id=1, source_target_pairs={{4,0},{8,4},{12,8},{16,12},{20,16},{24,20},{28,24},{5,1},{9,5},{13... | collective-permute-start | bytes 663560 | tf_op jit(solution)/shard_map/ppermute | solution.py:444
  34.0 3.8 %all-to-all-done.1.pencil = bf16[8,5,16,128]{3,2,1,0:T(8,128)(2,1)} async-done(((bf16[8,5,16,128]{3,2,1,0:T(8,128)(2,1)}), bf16[8,5,16,128]{3,2,1,0:T(8,128)(2,1)}, u32[]{:S(2)}, u32[]{:S(2)}) %all-to-all-start.1) | async-done | bytes 163872 | tf_op jit(solution)/shard_map/all_to_all | solution.py:497
  37.7 0.0 copy-done.1
  37.7 4.7 %copy-done = f32[2,20,20,2,16,64]{5,4,3,2,1,0:T(8,128)S(1)} copy-done((f32[2,20,20,2,16,64]{5,4,3,2,1,0:T(8,128)S(1)}, f32[2,20,20,2,16,64]{5,4,3,2,1,0:T(8,128)}, u32[]{:S(2)}) %copy-start) | copy-done | bytes 6553624
  42.5 1.6 %copy-done.2 = bf16[1024,1024]{1,0:T(8,128)(2,1)S(1)} copy-done((bf16[1024,1024]{1,0:T(8,128)(2,1)S(1)}, bf16[1024,1024]{1,0:T(8,128)(2,1)}, u32[]{:S(2)}) %copy-start.2) | copy-done | bytes 2097176
  44.1 5.3 %shard_map.203 = bf16[8,5,16,128]{3,2,1,0:T(8,128)(2,1)S(1)} custom-call(bf16[8,5,16,128]{3,2,1,0:T(8,128)(2,1)} %all-to-all-done.1.pencil, bf16[1024,1024]{1,0:T(8,128)(2,1)S(1)} %copy-done.1, f32[2,20,20,2,16,64]{5,4,3,2,1,0:T(8,128)S(1)} %copy-done, bf16[1024,1024]{1,0:T(8,128)(2,1)S(1)} %copy-done.2), custom_call_target="tpu_custom_call" | custom-call | flops 1000000000 | bytes 1000000 | tf_op jit(solution)/shard_map/pallas_call | solution.py:104
  49.4 0.6 copy-done.7
  50.1 3.5 %all-to-all-start.2 = ((bf16[8,5,16,128]{3,2,1,0:T(8,128)(2,1)}), bf16[8,5,16,128]{3,2,1,0:T(8,128)(2,1)S(1)}, u32[]{:S(2)}, u32[]{:S(2)}) async-start(bf16[8,5,16,128]{3,2,1,0:T(8,128)(2,1)} %copy-done.7), calls=%async_computation.2 | async-start | bytes 327680 | tf_op jit(solution)/shard_map/all_to_all | solution.py:512
  53.6 1.7 %pad_maximum_fusion = bf16[3,12,24,128]{3,2,1,0:T(8,128)(2,1)} fusion(bf16[3,2,24,128]{3,2,1,0:T(8,128)(2,1)} %get-tuple-element.16, bf16[3,8,24,128]{3,2,1,0:T(8,128)(2,1)} %get-tuple-element.10, bf16[3,2,24,128]{3,2,1,0:T(8,128)(2,1)S(1)} %copy-done.27), kind=kLoop, calls=%fused_computation.1 | loop fusion | flops 221184 | bytes 442368 | tf_op jit(solution)/shard_map/concatenate | solution.py:442
  55.2 2.3 %collective-permute-start.2 = (bf16[3,12,24,128]{3,2,1,0:T(8,128)(2,1)}, bf16[3,12,24,128]{3,2,1,0:T(8,128)(2,1)S(1)}, u32[]{:S(2)}, u32[]{:S(2)}) collective-permute-start(bf16[3,12,24,128]{3,2,1,0:T(8,128)(2,1)} %pad_maximum_fusion), channel_id=1, source_target_pairs={{0,4},{4,8},{8,12},{12,16},{16,20},{20,24},{24,28},{1,5},{5,9},{9,... | collective-permute-start | bytes 663560 | tf_op jit(solution)/shard_map/ppermute | solution.py:441
  57.5 1.1 %pad_bitcast_fusion = bf16[3,3,24,9,24]{4,2,3,1,0:T(8,128)(2,1)S(1)} fusion(bf16[3,3,9,20,20]{4,3,2,1,0:T(8,128)(2,1)} %bitcast.9), kind=kLoop, calls=%fused_computation | loop fusion | bytes 158112 | tf_op jit(solution)/shard_map/transpose | solution.py:457
  58.7 0.2 copy.28
  58.9 0.6 reshape.8.filters
  59.4 0.0 copy-done.28
  59.5 0.0 copy-start.18
  59.5 0.0 copy-start.25
  59.5 0.1 copy.26
  59.6 0.1 add_convert_fusion.flags
  59.7 1.1 %all-to-all-done.2.line = bf16[8,5,16,128]{3,2,1,0:T(8,128)(2,1)S(1)} async-done(((bf16[8,5,16,128]{3,2,1,0:T(8,128)(2,1)}), bf16[8,5,16,128]{3,2,1,0:T(8,128)(2,1)S(1)}, u32[]{:S(2)}, u32[]{:S(2)}) %all-to-all-start.2) | async-done | bytes 163872 | tf_op jit(solution)/shard_map/all_to_all | solution.py:512
  60.7 1.0 %shard_map.204 = bf16[4,5,32,128]{3,2,1,0:T(8,128)(2,1)} custom-call(bf16[8,5,16,128]{3,2,1,0:T(8,128)(2,1)S(1)} %all-to-all-done.2.line, bf16[128,256]{1,0:T(8,128)(2,1)S(1)} %copy-done.21, bf16[128,128]{1,0:T(8,128)(2,1)S(1)} %copy-done.23), custom_call_target="tpu_custom_call" | custom-call | flops 1000000000 | bytes 1000000 | tf_op jit(solution)/shard_map/pallas_call | solution.py:104
  61.7 3.3 %all-to-all-start.3 = ((bf16[4,5,32,128]{3,2,1,0:T(8,128)(2,1)}), bf16[4,5,32,128]{3,2,1,0:T(8,128)(2,1)S(1)}, u32[]{:S(2)}, u32[]{:S(2)}) async-start(bf16[4,5,32,128]{3,2,1,0:T(8,128)(2,1)} %shard_map.204), calls=%async_computation.3 | async-start | bytes 327680 | tf_op jit(solution)/shard_map/all_to_all | solution.py:520
  65.1 0.0 collective-permute-done.3.x_high
  65.1 0.0 collective-permute-done.2.x_low
  65.1 0.0 copy-start.12
  65.1 0.7 copy-done.12
  65.8 0.0 copy-done.6
  65.8 0.9 %copy-done.13 = bf16[3,12,24,128]{3,2,1,0:T(8,128)(2,1)S(1)} copy-done((bf16[3,12,24,128]{3,2,1,0:T(8,128)(2,1)S(1)}, bf16[3,12,24,128]{3,2,1,0:T(8,128)(2,1)}, u32[]{:S(2)}) %copy-start.13) | copy-done | bytes 221208
  66.7 0.9 %copy-done.15 = bf16[320,320]{1,0:T(8,128)(2,1)S(1)} copy-done((bf16[320,320]{1,0:T(8,128)(2,1)S(1)}, bf16[320,320]{1,0:T(8,128)(2,1)}, u32[]{:S(2)}) %copy-start.15) | copy-done | bytes 204824
  67.7 0.9 %copy-done.17 = bf16[320,192]{1,0:T(8,128)(2,1)S(1)} copy-done((bf16[320,192]{1,0:T(8,128)(2,1)S(1)}, bf16[320,192]{1,0:T(8,128)(2,1)}, u32[]{:S(2)}) %copy-start.17) | copy-done | bytes 122904
  68.6 0.8 copy-done.19
  69.4 12.5 %shard_map.200 = (bf16[4,16,24,128]{3,2,1,0:T(8,128)(2,1)S(1)}, bf16[320,512]{1,0:T(8,128)(2,1)S(1)}) custom-call(f32[4]{0:T(128)S(1)} %add_convert_fusion.flags, bf16[4,8,24,128]{3,2,1,0:T(8,128)(2,1)S(1)} %copy-done.6, bf16[4,2,24,128]{3,2,1,0:T(8,128)(2,1)S(1)} %collective-permute-done.y_low, bf16[4,2,24,128]{3,2,1,0:T(8,128)(2,1)S(1)} %collective-permute-done.1.y_high, ...), custom_call_target="tpu_custom_call" | custom-call | flops 6000000000 | bytes 6000000 | tf_op jit(solution)/shard_map/pallas_call | solution.py:104
  81.9 0.0 all-to-all-done.3.line
  81.9 3.2 %shard_map.205 = bf16[20,8,32,128]{3,2,1,0:T(8,128)(2,1)} custom-call(bf16[20,8,32,128]{3,2,1,0:T(8,128)(2,1)S(1)} %copy-done.4, bf16[4,16,24,128]{3,2,1,0:T(8,128)(2,1)S(1)} %get-tuple-element.7.third, bf16[4,5,32,128]{3,2,1,0:T(8,128)(2,1)S(1)} %all-to-all-done.3.line, bf16[320,512]{1,0:T(8,128)(2,1)S(1)} %get-tuple-element.8.lift, ...), custom_call_target="tpu_custom_call" | custom-call | flops 1000000000 | bytes 1000000 | tf_op jit(solution)/shard_map/pallas_call | solution.py:104
  (29 shorter events, 0.1 us)
Async XLA Ops:
  0.0 1.3 %copy-start.3 = (bf16[20,8,32,128]{3,2,1,0:T(8,128)(2,1)S(1)}, bf16[20,8,32,128]{3,2,1,0:T(8,128)(2,1)}, u32[]{:S(2)}) copy-start(bf16[20,8,32,128]{3,2,1,0:T(8,128)(2,1)} %field.5) | copy-start | bytes 3932164
  1.3 0.9 %copy-start.16 = (bf16[192,640]{1,0:T(8,128)(2,1)S(1)}, bf16[192,640]{1,0:T(8,128)(2,1)}, u32[]{:S(2)}) copy-start(bf16[192,640]{1,0:T(8,128)(2,1)} %constant.49.clone.rows_table) | copy-start | bytes 737284
  2.3 0.8 copy-start.22
  3.1 7.9 %copy-start.4 = (bf16[20,8,32,128]{3,2,1,0:T(8,128)(2,1)S(1)}, bf16[20,8,32,128]{3,2,1,0:T(8,128)(2,1)}, u32[]{:S(2)}) copy-start(bf16[20,8,32,128]{3,2,1,0:T(8,128)(2,1)} %field.5) | copy-start | bytes 3932164
  3.1 7.9 %copy-start.8 = (bf16[512,512]{1,0:T(8,128)(2,1)S(1)}, bf16[512,512]{1,0:T(8,128)(2,1)}, u32[]{:S(2)}) copy-start(bf16[512,512]{1,0:T(8,128)(2,1)} %constant.48.clone.regroup) | copy-start | bytes 1572868
  3.1 7.9 %copy-start.14 = (bf16[1024,128]{1,0:T(8,128)(2,1)S(1)}, bf16[1024,128]{1,0:T(8,128)(2,1)}, u32[]{:S(2)}) copy-start(bf16[1024,128]{1,0:T(8,128)(2,1)} %constant.47.clone.table) | copy-start | bytes 786436
  4.0 13.3 %copy-start.5 = (bf16[4,8,24,128]{3,2,1,0:T(8,128)(2,1)}, bf16[4,8,24,128]{3,2,1,0:T(8,128)(2,1)S(1)}, u32[]{:S(2)}) copy-start(bf16[4,8,24,128]{3,2,1,0:T(8,128)(2,1)S(1)} %shard_map.199.own) | copy-start | bytes 589828
  4.7 14.8 %collective-permute-start = (bf16[4,2,24,128]{3,2,1,0:T(8,128)(2,1)S(1)}, bf16[4,2,24,128]{3,2,1,0:T(8,128)(2,1)S(1)}, u32[]{:S(2)}, u32[]{:S(2)}) collective-permute-start(bf16[4,2,24,128]{3,2,1,0:T(8,128)(2,1)S(1)} %get-tuple-element.12), channel_id=1, source_target_pairs={{0,1},{1,2},{2,3},{4,5},{5,6},{6,7},{8,9},{9,10},{10,11},{12,13},{... | collective-permute-start | bytes 147464 | tf_op jit(solution)/shard_map/ppermute | solution.py:437
  9.6 8.6 %copy-start.26 = (bf16[3,27,20,20]{1,3,2,0:T(8,128)(2,1)S(1)}, bf16[3,27,20,20]{1,3,2,0:T(8,128)(2,1)}, u32[]{:S(2)}) copy-start(bf16[3,27,20,20]{1,3,2,0:T(8,128)(2,1)} %param.23) | copy-start | bytes 194404
  9.6 13.2 %copy-start.24 = (bf16[128,128]{1,0:T(8,128)(2,1)S(1)}, bf16[128,128]{1,0:T(8,128)(2,1)}, u32[]{:S(2)}) copy-start(bf16[128,128]{1,0:T(8,128)(2,1)} %constant.57.clone.swap) | copy-start | bytes 98308
  9.6 20.8 %collective-permute-start.1 = (bf16[4,2,24,128]{3,2,1,0:T(8,128)(2,1)}, bf16[4,2,24,128]{3,2,1,0:T(8,128)(2,1)S(1)}, u32[]{:S(2)}, u32[]{:S(2)}) collective-permute-start(bf16[4,2,24,128]{3,2,1,0:T(8,128)(2,1)} %get-tuple-element.11), channel_id=1, source_target_pairs={{1,0},{2,1},{3,2},{5,4},{6,5},{7,6},{9,8},{10,9},{11,10},{13,12},{... | collective-permute-start | bytes 147464 | tf_op jit(solution)/shard_map/ppermute | solution.py:438
  12.5 10.3 %all-to-all-start = ((bf16[4,5,32,128]{3,2,1,0:T(8,128)(2,1)}), bf16[4,5,32,128]{3,2,1,0:T(8,128)(2,1)}, u32[]{:S(2)}, u32[]{:S(2)}) async-start(bf16[4,5,32,128]{3,2,1,0:T(8,128)(2,1)} %shard_map.201), calls=%async_computation | async-start | bytes 327680 | tf_op jit(solution)/shard_map/all_to_all | solution.py:427
  20.1 17.6 %copy-start.1 = (bf16[1024,1024]{1,0:T(8,128)(2,1)S(1)}, bf16[1024,1024]{1,0:T(8,128)(2,1)}, u32[]{:S(2)}) copy-start(bf16[1024,1024]{1,0:T(8,128)(2,1)} %constant.58.clone.forward) | copy-start | bytes 6291460
  22.8 0.8 copy-start.20
  24.9 0.7 copy-start.11
  25.5 12.2 %all-to-all-start.1 = ((bf16[8,5,16,128]{3,2,1,0:T(8,128)(2,1)}), bf16[8,5,16,128]{3,2,1,0:T(8,128)(2,1)}, u32[]{:S(2)}, u32[]{:S(2)}) async-start(bf16[8,5,16,128]{3,2,1,0:T(8,128)(2,1)} %copy-done.11), calls=%async_computation.1 | async-start | bytes 327680 | tf_op jit(solution)/shard_map/all_to_all | solution.py:497
  31.0 22.5 %copy-start.27 = (bf16[3,2,24,128]{3,2,1,0:T(8,128)(2,1)S(1)}, bf16[3,2,24,128]{3,2,1,0:T(8,128)(2,1)}, u32[]{:S(2)}) copy-start(bf16[3,2,24,128]{3,2,1,0:T(8,128)(2,1)} %get-tuple-element.14) | copy-start | bytes 110596
  32.7 32.4 %collective-permute-start.3 = (bf16[3,12,24,128]{3,2,1,0:T(8,128)(2,1)}, bf16[3,12,24,128]{3,2,1,0:T(8,128)(2,1)}, u32[]{:S(2)}, u32[]{:S(2)}) collective-permute-start(bf16[3,12,24,128]{3,2,1,0:T(8,128)(2,1)} %pad_maximum_fusion.1), channel_id=1, source_target_pairs={{4,0},{8,4},{12,8},{16,12},{20,16},{24,20},{28,24},{5,1},{9,5},{13... | collective-permute-start | bytes 663560 | tf_op jit(solution)/shard_map/ppermute | solution.py:444
  37.7 4.7 %copy-start = (f32[2,20,20,2,16,64]{5,4,3,2,1,0:T(8,128)S(1)}, f32[2,20,20,2,16,64]{5,4,3,2,1,0:T(8,128)}, u32[]{:S(2)}) copy-start(f32[2,20,20,2,16,64]{5,4,3,2,1,0:T(8,128)} %weight.1) | copy-start | bytes 19660804
  42.5 1.6 %copy-start.2 = (bf16[1024,1024]{1,0:T(8,128)(2,1)S(1)}, bf16[1024,1024]{1,0:T(8,128)(2,1)}, u32[]{:S(2)}) copy-start(bf16[1024,1024]{1,0:T(8,128)(2,1)} %constant.59.clone.inverse) | copy-start | bytes 6291460
  49.4 0.7 copy-start.7
  50.0 9.4 %copy-start.28 = (bf16[20,20]{1,0:T(8,128)(2,1)S(1)}, bf16[20,20]{1,0:T(8,128)(2,1)}, u32[]{:S(2)}) copy-start(bf16[20,20]{1,0:T(8,128)(2,1)} %param.24) | copy-start | bytes 2404
  50.0 10.7 %copy-start.21 = (bf16[128,256]{1,0:T(8,128)(2,1)S(1)}, bf16[128,256]{1,0:T(8,128)(2,1)}, u32[]{:S(2)}) copy-start(bf16[128,256]{1,0:T(8,128)(2,1)} %constant.56.clone.table) | copy-start | bytes 196612
  50.0 10.7 %copy-start.23 = (bf16[128,128]{1,0:T(8,128)(2,1)S(1)}, bf16[128,128]{1,0:T(8,128)(2,1)}, u32[]{:S(2)}) copy-start(bf16[128,128]{1,0:T(8,128)(2,1)} %constant.60.clone.swap) | copy-start | bytes 98308
  50.1 10.7 %all-to-all-start.2 = ((bf16[8,5,16,128]{3,2,1,0:T(8,128)(2,1)}), bf16[8,5,16,128]{3,2,1,0:T(8,128)(2,1)S(1)}, u32[]{:S(2)}, u32[]{:S(2)}) async-start(bf16[8,5,16,128]{3,2,1,0:T(8,128)(2,1)} %copy-done.7), calls=%async_computation.2 | async-start | bytes 327680 | tf_op jit(solution)/shard_map/all_to_all | solution.py:512
  55.2 9.9 %collective-permute-start.2 = (bf16[3,12,24,128]{3,2,1,0:T(8,128)(2,1)}, bf16[3,12,24,128]{3,2,1,0:T(8,128)(2,1)S(1)}, u32[]{:S(2)}, u32[]{:S(2)}) collective-permute-start(bf16[3,12,24,128]{3,2,1,0:T(8,128)(2,1)} %pad_maximum_fusion), channel_id=1, source_target_pairs={{0,4},{4,8},{8,12},{12,16},{16,20},{20,24},{24,28},{1,5},{5,9},{9,... | collective-permute-start | bytes 663560 | tf_op jit(solution)/shard_map/ppermute | solution.py:441
  59.5 6.3 %copy-start.6 = (bf16[4,8,24,128]{3,2,1,0:T(8,128)(2,1)S(1)}, bf16[4,8,24,128]{3,2,1,0:T(8,128)(2,1)}, u32[]{:S(2)}) copy-start(bf16[4,8,24,128]{3,2,1,0:T(8,128)(2,1)} %copy-done.5) | copy-start | bytes 589828
  59.5 6.3 %copy-start.18 = (bf16[320,20]{1,0:T(8,128)(2,1)S(1)}, bf16[320,20]{1,0:T(8,128)(2,1)}, u32[]{:S(2)}) copy-start(bf16[320,20]{1,0:T(8,128)(2,1)} %constant.52.clone.pick_o) | copy-start | bytes 38404
  59.5 6.3 %copy-start.25 = (bf16[20,320]{1,0:T(8,128)(2,1)S(1)}, bf16[20,320]{1,0:T(8,128)(2,1)}, u32[]{:S(2)}) copy-start(bf16[20,320]{1,0:T(8,128)(2,1)} %constant.53.clone.pick_i) | copy-start | bytes 38404
  61.7 20.2 %all-to-all-start.3 = ((bf16[4,5,32,128]{3,2,1,0:T(8,128)(2,1)}), bf16[4,5,32,128]{3,2,1,0:T(8,128)(2,1)S(1)}, u32[]{:S(2)}, u32[]{:S(2)}) async-start(bf16[4,5,32,128]{3,2,1,0:T(8,128)(2,1)} %shard_map.204), calls=%async_computation.3 | async-start | bytes 327680 | tf_op jit(solution)/shard_map/all_to_all | solution.py:520
  65.1 0.7 copy-start.12
  65.8 0.9 %copy-start.13 = (bf16[3,12,24,128]{3,2,1,0:T(8,128)(2,1)S(1)}, bf16[3,12,24,128]{3,2,1,0:T(8,128)(2,1)}, u32[]{:S(2)}) copy-start(bf16[3,12,24,128]{3,2,1,0:T(8,128)(2,1)} %copy-done.12) | copy-start | bytes 663556
  66.7 0.9 %copy-start.15 = (bf16[320,320]{1,0:T(8,128)(2,1)S(1)}, bf16[320,320]{1,0:T(8,128)(2,1)}, u32[]{:S(2)}) copy-start(bf16[320,320]{1,0:T(8,128)(2,1)} %constant.54.clone.diag) | copy-start | bytes 614404
  67.7 0.9 %copy-start.17 = (bf16[320,192]{1,0:T(8,128)(2,1)S(1)}, bf16[320,192]{1,0:T(8,128)(2,1)}, u32[]{:S(2)}) copy-start(bf16[320,192]{1,0:T(8,128)(2,1)} %constant.55.clone.fixed) | copy-start | bytes 368644
  68.6 0.8 copy-start.19
  69.4 12.5 %copy-start.9 = (bf16[512,512]{1,0:T(8,128)(2,1)S(1)}, bf16[512,512]{1,0:T(8,128)(2,1)}, u32[]{:S(2)}) copy-start(bf16[512,512]{1,0:T(8,128)(2,1)} %constant.48.clone.regroup) | copy-start | bytes 1572868
  69.4 12.5 %copy-start.10 = (bf16[128,1024]{1,0:T(8,128)(2,1)S(1)}, bf16[128,1024]{1,0:T(8,128)(2,1)}, u32[]{:S(2)}) copy-start(bf16[128,1024]{1,0:T(8,128)(2,1)} %constant.61.clone.inverse) | copy-start | bytes 786436
where the time goes:
time: 86.4 us; the launch traced here: 85.2 us
  starting transfers between devices  26.4 us (31%)
  Pallas kernels  25.7 us (30%)
  local copies, waits for them, and re-layouts  22 us (25%)
  waiting for transfers between devices  7.47 us (9%)
  other arithmetic  3.36 us (4%)
    pallas_call x7, Pallas kernels, call(): pl.pallas_call(body, out_shape=outs, in_specs=specs or [VMEM] * len(input...  25.7 us
    unnamed x60, local copies, waits for them, and re-layouts  17.4 us
    all_to_all x1, starting transfers between devices, on_device(): pencil = lax.all_to_all(y_spec, 'gx', 0, 0, tiled=True)  4.87 us
    all_to_all x1, starting transfers between devices, on_device(): lines = lax.all_to_all(z_spec, 'gy', 0, 0, tiled=True)  4.87 us
    ppermute x1, starting transfers between devices, on_device(): y_low = lax.ppermute(coarse[:, -2:], 'gy', up_y)  4.83 us
    all_to_all x1, waiting for transfers between devices, on_device(): pencil = lax.all_to_all(y_spec, 'gx', 0, 0, tiled=True)  3.78 us
    all_to_all x1, starting transfers between devices, on_device(): back = lax.all_to_all(back, 'gx', 0, 0, tiled=True)  3.51 us
    all_to_all x1, starting transfers between devices, on_device(): y_cells = lax.all_to_all(y_cells, 'gy', 0, 0, tiled=True)  3.34 us
  transfers between devices with their start and end apart: 8, of which 3 were waited for; matrix products, arithmetic and copies ran while one was open for 10% of the time, Pallas kernels for 25%

commit v1 on v0

v1 whole, which is shorter than its diff:
```python
import functools
import math

import jax
import jax.numpy as jnp
import numpy as np
from jax import lax
from jax.experimental import pallas as pl
from jax.experimental.pallas import tpu as pltpu
from jax.sharding import PartitionSpec as P

LANES = 128
CP = 24
BF16 = jnp.bfloat16
F32 = jnp.float32
MIB = 1024 * 1024


def dot(left, right):
    return jnp.dot(left, right, preferred_element_type=F32)


def signed_modes(count):
    position = np.arange(count)
    return np.where(position < count // 2, position, position - count)


def phase(frequency, length):
    index = np.mod(frequency[:, None] * np.arange(length)[None, :], length)
    angle = index.astype(np.float32) * np.float32(2.0 * math.pi / length)
    return (
        np.cos(angle).astype(BF16).astype(np.float32),
        np.sin(angle).astype(BF16).astype(np.float32),
    )


def const(array):
    return np.asarray(array, np.float32).astype(BF16)


class Plan:
    def __init__(self, features, spectral_weight, devices_x, devices_y):
        self.channels, self.cx, self.cy, self.cz = features
        self.dx, self.dy = devices_x, devices_y
        self.kz, self.ky, self.kx = spectral_weight[3:]
        self.gx, self.gy = self.cx * self.dx, self.cy * self.dy
        self.my = self.ky * self.dx
        self.mz = self.kz * self.dy
        self.unit = 2 * self.kz * self.cx
        self.groups = LANES // self.unit
        self.cg = self.channels // self.groups

    def forward_z(self):
        cos, sin = phase(np.arange(self.mz), self.cz)
        table = np.stack([cos, -sin], 0).reshape(2, self.dy, self.kz, self.cz)
        out = np.einsum("pdkz,xw->xzdpkw", table, np.eye(self.cx))
        return const(out.reshape(self.cx * self.cz, self.dy * self.unit))

    def inverse_z(self):
        cos, sin = phase(np.arange(self.mz), self.cz)
        scale = np.where(np.arange(self.mz) == 0, 1.0, 2.0) / float(self.gx * self.gy * self.cz)
        table = np.stack([cos, -sin], 0) * scale[None, :, None]
        table = table.reshape(2, self.dy, self.kz, self.cz)
        out = np.einsum("pdkz,xw->dpkxwz", table, np.eye(self.cx))
        return const(out.reshape(self.dy * self.unit, self.cx * self.cz))

    def regroup(self, outer, inner):
        out = np.einsum("ac,bd,lm->abldcm", np.eye(outer), np.eye(inner), np.eye(self.unit))
        size = outer * inner * self.unit
        return const(out.reshape(size, size))

    def swap(self, sign):
        turn = np.array([[0.0, -sign], [sign, 0.0]])
        half = self.unit // 2
        return const(np.kron(np.eye(self.groups), np.kron(turn, np.eye(half))))

    def forward_y(self):
        cos, sin = phase(signed_modes(self.my), self.gy)
        return const(np.concatenate([cos, sin], 1))

    def inverse_y(self):
        cos, sin = phase(signed_modes(self.my), self.gy)
        return const(np.concatenate([cos.T, sin.T], 1))

    def forward_x(self):
        cos, sin = phase(signed_modes(self.kx), self.gx)
        turn = np.stack([np.stack([cos, -sin]), np.stack([sin, cos])])
        turn = turn.reshape(2, 2, self.kx, self.dx, self.cx)
        out = np.einsum("pqjsx,gh,kl->sgpkxhqlj", turn, np.eye(self.groups), np.eye(self.kz))
        return const(out.reshape(self.dx * LANES, self.groups * self.kz * 2 * self.kx))

    def inverse_x(self):
        cos, sin = phase(signed_modes(self.kx), self.gx)
        turn = np.stack([np.stack([cos, sin]), np.stack([-sin, cos])])
        turn = turn.reshape(2, 2, self.kx, self.dx, self.cx)
        out = np.einsum("pqjsx,gh,kl->gpkjshqlx", turn, np.eye(self.groups), np.eye(self.kz))
        return const(out.reshape(self.groups * self.kz * 2 * self.kx, self.dx * LANES))


VMEM = pl.BlockSpec(memory_space=pltpu.VMEM)
PLAIN = pl.BlockSpec(memory_space=pltpu.VMEM)
FAR = pl.BlockSpec(memory_space=pltpu.VMEM)


ANY = pl.BlockSpec(memory_space=pl.ANY)
HBM = pl.BlockSpec(memory_space=pltpu.HBM)


def pinned(value, spec):
    if spec is HBM or spec is FAR:
        return pltpu.with_memory_space_constraint(jnp.asarray(value), pltpu.HBM)
    if spec is ANY or spec is PLAIN or isinstance(value, np.ndarray):
        return value
    return pltpu.with_memory_space_constraint(value, pltpu.VMEM)


def call(
    body, outs, inputs, scratch=(), specs=None, out_specs=None, vmem=8, flops=1e9, moved=1e6,
    pin=True, **kw,
):
    single = not isinstance(outs, (tuple, list))
    outs = [outs] if single else list(outs)
    specs = specs or [VMEM] * len(inputs)
    out_specs = out_specs or [VMEM] * len(outs)
    if pin:
        inputs = [pinned(value, spec) for value, spec in zip(inputs, specs)]
        outs = [
            pltpu.VMEM(o.shape, o.dtype)
            if spec is VMEM
            else pltpu.HBM(o.shape, o.dtype) if spec is FAR else o
            for o, spec in zip(outs, out_specs)
        ]
    result = pl.pallas_call(
        body,
        out_shape=outs,
        in_specs=specs,
        out_specs=out_specs,
        scratch_shapes=scratch,
        compiler_params=pltpu.CompilerParams(vmem_limit_bytes=vmem * MIB),
        cost_estimate=pl.CostEstimate(
            flops=int(flops), bytes_accessed=int(moved), transcendentals=0
        ),
        **kw,
    )(*inputs)
    return result[0] if single else result


def turn(index, shift, count):
    return lax.rem(index + shift + count, count)


def first_body(
    plan, field_in, table_in, regroup_in, rows_in, pair_in, ytable_in, swap_in,
    own, low_message, high_message, *rest,
):
    middle = rest[: plan.dy - 3]
    coarse, ytable, swap, field, table, regroup, rows_table, pair_table, chunks, sems = rest[
        plan.dy - 3 :
    ]
    sources = (field_in, table_in, regroup_in, rows_in, pair_in, ytable_in, swap_in)
    targets = (field, table, regroup, rows_table, pair_table, ytable, swap)
    copies = [
        pltpu.make_async_copy(s, t, sems.at[n]) for n, (s, t) in enumerate(zip(sources, targets))
    ]
    for copy in copies:
        copy.start()
    for copy in copies[:3]:
        copy.wait()
    rows = plan.channels * plan.cy
    lhs = jnp.concatenate(
        [field[:, x].reshape(rows, plan.cz) for x in range(plan.cx)], axis=1
    )
    modes = dot(lhs, table[...]).astype(BF16)
    part = plan.cg * plan.cy
    lanes = jnp.concatenate(
        [modes[g * part : (g + 1) * part] for g in range(plan.groups)], axis=1
    )
    result = dot(lanes, regroup[...]).astype(BF16)
    for d in range(plan.dy):
        chunks[d] = result[:, d * LANES : (d + 1) * LANES]
    for copy in copies[3:]:
        copy.wait()
    pool_body(plan, field, rows_table, pair_table, coarse)
    here = lax.axis_index("gy")
    own[...] = chunks[here]
    low_message[:part] = chunks[turn(here, 1, plan.dy)]
    high_message[:part] = chunks[turn(here, plan.dy - 1, plan.dy)]
    for s, message in enumerate(middle):
        message[...] = chunks[turn(here, s + 2, plan.dy)]
    tiles = plan.cy // 4
    index = 0
    for x in range(plan.cx // 2):
        for j in range(2):
            at = slice(part + index * CP, part + (index + 1) * CP)
            low_message[at] = coarse[x, tiles - 2 + j]
            high_message[at] = coarse[x, j]
            index += 1


def y_transform(plan, line, table, swap):
    columns = []
    for value in line:
        turned = dot(value, swap[...]).astype(BF16)
        columns.append(jnp.concatenate([value, turned], axis=0))
    return dot(table[...], jnp.concatenate(columns, axis=1)).astype(BF16)


def forward_y_body(plan, own, low_message, high_message, *rest):
    middle = rest[: plan.dy - 3]
    coarse, table, swap, out, up, down, volume, line = rest[plan.dy - 3 :]
    part = plan.cg * plan.cy
    here = lax.axis_index("gy")
    line[here] = own[...]
    line[turn(here, -1, plan.dy)] = low_message[:part]
    line[turn(here, 1, plan.dy)] = high_message[:part]
    for s, message in enumerate(middle):
        line[turn(here, -(s + 2), plan.dy)] = message[...]
    values = [
        jnp.concatenate(
            [line[s, c * plan.cy : (c + 1) * plan.cy] for s in range(plan.dy)], axis=0
        )
        for c in range(plan.cg)
    ]
    result = y_transform(plan, values, table, swap)
    targets, _, rows_out, _ = out.shape
    for d in range(targets):
        for c in range(plan.cg):
            out[d, c] = result[
                d * rows_out : (d + 1) * rows_out, c * LANES : (c + 1) * LANES
            ]
    nx = plan.cx // 2
    tiles = plan.cy // 4
    for x in range(nx):
        planes = [volume.at[x]]
        if x < 3:
            planes.append(down.at[x])
        if x >= nx - 3:
            planes.append(up.at[x - nx + 3])
        for j in range(2):
            at = slice(part + (x * 2 + j) * CP, part + (x * 2 + j + 1) * CP)
            low = jnp.where(here > 0, low_message[at], jnp.zeros((CP, LANES), BF16))
            high = jnp.where(here < plan.dy - 1, high_message[at], jnp.zeros((CP, LANES), BF16))
            for plane in planes:
                plane[j] = low
                plane[2 + tiles + j] = high
        for j in range(tiles):
            for plane in planes:
                plane[2 + j] = coarse[x, j]


def inverse_y_body(plan, line, table_in, swap_in, own, *rest):
    messages = rest[: plan.dy - 1]
    table, swap, chunks, sems = rest[plan.dy - 1 :]
    copies = [
        pltpu.make_async_copy(swap_in, swap, sems.at[0]),
        pltpu.make_async_copy(table_in, table, sems.at[1]),
    ]
    for copy in copies:
        copy.start()
    for copy in copies:
        copy.wait()
    sources = line.shape[0]
    values = [
        jnp.concatenate([line[s, c] for s in range(sources)], axis=0) for c in range(plan.cg)
    ]
    result = y_transform(plan, values, table, swap)
    for d in range(plan.dy):
        for c in range(plan.cg):
            chunks[d, c * plan.cy : (c + 1) * plan.cy] = result[
                d * plan.cy : (d + 1) * plan.cy, c * LANES : (c + 1) * LANES
            ]
    here = lax.axis_index("gy")
    own[...] = chunks[here]
    for s, message in enumerate(messages):
        message[...] = chunks[turn(here, s + 1, plan.dy)]


def mix(plan, spec, weight, mixed):
    def step(o, carry):
        for k in range(plan.kz):
            real = jnp.zeros((plan.ky, plan.kx), F32)
            imag = jnp.zeros((plan.ky, plan.kx), F32)
            for i in range(plan.channels):
                wr = weight[0, i, o, k]
                wi = weight[1, i, o, k]
                xr = spec[0, k, i]
                xi = spec[1, k, i]
                real += xr * wr - xi * wi
                imag += xr * wi + xi * wr
            mixed[k, o] = jnp.concatenate([real, imag], axis=1)
        return carry

    lax.fori_loop(0, plan.channels, step, 0)


def window_body(
    plan, steps, after, volume_in, filters, point, weight, packed, partial, lift, held, held_sems,
):
    c = plan.channels
    loads = [
        pltpu.make_async_copy(
            weight.at[:, :, pl.ds(n * steps, steps)],
            held.at[:, :, pl.ds(n * steps, steps)],
            held_sems.at[n],
        )
        for n in range(c // steps)
    ]
    for load in loads:
        load.start()
    conv_own_body(plan, volume_in, filters, point, partial, lift)
    for n, load in enumerate(loads):
        load.wait()
        for o in range(n * steps, (n + 1) * steps):
            for p in range(2):
                for i in range(c):
                    packed[o, p, i] = jnp.concatenate(
                        [held[p, i, o, k] for k in range(plan.kz)], axis=1
                    ).astype(BF16)


def x_body(
    plan, pencil, forward_in, packed_in, inverse_in, out, forward, packed, inverse, sems, spec, mixed
):
    halves = 2
    block = plan.channels // halves
    copies = [pltpu.make_async_copy(forward_in, forward, sems.at[0])]
    for n in range(halves):
        at = pl.ds(n * block, block)
        copies.append(pltpu.make_async_copy(packed_in.at[at], packed.at[at], sems.at[n + 1]))
    copies.append(pltpu.make_async_copy(inverse_in, inverse, sems.at[halves + 1]))
    for copy in copies:
        copy.start()
    copies[0].wait()
    rows = plan.cg * plan.ky
    wide = plan.kz * plan.kx
    lhs = jnp.concatenate([pencil[s].reshape(rows, LANES) for s in range(plan.dx)], axis=1)
    spectrum = dot(lhs, forward[...])
    for g in range(plan.groups):
        for p in range(2):
            start = (g * 2 + p) * wide
            modes = spectrum[:, start : start + wide].reshape(plan.cg, plan.ky, wide)
            spec[p, g * plan.cg : (g + 1) * plan.cg] = modes

    def step(o, carry):
        real = jnp.zeros((plan.ky, wide), F32)
        imag = jnp.zeros((plan.ky, wide), F32)
        for i in range(plan.channels):
            wr = packed[o, 0, i].astype(F32)
            wi = packed[o, 1, i].astype(F32)
            xr = spec[0, i]
            xi = spec[1, i]
            real += xr * wr - xi * wi
            imag += xr * wi + xi * wr
        mixed[0, o] = real
        mixed[1, o] = imag
        return carry

    for n in range(halves):
        copies[n + 1].wait()
        lax.fori_loop(n * block, (n + 1) * block, step, 0)
    copies[-1].wait()
    back = jnp.concatenate(
        [
            mixed[p, g * plan.cg : (g + 1) * plan.cg].reshape(rows, wide).astype(BF16)
            for g in range(plan.groups)
            for p in range(2)
        ],
        axis=1,
    )
    result = dot(back, inverse[...]).astype(BF16)
    for d in range(plan.dx):
        out[d] = result[:, d * LANES : (d + 1) * LANES].reshape(plan.cg, plan.ky, LANES)


def x_stage_general(plan, pencil, weight):
    groups, cg, ky, kz, kx = plan.groups, plan.cg, plan.ky, plan.kz, plan.kx
    lhs = jnp.transpose(pencil, (1, 2, 0, 3)).reshape(cg * ky, plan.dx * LANES)
    spectrum = dot(lhs, plan.forward_x()).reshape(cg, ky, groups, 2, kz, kx)
    spectrum = jnp.transpose(spectrum, (3, 4, 2, 0, 1, 5)).reshape(2, kz, groups * cg, ky, kx)
    mixed = call(
        functools.partial(mix, plan),
        jax.ShapeDtypeStruct((kz, groups * cg, ky, 2 * kx), F32),
        (spectrum, weight),
        vmem=32,
        pin=False,
    )
    back = jnp.transpose(mixed.reshape(kz, groups, cg, ky, 2, kx), (2, 3, 1, 4, 0, 5))
    back = back.reshape(cg * ky, groups * kz * 2 * kx).astype(BF16)
    back = dot(back, plan.inverse_x()).astype(BF16).reshape(cg, ky, plan.dx, LANES)
    return jnp.transpose(back, (2, 0, 1, 3))


def gelu(value):
    return 0.5 * value * (1.0 + lax.erf(value * (0.5**0.5)))


def pool_tables(plan):
    half = plan.cy // 2
    quarter = half // 2
    rows = np.einsum(
        "cC,yY->ycCY", np.eye(CP)[:, : plan.channels], np.kron(np.eye(quarter), np.ones((1, 2)))
    ).reshape(quarter * CP, plan.channels * half)
    rows = np.concatenate([rows, rows], 1)
    pairs = np.kron(np.eye(plan.cz), np.full((2, 1), 0.125))
    return const(rows), const(pairs)


def pool_body(plan, field, rows_table, pair_table, out):
    half = plan.cy // 2
    quarter = half // 2
    cells = plan.channels * half
    for h in range(2):
        columns = []
        for x in range(plan.cx // 2):
            columns.append(
                jnp.concatenate(
                    [
                        field[:, 2 * x + e, h * half : (h + 1) * half].reshape(cells, plan.cz)
                        for e in range(2)
                    ],
                    axis=0,
                )
            )
        summed = dot(rows_table[...], jnp.concatenate(columns, axis=1))
        blocks = []
        for x in range(plan.cx // 2):
            for j in range(quarter // 2):
                blocks.append(
                    jnp.concatenate(
                        [
                            summed[
                                (2 * j + e) * CP : (2 * j + e + 1) * CP,
                                x * plan.cz : (x + 1) * plan.cz,
                            ]
                            for e in range(2)
                        ],
                        axis=1,
                    )
                )
        block = jnp.concatenate(blocks, axis=0)
        high = block.astype(BF16)
        low = (block - high.astype(F32)).astype(BF16)
        result = dot(high, pair_table[...]) + dot(low, pair_table[...])
        index = 0
        for x in range(plan.cx // 2):
            for j in range(quarter // 2):
                out[x, h * (quarter // 2) + j] = result[index * CP : (index + 1) * CP].astype(BF16)
                index += 1


def tap_columns(volume, x, tiles):
    lane = lax.broadcasted_iota(jnp.int32, (CP, LANES), 1)
    z = lane % (LANES // 2)
    lower = lane < LANES // 2
    shifted = {}
    for j in range(tiles[0] - 1, tiles[1] + 1):
        value = volume[x, j].astype(F32)
        versions = (
            jnp.where(z == 0, 0.0, pltpu.roll(value, 1, 1)),
            value,
            jnp.where(z == LANES // 2 - 1, 0.0, pltpu.roll(value, LANES - 1, 1)),
        )
        shifted[j] = (versions, [pltpu.roll(v, LANES // 2, 1) for v in versions])
    columns = []
    for j in range(tiles[0], tiles[1]):
        pieces = []
        for e in range(3):
            pieces.append(jnp.where(lower, shifted[j - 1][1][e], shifted[j][1][e]))
        for e in range(3):
            pieces.append(shifted[j][0][e])
        for e in range(3):
            pieces.append(jnp.where(lower, shifted[j][1][e], shifted[j + 1][1][e]))
        columns.append(jnp.concatenate(pieces, axis=0).astype(BF16))
    return jnp.concatenate(columns, axis=1)


def combined(partial, x, cols):
    return (
        partial[x, 0:CP, cols]
        + partial[x + 1, CP : 2 * CP, cols]
        + partial[x + 2, 2 * CP : 3 * CP, cols]
    )


def activate(plan, planes, tiles, partial, volume):
    nx = plan.cx // 2
    ny = plan.cy // 4
    here_x = lax.axis_index("gx")
    here_y = lax.axis_index("gy")
    one = jnp.float32(1.0)
    zero = jnp.float32(0.0)
    below_x = jnp.where(here_x > 0, one, zero)
    above_x = jnp.where(here_x < plan.dx - 1, one, zero)
    below_y = jnp.where(here_y > 0, one, zero)
    above_y = jnp.where(here_y < plan.dy - 1, one, zero)
    margin = (planes - nx) // 2

    def body(x, carry):
        inside = jnp.where(x < margin, below_x, one) * jnp.where(x >= margin + nx, above_x, one)
        for j in range(tiles[0], tiles[1]):
            cols = slice((j - tiles[0]) * LANES, (j - tiles[0] + 1) * LANES)
            scale = inside
            if j < 2:
                scale = scale * below_y
            if j >= 2 + ny:
                scale = scale * above_y
            value = gelu(combined(partial, x, cols)) * scale
            volume[x, j] = value.astype(volume.dtype)
        return carry

    lax.fori_loop(0, planes, body, 0)


def where_bf16(mask):
    return jnp.where(mask, 1.0, 0.0).astype(BF16)


def iota(shape, dim):
    return lax.broadcasted_iota(jnp.int32, shape, dim)


def make_lift(plan, point, lift):
    half = plan.cy // 2
    cells = plan.channels * half
    tall = (cells, plan.channels)
    flat = (plan.channels, cells)
    square = (cells, cells)
    pick_o = where_bf16(iota(tall, 0) // half == iota(tall, 1))
    pick_i = where_bf16(iota(flat, 1) // half == iota(flat, 0))
    expanded = dot(dot(pick_o, point[...]).astype(BF16), pick_i)
    diagonal = iota(square, 0) % half == iota(square, 1) % half
    lift[:, :cells] = jnp.where(diagonal, expanded, 0.0).astype(BF16)
    coarse = (cells, half // 2 * CP)
    row, col = iota(coarse, 0), iota(coarse, 1)
    lift[:, cells:] = where_bf16(
        (row // half == col % CP) & ((row % half) // 2 == col // CP)
    )


def conv_own_body(plan, volume_in, filters, point, partial, lift):
    nx = plan.cx // 2
    ny = plan.cy // 4
    make_lift(plan, point, lift)

    def body(x, carry):
        partial[x] = dot(filters[0], tap_columns(volume_in, x, (1, ny + 3)))
        return carry

    lax.fori_loop(0, nx, body, 0)


def conv_middle_body(plan, after, x_low, x_high, own, filters, second, partial, volume):
    nx = plan.cx // 2
    ny = plan.cy // 4
    wide = ny + 4
    tiles = (1, ny + 3)

    def edges(x, carry):
        partial[x] = dot(filters[0], tap_columns(x_low, x, tiles))
        partial[x + 3 + nx] = dot(filters[0], tap_columns(x_high, x, tiles))
        return carry

    lax.fori_loop(0, 3, edges, 0)
    for x in range(nx):
        partial[x + 3] = own[x]
    activate(plan, nx + 4, tiles, partial, volume)
    zero = jnp.zeros((CP, LANES), volume.dtype)
    for x in range(nx + 4):
        volume[x, 0] = zero
        volume[x, wide - 1] = zero

    def body(x, carry):
        partial[x] = dot(filters[1], tap_columns(volume, x, tiles))
        return carry

    lax.fori_loop(0, nx + 4, body, 0)
    activate(plan, nx + 2, tiles, partial, second)


def conv_last_body(plan, after, second, filters, third, partial):
    nx = plan.cx // 2
    ny = plan.cy // 4
    tiles = (2, ny + 2)

    def body(x, carry):
        partial[x] = dot(filters[2], tap_columns(second, x, tiles))
        return carry

    lax.fori_loop(0, nx + 2, body, 0)

    square = (LANES, 2 * LANES)
    spread = where_bf16(iota(square, 1) // 2 == iota(square, 0))

    def up(x, carry):
        for j in range(ny):
            total = combined(partial, x, slice(j * LANES, (j + 1) * LANES))
            wide = dot(total.astype(BF16), spread).astype(BF16)
            third[x, 2 * j] = wide[:, : plan.cz]
            third[x, 2 * j + 1] = wide[:, plan.cz :]
        return carry

    lax.fori_loop(0, nx, up, 0)


def final_body(plan, field, third, lift, regroup, inverse, own, *rest):
    messages = rest[: plan.dy - 1]
    out, line, lanes = rest[plan.dy - 1 :]
    step = pl.program_id(0)
    half = plan.cy // 2
    part = plan.cg * plan.cy

    @pl.when(step == 0)
    def _():
        here = lax.axis_index("gy")
        line[here] = own[...]
        for s, message in enumerate(messages):
            line[turn(here, -(s + 1), plan.dy)] = message[...]
        gathered = jnp.concatenate([line[s] for s in range(plan.dy)], axis=1)
        result = dot(gathered, regroup[...]).astype(BF16)
        width = plan.dy * plan.unit
        for g in range(plan.groups):
            lanes[g * part : (g + 1) * part] = result[:, g * width : (g + 1) * width]

    cells = plan.channels * half
    columns = []
    for e in range(2):
        for h in range(2):
            cols = third[0, h * (half // 2) : (h + 1) * (half // 2)]
            columns.append(
                jnp.concatenate(
                    [
                        field[:, e, h * half : (h + 1) * half].reshape(cells, plan.cz),
                        cols.astype(F32).reshape(half // 2 * CP, plan.cz).astype(BF16),
                    ],
                    axis=0,
                )
            )
    local = dot(lift[...], jnp.concatenate(columns, axis=1))
    spectral = dot(lanes[...], inverse[...]).reshape(plan.channels, plan.cy, 2 * plan.cz)
    for e in range(2):
        for h in range(2):
            index = e * 2 + h
            total = local[:, index * plan.cz : (index + 1) * plan.cz].reshape(
                plan.channels, half, plan.cz
            ) + spectral[:, h * half : (h + 1) * half, e * plan.cz : (e + 1) * plan.cz]
            out[:, e, h * half : (h + 1) * half] = gelu(total).astype(BF16)


def after(values, marker):
    return lax.optimization_barrier((values, marker))[0]


def ring(value, axis, shift):
    count = lax.axis_size(axis)
    return lax.ppermute(value, axis, [(i, (i + shift) % count) for i in range(count)])


def on_device(features, spectral_weight, conv_weight, point_weight):
    devices_x = lax.axis_size("gx")
    devices_y = lax.axis_size("gy")
    plan = Plan(features.shape, spectral_weight.shape, devices_x, devices_y)
    channels, cx, cy, cz = features.shape
    shape = jax.ShapeDtypeStruct
    cg = plan.cg
    nx, ny = cx // 2, cy // 4
    part = cg * cy
    split = plan.ky % 16 == 0 and plan.kz * plan.kx == LANES
    half = cy // 2

    rows_table, pair_table = pool_tables(plan)
    tables = (
        plan.forward_z(), plan.regroup(plan.groups, devices_y), rows_table, pair_table,
        plan.forward_y(), plan.swap(1.0),
    )
    chunk = shape((part, LANES), BF16)
    message = shape((part + nx * 2 * CP, LANES), BF16)
    outs = [chunk, message, message] + [chunk] * (devices_y - 3)
    outs += [shape((nx, ny, CP, cz), BF16)] + [shape(t.shape, BF16) for t in tables[4:]]
    first = call(
        functools.partial(first_body, plan),
        outs,
        (features,) + tables,
        scratch=[pltpu.VMEM(features.shape, BF16)]
        + [pltpu.VMEM(t.shape, BF16) for t in tables[:4]]
        + [pltpu.VMEM((devices_y, part, LANES), BF16), pltpu.SemaphoreType.DMA((7,))],
        specs=[HBM] * 7,
        vmem=16,
    )
    own, to_up, to_down = first[:3]
    middle = first[3:-3]
    coarse, y_table, y_swap = first[-3:]
    low_message = ring(to_up, "gy", 1)
    high_message = ring(to_down, "gy", -1)
    middle = [ring(m, "gy", s + 2) for s, m in enumerate(middle)]

    y_out = (devices_x, cg, plan.ky) if split else (1, cg, plan.my)
    planes = shape((3, ny + 4, CP, LANES), BF16)
    y_spec, up, down, volume = call(
        functools.partial(forward_y_body, plan),
        (shape(y_out + (LANES,), BF16), planes, planes, shape((nx, ny + 4, CP, LANES), BF16)),
        (own, low_message, high_message, *middle, coarse, y_table, y_swap),
        out_specs=[PLAIN, FAR, FAR, VMEM],
        scratch=[pltpu.VMEM((devices_y, part, LANES), BF16)],
    )
    if not split:
        y_spec = jnp.transpose(y_spec.reshape(cg, devices_x, plan.ky, LANES), (1, 0, 2, 3))
    pencil = lax.all_to_all(y_spec, "gx", 0, 0, tiled=True)

    filters = jnp.pad(
        conv_weight.reshape(3, 3, 9, channels, channels),
        ((0, 0), (0, 0), (0, 0), (0, CP - channels), (0, CP - channels)),
    )
    filters = jnp.transpose(filters, (0, 1, 3, 2, 4)).reshape(3, 3 * CP, 9 * CP)
    wide = (ny + 2) * LANES
    small = (
        shape((nx, 3 * CP, wide), F32),
        shape((channels * half, channels * half + half // 2 * CP), BF16),
    )
    local = (volume, filters, jnp.transpose(point_weight))
    if split:
        steps = 2 if channels % 2 == 0 else 1
        forward_x = plan.forward_x()
        inverse_x = plan.inverse_x()
        packed, partial_own, lift = call(
            functools.partial(window_body, plan, steps),
            (shape((channels, 2, channels, plan.ky, LANES), BF16),) + small,
            (y_spec,) + local + (spectral_weight,),
            specs=[ANY] + [VMEM, PLAIN, PLAIN] + [HBM],
            out_specs=[FAR, FAR, FAR],
            scratch=[
                pltpu.VMEM(spectral_weight.shape, F32),
                pltpu.SemaphoreType.DMA((channels // steps,)),
            ],
            vmem=24,
            flops=4e9,
            moved=16e6,
        )
    else:
        partial_own, lift = call(
            functools.partial(conv_own_body, plan),
            small,
            local,
            specs=[VMEM, PLAIN, PLAIN],
            out_specs=[FAR, FAR],
            flops=2e9,
        )
    up, down = after((up, down), lift)
    x_low = lax.ppermute(up, "gx", [(i, i + 1) for i in range(devices_x - 1)])
    x_high = lax.ppermute(down, "gx", [(i + 1, i) for i in range(devices_x - 1)])

    if split:
        back = call(
            functools.partial(x_body, plan),
            shape((devices_x, cg, plan.ky, LANES), BF16),
            (pencil, forward_x, packed, inverse_x),
            specs=[VMEM, HBM, HBM, HBM],
            out_specs=[PLAIN],
            scratch=[
                pltpu.VMEM(forward_x.shape, BF16),
                pltpu.VMEM(packed.shape, BF16),
                pltpu.VMEM(inverse_x.shape, BF16),
                pltpu.SemaphoreType.DMA((4,)),
                pltpu.VMEM((2, channels, plan.ky, LANES), F32),
                pltpu.VMEM((2, channels, plan.ky, LANES), F32),
            ],
            vmem=14,
        )
    else:
        back = x_stage_general(plan, pencil, spectral_weight)
    line = lax.all_to_all(back, "gx", 0, 0, tiled=True)

    second = call(
        functools.partial(conv_middle_body, plan),
        shape((nx + 2, ny + 4, CP, LANES), F32),
        (back, x_low, x_high, partial_own, filters),
        scratch=[
            pltpu.VMEM((nx + 6, 3 * CP, wide), F32),
            pltpu.VMEM((nx + 4, ny + 4, CP, LANES), F32),
        ],
        specs=[ANY, PLAIN, PLAIN, FAR, PLAIN],
        out_specs=[PLAIN],
        vmem=7,
        flops=6e9,
    )
    if not split:
        line = jnp.transpose(line, (1, 0, 2, 3)).reshape(1, cg, plan.my, LANES)
    own, *messages = call(
        functools.partial(inverse_y_body, plan),
        [chunk] * devices_y,
        (line, plan.inverse_y(), plan.swap(-1.0)),
        specs=[VMEM, HBM, HBM],
        scratch=[
            pltpu.VMEM((plan.gy, 2 * plan.my), BF16),
            pltpu.VMEM((LANES, LANES), BF16),
            pltpu.VMEM((devices_y, part, LANES), BF16),
            pltpu.SemaphoreType.DMA((2,)),
        ],
    )
    arrived = [ring(m, "gy", s + 1) for s, m in enumerate(messages)]
    third = call(
        functools.partial(conv_last_body, plan),
        shape((nx, 2 * ny, CP, cz), BF16),
        (own, second, filters),
        scratch=[pltpu.VMEM((nx + 2, 3 * CP, ny * LANES), F32)],
        specs=[ANY, PLAIN, PLAIN],
        out_specs=[PLAIN],
        flops=3e9,
    )

    full = lambda array: pl.BlockSpec(array.shape, lambda s: (0,) * array.ndim)
    regroup = plan.regroup(devices_y, plan.groups)
    inverse_z = plan.inverse_z()
    far = lambda array: pltpu.with_memory_space_constraint(jnp.asarray(array), pltpu.HBM)
    return call(
        functools.partial(final_body, plan),
        shape(features.shape, BF16),
        (far(features), third, far(lift), far(regroup), far(inverse_z), own, *arrived),
        pin=False,
        grid=(nx,),
        specs=[
            pl.BlockSpec((channels, 2, cy, cz), lambda s: (0, s, 0, 0)),
            pl.BlockSpec((1, cy // 2, CP, cz), lambda s: (s, 0, 0, 0)),
            full(lift),
            full(regroup),
            pl.BlockSpec((devices_y * plan.unit, 2 * cz), lambda s: (0, s)),
        ]
        + [full(own)] * devices_y,
        out_specs=[pl.BlockSpec((channels, 2, cy, cz), lambda s: (0, s, 0, 0))],
        scratch=[
            pltpu.VMEM((devices_y, part, LANES), BF16),
            pltpu.VMEM((channels * cy, devices_y * plan.unit), BF16),
        ],
        vmem=12,
    )


def solution(mesh):
    in_specs = (P(None, ("grp", "gx"), "gy", None), P(None, None, None, "gy", "gx", None), P(), P())
    out_specs = P(None, ("grp", "gx"), "gy", None)
    return jax.shard_map(
        on_device, mesh=mesh, in_specs=in_specs, out_specs=out_specs, check_vma=False
    )
```

time: 86.4 us -> 62.1 us (0.72)
  local copies, waits for them, and re-layouts: 22 us -> 1.62 us
  Pallas kernels: 25.7 us -> 32.7 us
  waiting for transfers between devices: 7.47 us -> 1.42 us
  other arithmetic: 3.36 us -> 0 us
    unnamed x60 -> x10, local copies, waits for them, and re-layouts: 17.4 us -> 0.71 us
    pallas_call x7 -> x8, Pallas kernels: 25.7 us -> 32.7 us  [call(): pl.pallas_call(body, out_shape=outs, in_specs=specs, out_specs=out_specs,...]
    all_to_all x3 -> x1, starting transfers between devices: 11.7 us -> 6.96 us  [on_device(): line = lax.all_to_all(back, 'gx', 0, 0, tiled=True)]
    ppermute x4 -> x8, starting transfers between devices: 9.83 us -> 13.8 us  [the longest x6 10.1 us: ring(): lax.ppermute(value, axis, [(i, (i + shift) % count) for i in range(count)])]
    all_to_all x1, waiting for transfers between devices: 3.78 us -> 0.01 us  [on_device(): pencil = lax.all_to_all(y_spec, 'gx', 0, 0, tiled=True)]
    all_to_all x3 -> x1, waiting for transfers between devices: 3.68 us -> 0.23 us  [on_device(): line = lax.all_to_all(back, 'gx', 0, 0, tiled=True)]
    concatenate x2 -> x0, other arithmetic: 3.28 us -> none  [the longest x1 1.66 us: on_device(): jnp.concatenate([y_low[-3:], coarse[-3:], y_high[-3:]], axis=1)]
    slice x4 -> x0, local copies, waits for them, and re-layouts: 2.69 us -> none  [the longest x1 0.75 us: on_device(): coarse[:3]]
  transfers between devices with their start and end apart: 8 -> 10, of which waited for: 3 -> 3; matrix products, arithmetic and copies ran while one was open for 10% -> 3% of each run, Pallas kernels for 25% -> 35%
where the time goes in v1:
time: 62.1 us; the launch traced here: 61.6 us
  Pallas kernels  32.7 us (53%)
  starting transfers between devices  25.7 us (41%)
  local copies, waits for them, and re-layouts  1.62 us (3%)
  waiting for transfers between devices  1.42 us (2%)
    pallas_call x8, Pallas kernels, call(): pl.pallas_call(body, out_shape=outs, in_specs=specs, out_specs=out_specs,...  32.7 us
    ppermute x6, starting transfers between devices, ring(): lax.ppermute(value, axis, [(i, (i + shift) % count) for i in range(count)])  10.1 us
    all_to_all x1, starting transfers between devices, on_device(): line = lax.all_to_all(back, 'gx', 0, 0, tiled=True)  6.96 us
    all_to_all x1, starting transfers between devices, on_device(): pencil = lax.all_to_all(y_spec, 'gx', 0, 0, tiled=True)  4.88 us
    ppermute x1, starting transfers between devices, on_device(): x_low = lax.ppermute(up, 'gx', [(i, i + 1) for i in range(devices_x - 1)])  2.41 us
    ppermute x1, starting transfers between devices, on_device(): lax.ppermute(down, 'gx', [(i + 1, i) for i in range(devices_x - 1)])  1.29 us
  transfers between devices with their start and end apart: 10, of which 3 were waited for; matrix products, arithmetic and copies ran while one was open for 3% of the time, Pallas kernels for 35%

profile of v1, /device:TPU:0, one launch (start us, length us, event | category | flops | bytes accessed | tf_op | source)
XLA Modules:
  0.0 61.6 jit_solution(14418868679740713624)
XLA Ops:
  0.0 0.0 copy-start
  0.0 3.7 %shard_map.154 = (bf16[160,128]{1,0:T(8,128)(2,1)S(1)}, bf16[352,128]{1,0:T(8,128)(2,1)S(1)}, bf16[352,128]{1,0:T(8,128)(2,1)S(1)}, bf16[160,128]{1,0:T(8,128)(2...) custom-call(bf16[20,8,32,128]{3,2,1,0:T(8,128)(2,1)} %field.1, ...), custom_call_target="tpu_custom_call" | custom-call | flops 1000000000 | bytes 1000000 | tf_op jit(solution)/shard_map/pallas_call | solution.py:133
  3.7 3.0 %collective-permute-start = (bf16[352,128]{1,0:T(8,128)(2,1)S(1)}, bf16[352,128]{1,0:T(8,128)(2,1)S(1)}, u32[]{:S(2)}, u32[]{:S(2)}) collective-permute-start(bf16[352,128]{1,0:T(8,128)(2,1)S(1)} %get-tuple-element.26), channel_id=1, source_target_pairs={{0,1},{1,2},{2,3},{3,0},{4,5},{5,6},{6,7},{7,4},{8,9},{9,10},{10,1... | collective-permute-start | bytes 270344 | tf_op jit(solution)/shard_map/ppermute | solution.py:655
  6.7 1.0 %collective-permute-start.1 = (bf16[352,128]{1,0:T(8,128)(2,1)S(1)}, bf16[352,128]{1,0:T(8,128)(2,1)S(1)}, u32[]{:S(2)}, u32[]{:S(2)}) collective-permute-start(bf16[352,128]{1,0:T(8,128)(2,1)S(1)} %get-tuple-element.27), channel_id=1, source_target_pairs={{0,3},{1,0},{2,1},{3,2},{4,7},{5,4},{6,5},{7,6},{8,11},{9,8},{10,9... | collective-permute-start | bytes 270344 | tf_op jit(solution)/shard_map/ppermute | solution.py:655
  7.7 0.0 copy-start.1
  7.7 1.9 %collective-permute-start.2 = (bf16[160,128]{1,0:T(8,128)(2,1)S(1)}, bf16[160,128]{1,0:T(8,128)(2,1)S(1)}, u32[]{:S(2)}, u32[]{:S(2)}) collective-permute-start(bf16[160,128]{1,0:T(8,128)(2,1)S(1)} %get-tuple-element.28), channel_id=1, source_target_pairs={{0,2},{1,3},{2,0},{3,1},{4,6},{5,7},{6,4},{7,5},{8,10},{9,11},{10,... | collective-permute-start | bytes 122888 | tf_op jit(solution)/shard_map/ppermute | solution.py:655
  9.7 0.0 copy-done
  9.7 0.6 copy.19
  10.3 0.1 pad_bitcast_fusion
  10.4 0.2 copy.25
  10.5 0.6 %reshape.8.filters = bf16[3,72,216]{2,1,0:T(8,128)(2,1)S(1)} reshape(bf16[3,3,24,9,24]{4,3,2,1,0:T(8,128)(2,1)S(1)} %copy.25) | data formatting | bytes 186624 | tf_op jit(solution)/shard_map/reshape | solution.py:713
  11.2 0.0 copy-done.1
  11.2 0.1 copy.21
  11.3 0.4 collective-permute-done.2.rest_0_
  11.7 0.0 collective-permute-done.low_message
  11.7 0.7 %collective-permute-done.1.high_message = bf16[352,128]{1,0:T(8,128)(2,1)S(1)} collective-permute-done((bf16[352,128]{1,0:T(8,128)(2,1)S(1)}, bf16[352,128]{1,0:T(8,128)(2,1)S(1)}, u32[]{:S(2)}, u32[]{:S(2)}) %collective-permute-start.1) | collective-permute-done | bytes 90144 | tf_op jit(solution)/shard_map/ppermute | solution.py:655
  12.5 1.1 %shard_map.155 = (bf16[8,5,16,128]{3,2,1,0:T(8,128)(2,1)}, bf16[3,12,24,128]{3,2,1,0:T(8,128)(2,1)}, bf16[3,12,24,128]{3,2,1,0:T(8,128)(2,1)}, bf16[4,12,24,128]{3,2,1,0:T(8,128)(2,1)S(1)}) custom-call(bf16[160,128]{1,0:T(8,128)(2,1)S(1)} %get-tuple-element.25.own, bf16[352,128]{1,0:T(8,128)(2,1)S(1)} %collective-permute-done.low_message, ...), custom_call_target="tpu_custom_call" | custom-call | flops 1000000000 | bytes 1000000 | tf_op jit(solution)/shard_map/pallas_call | solution.py:133
  13.5 4.9 %all-to-all-start = ((bf16[8,5,16,128]{3,2,1,0:T(8,128)(2,1)}), bf16[8,5,16,128]{3,2,1,0:T(8,128)(2,1)S(1)}, u32[]{:S(2)}, u32[]{:S(2)}) async-start(bf16[8,5,16,128]{3,2,1,0:T(8,128)(2,1)} %get-tuple-element.32.after), calls=%async_computation | async-start | bytes 327680 | tf_op jit(solution)/shard_map/all_to_all | solution.py:707
  18.4 0.0 copy-start.3
  18.4 0.0 copy-start.2
  18.4 7.1 %shard_map.156 = (bf16[20,2,20,16,128]{4,3,2,1,0:T(8,128)(2,1)}, f32[4,72,1280]{2,1,0:T(8,128)}, bf16[320,512]{1,0:T(8,128)(2,1)}) custom-call(bf16[8,5,16,128]{3,2,1,0:T(8,128)(2,1)} %get-tuple-element.32.after, bf16[4,12,24,128]{3,2,1,0:T(8,128)(2,1)S(1)} %get-tuple-element.33.volume_in, bf16[3,72,216]{2,1,0:T(8,128)(2,1)S(1)} %reshape.8.filters, ...), custom_call_target="tpu_custom_call" | custom-call | flops 4000000000 | bytes 16000000 | tf_op jit(solution)/shard_map/pallas_call | solution.py:133
  25.6 0.0 copy-done.3
  25.6 2.4 %collective-permute-start.3 = (bf16[3,12,24,128]{3,2,1,0:T(8,128)(2,1)S(1)}, bf16[3,12,24,128]{3,2,1,0:T(8,128)(2,1)S(1)}, u32[]{:S(2)}, u32[]{:S(2)}) collective-permute-start(bf16[3,12,24,128]{3,2,1,0:T(8,128)(2,1)S(1)} %copy-done.3), channel_id=1, source_target_pairs={{0,4},{4,8},{8,12},{12,16},{16,20},{20,24},{24,28},{1,5},{5,9},{9,... | collective-permute-start | bytes 663560 | tf_op jit(solution)/shard_map/ppermute | solution.py:748
  28.0 0.0 copy-done.2
  28.0 1.3 %collective-permute-start.4 = (bf16[3,12,24,128]{3,2,1,0:T(8,128)(2,1)S(1)}, bf16[3,12,24,128]{3,2,1,0:T(8,128)(2,1)S(1)}, u32[]{:S(2)}, u32[]{:S(2)}) collective-permute-start(bf16[3,12,24,128]{3,2,1,0:T(8,128)(2,1)S(1)} %copy-done.2), channel_id=1, source_target_pairs={{4,0},{8,4},{12,8},{16,12},{20,16},{24,20},{28,24},{5,1},{9,5},{13... | collective-permute-start | bytes 663560 | tf_op jit(solution)/shard_map/ppermute | solution.py:749
  29.3 0.0 all-to-all-done.pencil
  29.3 4.5 %shard_map.157.after = bf16[8,5,16,128]{3,2,1,0:T(8,128)(2,1)} custom-call(bf16[8,5,16,128]{3,2,1,0:T(8,128)(2,1)S(1)} %all-to-all-done.pencil, bf16[1024,1024]{1,0:T(8,128)(2,1)} %constant.29.clone.forward_in, bf16[20,2,20,16,128]{4,3,2,1,0:T(8,128)(2,1)} %get-tuple-element.34.packed_in, bf16[1024,1024]{1,0:T(8,128)(2,1)} %constant.30.clone.inverse_in), custom_call_target="tpu_custom_call" | custom-call | flops 1000000000 | bytes 1000000 | tf_op jit(solution)/shard_map/pallas_call | solution.py:133
  33.9 7.0 %all-to-all-start.1 = ((bf16[8,5,16,128]{3,2,1,0:T(8,128)(2,1)}), bf16[8,5,16,128]{3,2,1,0:T(8,128)(2,1)S(1)}, u32[]{:S(2)}, u32[]{:S(2)}) async-start(bf16[8,5,16,128]{3,2,1,0:T(8,128)(2,1)} %shard_map.157.after), calls=%async_computation.1 | async-start | bytes 327680 | tf_op jit(solution)/shard_map/all_to_all | solution.py:770
  40.8 0.0 collective-permute-done.3.x_low
  40.8 0.0 collective-permute-done.4.x_high
  40.9 7.0 %shard_map.159.second = f32[6,12,24,128]{3,2,1,0:T(8,128)S(1)} custom-call(bf16[8,5,16,128]{3,2,1,0:T(8,128)(2,1)} %shard_map.157.after, bf16[3,12,24,128]{3,2,1,0:T(8,128)(2,1)S(1)} %collective-permute-done.3.x_low, bf16[3,12,24,128]{3,2,1,0:T(8,128)(2,1)S(1)} %collective-permute-done.4.x_high, f32[4,72,1280]{2,1,0:T(8,128)} %get-tuple-element.41.own, ...), custom_call_target="tpu_custom_call" | custom-call | flops 6000000000 | bytes 1000000 | tf_op jit(solution)/shard_map/pallas_call | solution.py:133
  47.8 0.2 all-to-all-done.1.line
  48.1 1.2 %shard_map.158 = (bf16[160,128]{1,0:T(8,128)(2,1)S(1)}, bf16[160,128]{1,0:T(8,128)(2,1)S(1)}, bf16[160,128]{1,0:T(8,128)(2,1)S(1)}, bf16[160,128]{1,0:T(8,128)(2,1)S(1)}) custom-call(bf16[8,5,16,128]{3,2,1,0:T(8,128)(2,1)S(1)} %all-to-all-done.1.line, bf16[128,256]{1,0:T(8,128)(2,1)} %constant.27.clone.ytable_in.table_in, ...), custom_call_target="tpu_custom_call" | custom-call | flops 1000000000 | bytes 1000000 | tf_op jit(solution)/shard_map/pallas_call | solution.py:133
  49.3 1.7 %collective-permute-start.5 = (bf16[160,128]{1,0:T(8,128)(2,1)S(1)}, bf16[160,128]{1,0:T(8,128)(2,1)S(1)}, u32[]{:S(2)}, u32[]{:S(2)}) collective-permute-start(bf16[160,128]{1,0:T(8,128)(2,1)S(1)} %get-tuple-element.42), channel_id=1, source_target_pairs={{0,1},{1,2},{2,3},{3,0},{4,5},{5,6},{6,7},{7,4},{8,9},{9,10},{10,1... | collective-permute-start | bytes 122888 | tf_op jit(solution)/shard_map/ppermute | solution.py:655
  51.0 0.9 %collective-permute-start.6 = (bf16[160,128]{1,0:T(8,128)(2,1)S(1)}, bf16[160,128]{1,0:T(8,128)(2,1)S(1)}, u32[]{:S(2)}, u32[]{:S(2)}) collective-permute-start(bf16[160,128]{1,0:T(8,128)(2,1)S(1)} %get-tuple-element.43), channel_id=1, source_target_pairs={{0,2},{1,3},{2,0},{3,1},{4,6},{5,7},{6,4},{7,5},{8,10},{9,11},{10,... | collective-permute-start | bytes 122888 | tf_op jit(solution)/shard_map/ppermute | solution.py:655
  52.0 1.5 %collective-permute-start.7 = (bf16[160,128]{1,0:T(8,128)(2,1)S(1)}, bf16[160,128]{1,0:T(8,128)(2,1)S(1)}, u32[]{:S(2)}, u32[]{:S(2)}) collective-permute-start(bf16[160,128]{1,0:T(8,128)(2,1)S(1)} %get-tuple-element.44), channel_id=1, source_target_pairs={{0,3},{1,0},{2,1},{3,2},{4,7},{5,4},{6,5},{7,6},{8,11},{9,8},{10,9... | collective-permute-start | bytes 122888 | tf_op jit(solution)/shard_map/ppermute | solution.py:655
  53.5 3.1 %shard_map.160.third = bf16[4,16,24,128]{3,2,1,0:T(8,128)(2,1)S(1)} custom-call(bf16[160,128]{1,0:T(8,128)(2,1)S(1)} %get-tuple-element.35.after.own, f32[6,12,24,128]{3,2,1,0:T(8,128)S(1)} %shard_map.159.second, bf16[3,72,216]{2,1,0:T(8,128)(2,1)S(1)} %reshape.8.filters), custom_call_target="tpu_custom_call" | custom-call | flops 3000000000 | bytes 1000000 | tf_op jit(solution)/shard_map/pallas_call | solution.py:133
  56.6 0.0 collective-permute-done.5.rest_0_
  56.7 0.0 collective-permute-done.6.rest_1_
  56.7 0.0 collective-permute-done.7.rest_2_
  56.7 4.9 %shard_map.161 = bf16[20,8,32,128]{3,2,1,0:T(8,128)(2,1)} custom-call(bf16[20,8,32,128]{3,2,1,0:T(8,128)(2,1)} %field.1, bf16[4,16,24,128]{3,2,1,0:T(8,128)(2,1)S(1)} %shard_map.160.third, bf16[320,512]{1,0:T(8,128)(2,1)} %get-tuple-element.38.lift, bf16[512,512]{1,0:T(8,128)(2,1)} %constant.24.clone.regroup_in.regroup, ...), custom_call_target="tpu_custom_call" | custom-call | flops 1000000000 | bytes 1000000 | tf_op jit(solution)/shard_map/pallas_call | solution.py:133
Async XLA Ops:
  0.0 9.7 %copy-start = (bf16[3,27,20,20]{1,3,2,0:T(8,128)(2,1)S(1)}, bf16[3,27,20,20]{1,3,2,0:T(8,128)(2,1)}, u32[]{:S(2)}) copy-start(bf16[3,27,20,20]{1,3,2,0:T(8,128)(2,1)} %param.18) | copy-start | bytes 194404
  3.7 8.0 %collective-permute-start = (bf16[352,128]{1,0:T(8,128)(2,1)S(1)}, bf16[352,128]{1,0:T(8,128)(2,1)S(1)}, u32[]{:S(2)}, u32[]{:S(2)}) collective-permute-start(bf16[352,128]{1,0:T(8,128)(2,1)S(1)} %get-tuple-element.26), channel_id=1, source_target_pairs={{0,1},{1,2},{2,3},{3,0},{4,5},{5,6},{6,7},{7,4},{8,9},{9,10},{10,1... | collective-permute-start | bytes 270344 | tf_op jit(solution)/shard_map/ppermute | solution.py:655
  6.7 5.8 %collective-permute-start.1 = (bf16[352,128]{1,0:T(8,128)(2,1)S(1)}, bf16[352,128]{1,0:T(8,128)(2,1)S(1)}, u32[]{:S(2)}, u32[]{:S(2)}) collective-permute-start(bf16[352,128]{1,0:T(8,128)(2,1)S(1)} %get-tuple-element.27), channel_id=1, source_target_pairs={{0,3},{1,0},{2,1},{3,2},{4,7},{5,4},{6,5},{7,6},{8,11},{9,8},{10,9... | collective-permute-start | bytes 270344 | tf_op jit(solution)/shard_map/ppermute | solution.py:655
  7.7 3.5 %copy-start.1 = (bf16[20,20]{1,0:T(8,128)(2,1)S(1)}, bf16[20,20]{1,0:T(8,128)(2,1)}, u32[]{:S(2)}) copy-start(bf16[20,20]{1,0:T(8,128)(2,1)} %param.19) | copy-start | bytes 2404
  7.7 4.0 %collective-permute-start.2 = (bf16[160,128]{1,0:T(8,128)(2,1)S(1)}, bf16[160,128]{1,0:T(8,128)(2,1)S(1)}, u32[]{:S(2)}, u32[]{:S(2)}) collective-permute-start(bf16[160,128]{1,0:T(8,128)(2,1)S(1)} %get-tuple-element.28), channel_id=1, source_target_pairs={{0,2},{1,3},{2,0},{3,1},{4,6},{5,7},{6,4},{7,5},{8,10},{9,11},{10,... | collective-permute-start | bytes 122888 | tf_op jit(solution)/shard_map/ppermute | solution.py:655
  13.5 15.8 %all-to-all-start = ((bf16[8,5,16,128]{3,2,1,0:T(8,128)(2,1)}), bf16[8,5,16,128]{3,2,1,0:T(8,128)(2,1)S(1)}, u32[]{:S(2)}, u32[]{:S(2)}) async-start(bf16[8,5,16,128]{3,2,1,0:T(8,128)(2,1)} %get-tuple-element.32.after), calls=%async_computation | async-start | bytes 327680 | tf_op jit(solution)/shard_map/all_to_all | solution.py:707
  18.4 7.2 %copy-start.3 = (bf16[3,12,24,128]{3,2,1,0:T(8,128)(2,1)S(1)}, bf16[3,12,24,128]{3,2,1,0:T(8,128)(2,1)}, u32[]{:S(2)}) copy-start(bf16[3,12,24,128]{3,2,1,0:T(8,128)(2,1)} %get-tuple-element.39) | copy-start | bytes 663556
  18.4 9.6 %copy-start.2 = (bf16[3,12,24,128]{3,2,1,0:T(8,128)(2,1)S(1)}, bf16[3,12,24,128]{3,2,1,0:T(8,128)(2,1)}, u32[]{:S(2)}) copy-start(bf16[3,12,24,128]{3,2,1,0:T(8,128)(2,1)} %get-tuple-element.40) | copy-start | bytes 663556
  25.6 15.2 %collective-permute-start.3 = (bf16[3,12,24,128]{3,2,1,0:T(8,128)(2,1)S(1)}, bf16[3,12,24,128]{3,2,1,0:T(8,128)(2,1)S(1)}, u32[]{:S(2)}, u32[]{:S(2)}) collective-permute-start(bf16[3,12,24,128]{3,2,1,0:T(8,128)(2,1)S(1)} %copy-done.3), channel_id=1, source_target_pairs={{0,4},{4,8},{8,12},{12,16},{16,20},{20,24},{24,28},{1,5},{5,9},{9,... | collective-permute-start | bytes 663560 | tf_op jit(solution)/shard_map/ppermute | solution.py:748
  28.0 12.8 %collective-permute-start.4 = (bf16[3,12,24,128]{3,2,1,0:T(8,128)(2,1)S(1)}, bf16[3,12,24,128]{3,2,1,0:T(8,128)(2,1)S(1)}, u32[]{:S(2)}, u32[]{:S(2)}) collective-permute-start(bf16[3,12,24,128]{3,2,1,0:T(8,128)(2,1)S(1)} %copy-done.2), channel_id=1, source_target_pairs={{4,0},{8,4},{12,8},{16,12},{20,16},{24,20},{28,24},{5,1},{9,5},{13... | collective-permute-start | bytes 663560 | tf_op jit(solution)/shard_map/ppermute | solution.py:749
  33.9 14.2 %all-to-all-start.1 = ((bf16[8,5,16,128]{3,2,1,0:T(8,128)(2,1)}), bf16[8,5,16,128]{3,2,1,0:T(8,128)(2,1)S(1)}, u32[]{:S(2)}, u32[]{:S(2)}) async-start(bf16[8,5,16,128]{3,2,1,0:T(8,128)(2,1)} %shard_map.157.after), calls=%async_computation.1 | async-start | bytes 327680 | tf_op jit(solution)/shard_map/all_to_all | solution.py:770
  49.3 7.3 %collective-permute-start.5 = (bf16[160,128]{1,0:T(8,128)(2,1)S(1)}, bf16[160,128]{1,0:T(8,128)(2,1)S(1)}, u32[]{:S(2)}, u32[]{:S(2)}) collective-permute-start(bf16[160,128]{1,0:T(8,128)(2,1)S(1)} %get-tuple-element.42), channel_id=1, source_target_pairs={{0,1},{1,2},{2,3},{3,0},{4,5},{5,6},{6,7},{7,4},{8,9},{9,10},{10,1... | collective-permute-start | bytes 122888 | tf_op jit(solution)/shard_map/ppermute | solution.py:655
  51.0 5.6 %collective-permute-start.6 = (bf16[160,128]{1,0:T(8,128)(2,1)S(1)}, bf16[160,128]{1,0:T(8,128)(2,1)S(1)}, u32[]{:S(2)}, u32[]{:S(2)}) collective-permute-start(bf16[160,128]{1,0:T(8,128)(2,1)S(1)} %get-tuple-element.43), channel_id=1, source_target_pairs={{0,2},{1,3},{2,0},{3,1},{4,6},{5,7},{6,4},{7,5},{8,10},{9,11},{10,... | collective-permute-start | bytes 122888 | tf_op jit(solution)/shard_map/ppermute | solution.py:655
  52.0 4.7 %collective-permute-start.7 = (bf16[160,128]{1,0:T(8,128)(2,1)S(1)}, bf16[160,128]{1,0:T(8,128)(2,1)S(1)}, u32[]{:S(2)}, u32[]{:S(2)}) collective-permute-start(bf16[160,128]{1,0:T(8,128)(2,1)S(1)} %get-tuple-element.44), channel_id=1, source_target_pairs={{0,3},{1,0},{2,1},{3,2},{4,7},{5,4},{6,5},{7,6},{8,11},{9,8},{10,9... | collective-permute-start | bytes 122888 | tf_op jit(solution)/shard_map/ppermute | solution.py:655

commit v2 on v1

--- a/solution.py
+++ b/solution.py
@@ -82,19 +82,18 @@
         cos, sin = phase(signed_modes(self.my), self.gy)
         return const(np.concatenate([cos.T, sin.T], 1))
 
+    def turn_x(self, sign):
+        cos, sin = phase(signed_modes(self.kx), self.gx)
+        turn = np.stack([np.stack([cos, -sign * sin]), np.stack([sign * sin, cos])])
+        return turn.reshape(2, 2, self.kx, self.dx, self.cx)
+
     def forward_x(self):
-        cos, sin = phase(signed_modes(self.kx), self.gx)
-        turn = np.stack([np.stack([cos, -sin]), np.stack([sin, cos])])
-        turn = turn.reshape(2, 2, self.kx, self.dx, self.cx)
-        out = np.einsum("pqjsx,gh,kl->sgpkxhqlj", turn, np.eye(self.groups), np.eye(self.kz))
-        return const(out.reshape(self.dx * LANES, self.groups * self.kz * 2 * self.kx))
+        out = np.einsum("pqjsx,g,kl->sgpkxqlj", self.turn_x(1.0), np.ones(self.groups), np.eye(self.kz))
+        return const(out.reshape(self.dx * LANES, self.kz * 2 * self.kx))
 
     def inverse_x(self):
-        cos, sin = phase(signed_modes(self.kx), self.gx)
-        turn = np.stack([np.stack([cos, sin]), np.stack([-sin, cos])])
-        turn = turn.reshape(2, 2, self.kx, self.dx, self.cx)
-        out = np.einsum("pqjsx,gh,kl->gpkjshqlx", turn, np.eye(self.groups), np.eye(self.kz))
-        return const(out.reshape(self.groups * self.kz * 2 * self.kx, self.dx * LANES))
+        out = np.einsum("pqjsx,h,kl->pkjshqlx", self.turn_x(-1.0), np.ones(self.groups), np.eye(self.kz))
+        return const(out.reshape(self.kz * 2 * self.kx, self.dx * LANES))
 
 
 VMEM = pl.BlockSpec(memory_space=pltpu.VMEM)
@@ -150,9 +149,13 @@
 
 
 def first_body(
-    plan, field_in, table_in, regroup_in, rows_in, pair_in, ytable_in, swap_in,
-    own, low_message, high_message, *rest,
+    plan, field_in, table_in, regroup_in, rows_in, pair_in, ytable_in, swap_in, *rest
 ):
+    weight = held = None
+    if len(rest) > plan.dy + 11:
+        weight, *rest, held, held_sems = rest
+        packed = rest.pop(plan.dy + 3)
+    own, low_message, high_message, *rest = rest
     middle = rest[: plan.dy - 3]
     coarse, ytable, swap, field, table, regroup, rows_table, pair_table, chunks, sems = rest[
         plan.dy - 3 :
@@ -164,6 +167,8 @@
     ]
     for copy in copies:
         copy.start()
+    if held is not None:
+        start_weights(weight, held, held_sems, 0)
     for copy in copies[:3]:
         copy.wait()
     rows = plan.channels * plan.cy
@@ -195,6 +200,8 @@
             low_message[at] = coarse[x, tiles - 2 + j]
             high_message[at] = coarse[x, j]
             index += 1
+    if held is not None:
+        pack_weights(plan, weight, held, held_sems, 0, packed)
 
 
 def y_transform(plan, line, table, swap):
@@ -207,7 +214,7 @@
 
 def forward_y_body(plan, own, low_message, high_message, *rest):
     middle = rest[: plan.dy - 3]
-    coarse, table, swap, out, up, down, volume, line = rest[plan.dy - 3 :]
+    coarse, table, swap, out, near, far, volume, line = rest[plan.dy - 3 :]
     part = plan.cg * plan.cy
     here = lax.axis_index("gy")
     line[here] = own[...]
@@ -231,34 +238,24 @@
     nx = plan.cx // 2
     tiles = plan.cy // 4
     for x in range(nx):
-        planes = [volume.at[x]]
-        if x < 3:
-            planes.append(down.at[x])
-        if x >= nx - 3:
-            planes.append(up.at[x - nx + 3])
         for j in range(2):
             at = slice(part + (x * 2 + j) * CP, part + (x * 2 + j + 1) * CP)
-            low = jnp.where(here > 0, low_message[at], jnp.zeros((CP, LANES), BF16))
-            high = jnp.where(here < plan.dy - 1, high_message[at], jnp.zeros((CP, LANES), BF16))
-            for plane in planes:
-                plane[j] = low
-                plane[2 + tiles + j] = high
+            none = jnp.zeros((CP, LANES), BF16)
+            volume[x, j] = jnp.where(here > 0, low_message[at], none)
+            volume[x, 2 + tiles + j] = jnp.where(here < plan.dy - 1, high_message[at], none)
         for j in range(tiles):
-            for plane in planes:
-                plane[2 + j] = coarse[x, j]
-
-
-def inverse_y_body(plan, line, table_in, swap_in, own, *rest):
+            volume[x, 2 + j] = coarse[x, j]
+    even = lax.rem(lax.axis_index("gx"), 2) == 0
+    first_plane = jnp.where(even, nx - 3, 0)
+    last_plane = jnp.where(even, 0, nx - 3)
+    for x in range(3):
+        near[x] = volume[first_plane + x]
+        far[x] = volume[last_plane + x]
+
+
+def inverse_y_body(plan, line, table, swap, own, *rest):
     messages = rest[: plan.dy - 1]
-    table, swap, chunks, sems = rest[plan.dy - 1 :]
-    copies = [
-        pltpu.make_async_copy(swap_in, swap, sems.at[0]),
-        pltpu.make_async_copy(table_in, table, sems.at[1]),
-    ]
-    for copy in copies:
-        copy.start()
-    for copy in copies:
-        copy.wait()
+    chunks = rest[plan.dy - 1]
     sources = line.shape[0]
     values = [
         jnp.concatenate([line[s, c] for s in range(sources)], axis=0) for c in range(plan.cg)
@@ -293,60 +290,93 @@
     lax.fori_loop(0, plan.channels, step, 0)
 
 
+def weight_copy(weight, held, sems, begin, n):
+    return pltpu.make_async_copy(weight.at[:, begin + n], held.at[n], sems.at[n])
+
+
+def start_weights(weight, held, sems, begin):
+    def one(n, carry):
+        weight_copy(weight, held, sems, begin, n).start()
+        return carry
+
+    lax.fori_loop(0, held.shape[0], one, 0)
+
+
+def pack_weights(plan, weight, held, sems, begin, packed):
+    def one(n, carry):
+        weight_copy(weight, held, sems, begin, n).wait()
+        for p in range(2):
+            for o in range(plan.channels):
+                packed[n, p, o] = jnp.concatenate(
+                    [held[n, p, o, k] for k in range(plan.kz)], axis=1
+                ).astype(BF16)
+        return carry
+
+    lax.fori_loop(0, held.shape[0], one, 0)
+
+
 def window_body(
-    plan, steps, after, volume_in, filters, point, weight, packed, partial, lift, held, held_sems,
+    plan, begin, after, volume, filters, point, weight, forward_in, inverse_in,
+    packed, partial, lift, forward, inverse, held, sems, table_sems,
 ):
-    c = plan.channels
-    loads = [
-        pltpu.make_async_copy(
-            weight.at[:, :, pl.ds(n * steps, steps)],
-            held.at[:, :, pl.ds(n * steps, steps)],
-            held_sems.at[n],
-        )
-        for n in range(c // steps)
-    ]
-    for load in loads:
-        load.start()
-    conv_own_body(plan, volume_in, filters, point, partial, lift)
-    for n, load in enumerate(loads):
-        load.wait()
-        for o in range(n * steps, (n + 1) * steps):
-            for p in range(2):
-                for i in range(c):
-                    packed[o, p, i] = jnp.concatenate(
-                        [held[p, i, o, k] for k in range(plan.kz)], axis=1
-                    ).astype(BF16)
-
-
-def x_body(
-    plan, pencil, forward_in, packed_in, inverse_in, out, forward, packed, inverse, sems, spec, mixed
-):
-    halves = 2
-    block = plan.channels // halves
-    copies = [pltpu.make_async_copy(forward_in, forward, sems.at[0])]
-    for n in range(halves):
-        at = pl.ds(n * block, block)
-        copies.append(pltpu.make_async_copy(packed_in.at[at], packed.at[at], sems.at[n + 1]))
-    copies.append(pltpu.make_async_copy(inverse_in, inverse, sems.at[halves + 1]))
+    copies = prefetches((forward_in, inverse_in), (forward, inverse), table_sems)
     for copy in copies:
         copy.start()
-    copies[0].wait()
+    start_weights(weight, held, sems, begin)
+    conv_own_body(plan, volume, filters, point, partial, lift)
+    pack_weights(plan, weight, held, sems, begin, packed)
+    for copy in copies:
+        copy.wait()
+
+
+def lane_group(plan, shape):
+    return (lax.broadcasted_iota(jnp.int32, shape, 1) % LANES) // plan.unit
+
+
+def by_group(plan, lanes):
+    owner = lane_group(plan, lanes.shape)
+    return jnp.concatenate(
+        [jnp.where(owner == g, lanes, jnp.zeros_like(lanes)) for g in range(plan.groups)], axis=0
+    )
+
+
+def one_group(plan, stacked):
+    rows = stacked.shape[0] // plan.groups
+    owner = lane_group(plan, (rows, stacked.shape[1]))
+    result = stacked[:rows]
+    for g in range(1, plan.groups):
+        result = jnp.where(owner == g, stacked[g * rows : (g + 1) * rows], result)
+    return result
+
+
+def x_body(
+    plan, pencil, forward, packed_early, packed_late, inverse, weight, out,
+    packed, sems, held, held_sems, spec, mixed,
+):
+    early = packed_early.shape[0]
+    ready = packed.shape[0]
+    copies = [
+        pltpu.make_async_copy(packed_early, packed.at[pl.ds(0, early)], sems.at[0]),
+        pltpu.make_async_copy(packed_late, packed.at[pl.ds(early, ready - early)], sems.at[1]),
+    ]
+    for copy in copies:
+        copy.start()
+    start_weights(weight, held, held_sems, ready)
     rows = plan.cg * plan.ky
     wide = plan.kz * plan.kx
     lhs = jnp.concatenate([pencil[s].reshape(rows, LANES) for s in range(plan.dx)], axis=1)
-    spectrum = dot(lhs, forward[...])
+    spectrum = dot(by_group(plan, lhs), forward[...])
     for g in range(plan.groups):
         for p in range(2):
-            start = (g * 2 + p) * wide
-            modes = spectrum[:, start : start + wide].reshape(plan.cg, plan.ky, wide)
-            spec[p, g * plan.cg : (g + 1) * plan.cg] = modes
+            modes = spectrum[g * rows : (g + 1) * rows, p * wide : (p + 1) * wide]
+            spec[p, g * plan.cg : (g + 1) * plan.cg] = modes.reshape(plan.cg, plan.ky, wide)
 
     def step(o, carry):
         real = jnp.zeros((plan.ky, wide), F32)
         imag = jnp.zeros((plan.ky, wide), F32)
-        for i in range(plan.channels):
-            wr = packed[o, 0, i].astype(F32)
-            wi = packed[o, 1, i].astype(F32)
+        for i in range(ready):
+            wr = packed[i, 0, o].astype(F32)
+            wi = packed[i, 1, o].astype(F32)
             xr = spec[0, i]
             xi = spec[1, i]
             real += xr * wr - xi * wi
@@ -355,19 +385,37 @@
         mixed[1, o] = imag
         return carry
 
-    for n in range(halves):
-        copies[n + 1].wait()
-        lax.fori_loop(n * block, (n + 1) * block, step, 0)
-    copies[-1].wait()
+    def streamed(n, carry):
+        weight_copy(weight, held, held_sems, ready, n).wait()
+        xr = spec[0, ready + n]
+        xi = spec[1, ready + n]
+        for o in range(plan.channels):
+            wr, wi = (
+                jnp.concatenate([held[n, p, o, k] for k in range(plan.kz)], axis=1)
+                for p in range(2)
+            )
+            mixed[0, o] += xr * wr - xi * wi
+            mixed[1, o] += xr * wi + xi * wr
+        return carry
+
+    for copy in copies:
+        copy.wait()
+    lax.fori_loop(0, plan.channels, step, 0, unroll=2)
+    lax.fori_loop(0, plan.channels - ready, streamed, 0)
     back = jnp.concatenate(
         [
-            mixed[p, g * plan.cg : (g + 1) * plan.cg].reshape(rows, wide).astype(BF16)
+            jnp.concatenate(
+                [
+                    mixed[p, g * plan.cg : (g + 1) * plan.cg].reshape(rows, wide).astype(BF16)
+                    for p in range(2)
+                ],
+                axis=1,
+            )
             for g in range(plan.groups)
-            for p in range(2)
         ],
-        axis=1,
-    )
-    result = dot(back, inverse[...]).astype(BF16)
+        axis=0,
+    )
+    result = one_group(plan, dot(back, inverse[...])).astype(BF16)
     for d in range(plan.dx):
         out[d] = result[:, d * LANES : (d + 1) * LANES].reshape(plan.cg, plan.ky, LANES)
 
@@ -375,8 +423,8 @@
 def x_stage_general(plan, pencil, weight):
     groups, cg, ky, kz, kx = plan.groups, plan.cg, plan.ky, plan.kz, plan.kx
     lhs = jnp.transpose(pencil, (1, 2, 0, 3)).reshape(cg * ky, plan.dx * LANES)
-    spectrum = dot(lhs, plan.forward_x()).reshape(cg, ky, groups, 2, kz, kx)
-    spectrum = jnp.transpose(spectrum, (3, 4, 2, 0, 1, 5)).reshape(2, kz, groups * cg, ky, kx)
+    spectrum = dot(by_group(plan, lhs), plan.forward_x()).reshape(groups, cg, ky, 2, kz, kx)
+    spectrum = jnp.transpose(spectrum, (3, 4, 0, 1, 2, 5)).reshape(2, kz, groups * cg, ky, kx)
     mixed = call(
         functools.partial(mix, plan),
         jax.ShapeDtypeStruct((kz, groups * cg, ky, 2 * kx), F32),
@@ -384,9 +432,10 @@
         vmem=32,
         pin=False,
     )
-    back = jnp.transpose(mixed.reshape(kz, groups, cg, ky, 2, kx), (2, 3, 1, 4, 0, 5))
-    back = back.reshape(cg * ky, groups * kz * 2 * kx).astype(BF16)
-    back = dot(back, plan.inverse_x()).astype(BF16).reshape(cg, ky, plan.dx, LANES)
+    back = jnp.transpose(mixed.reshape(kz, groups, cg, ky, 2, kx), (1, 2, 3, 4, 0, 5))
+    back = back.reshape(groups * cg * ky, kz * 2 * kx).astype(BF16)
+    back = one_group(plan, dot(back, plan.inverse_x())).astype(BF16)
+    back = back.reshape(cg, ky, plan.dx, LANES)
     return jnp.transpose(back, (2, 0, 1, 3))
 
 
@@ -508,7 +557,7 @@
             volume[x, j] = value.astype(volume.dtype)
         return carry
 
-    lax.fori_loop(0, planes, body, 0)
+    lax.fori_loop(0, planes, body, 0, unroll=2)
 
 
 def where_bf16(mask):
@@ -546,18 +595,34 @@
         partial[x] = dot(filters[0], tap_columns(volume_in, x, (1, ny + 3)))
         return carry
 
-    lax.fori_loop(0, nx, body, 0)
-
-
-def conv_middle_body(plan, after, x_low, x_high, own, filters, second, partial, volume):
+    lax.fori_loop(0, nx, body, 0, unroll=2)
+
+
+def prefetches(sources, targets, sems):
+    return [
+        pltpu.make_async_copy(s, t, sems.at[n]) for n, (s, t) in enumerate(zip(sources, targets))
+    ]
+
+
+def conv_middle_body(
+    plan, after, near, far, own, filters, table_in, swap_in,
+    second, table, swap, partial, volume, sems,
+):
+    copies = prefetches((table_in, swap_in), (table, swap), sems)
+    for copy in copies:
+        copy.start()
     nx = plan.cx // 2
     ny = plan.cy // 4
     wide = ny + 4
     tiles = (1, ny + 3)
 
+    even = lax.rem(lax.axis_index("gx"), 2) == 0
+    near_at = jnp.where(even, 3 + nx, 0)
+    far_at = jnp.where(even, 0, 3 + nx)
+
     def edges(x, carry):
-        partial[x] = dot(filters[0], tap_columns(x_low, x, tiles))
-        partial[x + 3 + nx] = dot(filters[0], tap_columns(x_high, x, tiles))
+        partial[near_at + x] = dot(filters[0], tap_columns(near, x, tiles))
+        partial[far_at + x] = dot(filters[0], tap_columns(far, x, tiles))
         return carry
 
     lax.fori_loop(0, 3, edges, 0)
@@ -573,11 +638,17 @@
         partial[x] = dot(filters[1], tap_columns(volume, x, tiles))
         return carry
 
-    lax.fori_loop(0, nx + 4, body, 0)
+    lax.fori_loop(0, nx + 4, body, 0, unroll=2)
     activate(plan, nx + 2, tiles, partial, second)
-
-
-def conv_last_body(plan, after, second, filters, third, partial):
+    for copy in copies:
+        copy.wait()
+
+
+def conv_last_body(plan, after, second, filters, *rest):
+    sources, third, targets, partial, sems = rest[:4], rest[4], rest[5:9], rest[9], rest[10]
+    copies = prefetches(sources, targets, sems)
+    for copy in copies:
+        copy.start()
     nx = plan.cx // 2
     ny = plan.cy // 4
     tiles = (2, ny + 2)
@@ -586,7 +657,7 @@
         partial[x] = dot(filters[2], tap_columns(second, x, tiles))
         return carry
 
-    lax.fori_loop(0, nx + 2, body, 0)
+    lax.fori_loop(0, nx + 2, body, 0, unroll=True)
 
     square = (LANES, 2 * LANES)
     spread = where_bf16(iota(square, 1) // 2 == iota(square, 0))
@@ -599,7 +670,9 @@
             third[x, 2 * j + 1] = wide[:, plan.cz :]
         return carry
 
-    lax.fori_loop(0, nx, up, 0)
+    lax.fori_loop(0, nx, up, 0, unroll=True)
+    for copy in copies:
+        copy.wait()
 
 
 def final_body(plan, field, third, lift, regroup, inverse, own, *rest):
@@ -676,16 +749,27 @@
     message = shape((part + nx * 2 * CP, LANES), BF16)
     outs = [chunk, message, message] + [chunk] * (devices_y - 3)
     outs += [shape((nx, ny, CP, cz), BF16)] + [shape(t.shape, BF16) for t in tables[4:]]
+    if split:
+        early, late = channels // 10, 3 * channels // 10
+        pack = lambda n: shape((n, 2, channels, plan.ky, LANES), BF16)
+        hold = lambda n: [
+            pltpu.VMEM((n, 2) + spectral_weight.shape[2:], F32), pltpu.SemaphoreType.DMA((n,))
+        ]
+    packs = [pack(early)] if split else []
     first = call(
         functools.partial(first_body, plan),
-        outs,
-        (features,) + tables,
+        outs + packs,
+        (features,) + tables + ((spectral_weight,) if split else ()),
+        out_specs=[VMEM] * len(outs) + [FAR] * len(packs),
         scratch=[pltpu.VMEM(features.shape, BF16)]
         + [pltpu.VMEM(t.shape, BF16) for t in tables[:4]]
-        + [pltpu.VMEM((devices_y, part, LANES), BF16), pltpu.SemaphoreType.DMA((7,))],
-        specs=[HBM] * 7,
+        + [pltpu.VMEM((devices_y, part, LANES), BF16), pltpu.SemaphoreType.DMA((7,))]
+        + (hold(early) if split else []),
+        specs=[HBM] * (7 + len(packs)),
         vmem=16,
     )
+    packed_early = first[-1]
+    first = first[: len(outs)]
     own, to_up, to_down = first[:3]
     middle = first[3:-3]
     coarse, y_table, y_swap = first[-3:]
@@ -695,7 +779,7 @@
 
     y_out = (devices_x, cg, plan.ky) if split else (1, cg, plan.my)
     planes = shape((3, ny + 4, CP, LANES), BF16)
-    y_spec, up, down, volume = call(
+    y_spec, near, far, volume = call(
         functools.partial(forward_y_body, plan),
         (shape(y_out + (LANES,), BF16), planes, planes, shape((nx, ny + 4, CP, LANES), BF16)),
         (own, low_message, high_message, *middle, coarse, y_table, y_swap),
@@ -718,22 +802,17 @@
     )
     local = (volume, filters, jnp.transpose(point_weight))
     if split:
-        steps = 2 if channels % 2 == 0 else 1
-        forward_x = plan.forward_x()
-        inverse_x = plan.inverse_x()
-        packed, partial_own, lift = call(
-            functools.partial(window_body, plan, steps),
-            (shape((channels, 2, channels, plan.ky, LANES), BF16),) + small,
-            (y_spec,) + local + (spectral_weight,),
-            specs=[ANY] + [VMEM, PLAIN, PLAIN] + [HBM],
-            out_specs=[FAR, FAR, FAR],
-            scratch=[
-                pltpu.VMEM(spectral_weight.shape, F32),
-                pltpu.SemaphoreType.DMA((channels // steps,)),
-            ],
-            vmem=24,
+        tables = (plan.forward_x(), plan.inverse_x())
+        packed_late, partial_own, lift, forward_x, inverse_x = call(
+            functools.partial(window_body, plan, early),
+            (pack(late),) + small + tuple(shape(t.shape, BF16) for t in tables),
+            (y_spec,) + local + (spectral_weight,) + tables,
+            specs=[ANY] + [VMEM, PLAIN, PLAIN] + [HBM] * 3,
+            out_specs=[FAR, FAR, FAR, VMEM, VMEM],
+            scratch=hold(late) + [pltpu.SemaphoreType.DMA((2,))],
+            vmem=12,
             flops=4e9,
-            moved=16e6,
+            moved=8e6,
         )
     else:
         partial_own, lift = call(
@@ -744,42 +823,44 @@
             out_specs=[FAR, FAR],
             flops=2e9,
         )
-    up, down = after((up, down), lift)
-    x_low = lax.ppermute(up, "gx", [(i, i + 1) for i in range(devices_x - 1)])
-    x_high = lax.ppermute(down, "gx", [(i + 1, i) for i in range(devices_x - 1)])
+    near, far = after((near, far), partial_own)
+    pairs = [(i, i ^ 1) for i in range(devices_x)]
+    near = lax.ppermute(near, "gx", pairs)
+    pairs = [(i, i + 1) for i in range(1, devices_x - 1, 2)]
+    far = lax.ppermute(far, "gx", pairs + [(t, s) for s, t in pairs])
 
     if split:
         back = call(
             functools.partial(x_body, plan),
             shape((devices_x, cg, plan.ky, LANES), BF16),
-            (pencil, forward_x, packed, inverse_x),
-            specs=[VMEM, HBM, HBM, HBM],
+            (pencil, forward_x, packed_early, packed_late, inverse_x, spectral_weight),
+            specs=[VMEM, VMEM, HBM, HBM, VMEM, HBM],
             out_specs=[PLAIN],
             scratch=[
-                pltpu.VMEM(forward_x.shape, BF16),
-                pltpu.VMEM(packed.shape, BF16),
-                pltpu.VMEM(inverse_x.shape, BF16),
-                pltpu.SemaphoreType.DMA((4,)),
-                pltpu.VMEM((2, channels, plan.ky, LANES), F32),
-                pltpu.VMEM((2, channels, plan.ky, LANES), F32),
-            ],
-            vmem=14,
+                pltpu.VMEM((early + late, 2, channels, plan.ky, LANES), BF16),
+                pltpu.SemaphoreType.DMA((2,)),
+            ]
+            + hold(channels - early - late)
+            + [pltpu.VMEM((2, channels, plan.ky, LANES), F32)] * 2,
+            vmem=20,
         )
     else:
         back = x_stage_general(plan, pencil, spectral_weight)
     line = lax.all_to_all(back, "gx", 0, 0, tiled=True)
 
-    second = call(
+    tables = (plan.inverse_y(), plan.swap(-1.0))
+    second, inverse_table, inverse_swap = call(
         functools.partial(conv_middle_body, plan),
-        shape((nx + 2, ny + 4, CP, LANES), F32),
-        (back, x_low, x_high, partial_own, filters),
+        [shape((nx + 2, ny + 4, CP, LANES), F32)] + [shape(t.shape, BF16) for t in tables],
+        (back, near, far, partial_own, filters) + tables,
         scratch=[
             pltpu.VMEM((nx + 6, 3 * CP, wide), F32),
             pltpu.VMEM((nx + 4, ny + 4, CP, LANES), F32),
+            pltpu.SemaphoreType.DMA((2,)),
         ],
-        specs=[ANY, PLAIN, PLAIN, FAR, PLAIN],
-        out_specs=[PLAIN],
-        vmem=7,
+        specs=[ANY, PLAIN, PLAIN, FAR, PLAIN, HBM, HBM],
+        out_specs=[PLAIN, VMEM, VMEM],
+        vmem=8,
         flops=6e9,
     )
     if not split:
@@ -787,34 +868,30 @@
     own, *messages = call(
         functools.partial(inverse_y_body, plan),
         [chunk] * devices_y,
-        (line, plan.inverse_y(), plan.swap(-1.0)),
-        specs=[VMEM, HBM, HBM],
+        (line, inverse_table, inverse_swap),
+        scratch=[pltpu.VMEM((devices_y, part, LANES), BF16)],
+    )
+    arrived = [ring(m, "gy", s + 1) for s, m in enumerate(messages)]
+    tables = (features, lift, plan.regroup(devices_y, plan.groups), plan.inverse_z())
+    third, *tables = call(
+        functools.partial(conv_last_body, plan),
+        [shape((nx, 2 * ny, CP, cz), BF16)] + [shape(t.shape, BF16) for t in tables],
+        (own, second, filters) + tables,
         scratch=[
-            pltpu.VMEM((plan.gy, 2 * plan.my), BF16),
-            pltpu.VMEM((LANES, LANES), BF16),
-            pltpu.VMEM((devices_y, part, LANES), BF16),
-            pltpu.SemaphoreType.DMA((2,)),
+            pltpu.VMEM((nx + 2, 3 * CP, ny * LANES), F32), pltpu.SemaphoreType.DMA((4,))
         ],
-    )
-    arrived = [ring(m, "gy", s + 1) for s, m in enumerate(messages)]
-    third = call(
-        functools.partial(conv_last_body, plan),
-        shape((nx, 2 * ny, CP, cz), BF16),
-        (own, second, filters),
-        scratch=[pltpu.VMEM((nx + 2, 3 * CP, ny * LANES), F32)],
-        specs=[ANY, PLAIN, PLAIN],
-        out_specs=[PLAIN],
+        specs=[ANY, PLAIN, PLAIN] + [HBM] * 4,
+        out_specs=[PLAIN] + [VMEM] * 4,
         flops=3e9,
     )
+    near = lambda array: pltpu.with_memory_space_constraint(array, pltpu.VMEM)
+    field, lift, regroup, inverse_z = (near(t) for t in tables)
 
     full = lambda array: pl.BlockSpec(array.shape, lambda s: (0,) * array.ndim)
-    regroup = plan.regroup(devices_y, plan.groups)
-    inverse_z = plan.inverse_z()
-    far = lambda array: pltpu.with_memory_space_constraint(jnp.asarray(array), pltpu.HBM)
     return call(
         functools.partial(final_body, plan),
         shape(features.shape, BF16),
-        (far(features), third, far(lift), far(regroup), far(inverse_z), own, *arrived),
+        (field, third, lift, regroup, inverse_z, own, *arrived),
         pin=False,
         grid=(nx,),
         specs=[

time: 62.1 us -> 54.3 us (0.87)
  Pallas kernels: 32.7 us -> 26.7 us
  starting transfers between devices: 25.7 us -> 21 us
  waiting for transfers between devices: 1.42 us -> 4.51 us
    pallas_call x8, Pallas kernels: 32.7 us -> 26.7 us  [call(): pl.pallas_call(body, out_shape=outs, in_specs=specs, out_specs=out_specs,...]
    ppermute x2, starting transfers between devices: 3.7 us -> 1.22 us  [the longest x1 0.66 us: on_device(): far = lax.ppermute(far, 'gx', pairs + [(t, s) for s, t in pairs])]
    all_to_all x1, starting transfers between devices: 6.96 us -> 4.74 us  [on_device(): line = lax.all_to_all(back, 'gx', 0, 0, tiled=True)]
    all_to_all x1, waiting for transfers between devices: 0.01 us -> 1.8 us  [on_device(): pencil = lax.all_to_all(y_spec, 'gx', 0, 0, tiled=True)]
    all_to_all x1, waiting for transfers between devices: 0.23 us -> 1.27 us  [on_device(): line = lax.all_to_all(back, 'gx', 0, 0, tiled=True)]
  transfers between devices with their start and end apart: 10 -> 10, of which waited for: 3 -> 5; matrix products, arithmetic and copies ran while one was open for 3% -> 3% of each run, Pallas kernels for 35% -> 32%
where the time goes in v2:
time: 54.3 us; the launch traced here: 53.9 us
  Pallas kernels  26.7 us (49%)
  starting transfers between devices  21 us (39%)
  waiting for transfers between devices  4.51 us (8%)
  local copies, waits for them, and re-layouts  1.62 us (3%)
    pallas_call x8, Pallas kernels, call(): pl.pallas_call(body, out_shape=outs, in_specs=specs, out_specs=out_specs,...  26.7 us
    ppermute x6, starting transfers between devices, ring(): lax.ppermute(value, axis, [(i, (i + shift) % count) for i in range(count)])  10.1 us
    all_to_all x1, starting transfers between devices, on_device(): pencil = lax.all_to_all(y_spec, 'gx', 0, 0, tiled=True)  4.88 us
    all_to_all x1, starting transfers between devices, on_device(): line = lax.all_to_all(back, 'gx', 0, 0, tiled=True)  4.74 us
    all_to_all x1, waiting for transfers between devices, on_device(): pencil = lax.all_to_all(y_spec, 'gx', 0, 0, tiled=True)  1.8 us
    ppermute x6, waiting for transfers between devices, ring(): lax.ppermute(value, axis, [(i, (i + shift) % count) for i in range(count)])  1.43 us
    all_to_all x1, waiting for transfers between devices, on_device(): line = lax.all_to_all(back, 'gx', 0, 0, tiled=True)  1.27 us
  transfers between devices with their start and end apart: 10, of which 5 were waited for; matrix products, arithmetic and copies ran while one was open for 3% of the time, Pallas kernels for 32%

profile of v2, /device:TPU:0, one launch (start us, length us, event | category | flops | bytes accessed | tf_op | source)
XLA Modules:
  0.0 53.9 jit_solution(2274052716878114387)
XLA Ops:
  0.0 0.0 copy-start
  0.0 4.7 %shard_map.154 = (bf16[160,128]{1,0:T(8,128)(2,1)S(1)}, bf16[352,128]{1,0:T(8,128)(2,1)S(1)}, bf16[352,128]{1,0:T(8,128)(2,1)S(1)}, bf16[160,128]{1,0:T(8,128)(2...) custom-call(bf16[20,8,32,128]{3,2,1,0:T(8,128)(2,1)} %rest_0_.3, ...), custom_call_target="tpu_custom_call" | custom-call | flops 1000000000 | bytes 1000000 | tf_op jit(solution)/shard_map/pallas_call | solution.py:132
  4.7 3.0 %collective-permute-start = (bf16[352,128]{1,0:T(8,128)(2,1)S(1)}, bf16[352,128]{1,0:T(8,128)(2,1)S(1)}, u32[]{:S(2)}, u32[]{:S(2)}) collective-permute-start(bf16[352,128]{1,0:T(8,128)(2,1)S(1)} %get-tuple-element.37), channel_id=1, source_target_pairs={{0,1},{1,2},{2,3},{3,0},{4,5},{5,6},{6,7},{7,4},{8,9},{9,10},{10,1... | collective-permute-start | bytes 270344 | tf_op jit(solution)/shard_map/ppermute | solution.py:728
  7.7 1.0 %collective-permute-start.1 = (bf16[352,128]{1,0:T(8,128)(2,1)S(1)}, bf16[352,128]{1,0:T(8,128)(2,1)S(1)}, u32[]{:S(2)}, u32[]{:S(2)}) collective-permute-start(bf16[352,128]{1,0:T(8,128)(2,1)S(1)} %get-tuple-element.38), channel_id=1, source_target_pairs={{0,3},{1,0},{2,1},{3,2},{4,7},{5,4},{6,5},{7,6},{8,11},{9,8},{10,9... | collective-permute-start | bytes 270344 | tf_op jit(solution)/shard_map/ppermute | solution.py:728
  8.7 1.9 %collective-permute-start.2 = (bf16[160,128]{1,0:T(8,128)(2,1)S(1)}, bf16[160,128]{1,0:T(8,128)(2,1)S(1)}, u32[]{:S(2)}, u32[]{:S(2)}) collective-permute-start(bf16[160,128]{1,0:T(8,128)(2,1)S(1)} %get-tuple-element.39), channel_id=1, source_target_pairs={{0,2},{1,3},{2,0},{3,1},{4,6},{5,7},{6,4},{7,5},{8,10},{9,11},{10,... | collective-permute-start | bytes 122888 | tf_op jit(solution)/shard_map/ppermute | solution.py:728
  10.6 0.0 copy-done
  10.6 0.6 %copy.19 = bf16[3,27,20,20]{3,2,1,0:T(8,128)(2,1)S(1)} copy(bf16[3,27,20,20]{1,3,2,0:T(8,128)(2,1)S(1)} %copy-done) | data formatting | bytes 129600 | tf_op args[2]
  11.2 0.1 pad_bitcast_fusion
  11.3 0.0 copy-start.1
  11.4 0.2 copy.25
  11.5 0.6 %reshape.8.filters = bf16[3,72,216]{2,1,0:T(8,128)(2,1)S(1)} reshape(bf16[3,3,24,9,24]{4,3,2,1,0:T(8,128)(2,1)S(1)} %copy.25) | data formatting | bytes 186624 | tf_op jit(solution)/shard_map/reshape | solution.py:797
  12.1 0.0 copy-done.1
  12.2 0.1 copy.21
  12.3 0.4 collective-permute-done.2.rest_0_
  12.7 0.0 collective-permute-done.low_message
  12.7 0.7 %collective-permute-done.1.high_message = bf16[352,128]{1,0:T(8,128)(2,1)S(1)} collective-permute-done((bf16[352,128]{1,0:T(8,128)(2,1)S(1)}, bf16[352,128]{1,0:T(8,128)(2,1)S(1)}, u32[]{:S(2)}, u32[]{:S(2)}) %collective-permute-start.1) | collective-permute-done | bytes 90144 | tf_op jit(solution)/shard_map/ppermute | solution.py:728
  13.4 1.1 %shard_map.155 = (bf16[8,5,16,128]{3,2,1,0:T(8,128)(2,1)}, bf16[3,12,24,128]{3,2,1,0:T(8,128)(2,1)}, bf16[3,12,24,128]{3,2,1,0:T(8,128)(2,1)}, bf16[4,12,24,128]{3,2,1,0:T(8,128)(2,1)S(1)}) custom-call(bf16[160,128]{1,0:T(8,128)(2,1)S(1)} %get-tuple-element.36.own, bf16[352,128]{1,0:T(8,128)(2,1)S(1)} %collective-permute-done.low_message, ...), custom_call_target="tpu_custom_call" | custom-call | flops 1000000000 | bytes 1000000 | tf_op jit(solution)/shard_map/pallas_call | solution.py:132
  14.5 4.9 %all-to-all-start = ((bf16[8,5,16,128]{3,2,1,0:T(8,128)(2,1)}), bf16[8,5,16,128]{3,2,1,0:T(8,128)(2,1)S(1)}, u32[]{:S(2)}, u32[]{:S(2)}) async-start(bf16[8,5,16,128]{3,2,1,0:T(8,128)(2,1)} %get-tuple-element.43.after), calls=%async_computation | async-start | bytes 327680 | tf_op jit(solution)/shard_map/all_to_all | solution.py:791
  19.4 0.0 copy-start.3
  19.4 0.0 copy-start.2
  19.4 4.2 %shard_map.156 = (bf16[6,2,20,16,128]{4,3,2,1,0:T(8,128)(2,1)}, f32[4,72,1280]{2,1,0:T(8,128)}, bf16[320,512]{1,0:T(8,128)(2,1)}, bf16[1024,256]{1,0:T(8,128)(2,1)S(1)}, bf16[256,1024]{1,0:T(8,128)(2,1)S(1)}) custom-call(bf16[8,5,16,128]{3,2,1,0:T(8,128)(2,1)} %get-tuple-element.43.after, bf16[4,12,24,128]{3,2,1,0:T(8,128)(2,1)S(1)} %get-tuple-element.44.volume, ...), custom_call_target="tpu_custom_call" | custom-call | flops 4000000000 | bytes 8000000 | tf_op jit(solution)/shard_map/pallas_call | solution.py:132
  23.6 0.0 copy-done.3
  23.6 0.6 %collective-permute-start.3 = (bf16[3,12,24,128]{3,2,1,0:T(8,128)(2,1)S(1)}, bf16[3,12,24,128]{3,2,1,0:T(8,128)(2,1)S(1)}, u32[]{:S(2)}, u32[]{:S(2)}) collective-permute-start(bf16[3,12,24,128]{3,2,1,0:T(8,128)(2,1)S(1)} %copy-done.3), channel_id=1, source_target_pairs={{0,4},{4,0},{8,12},{12,8},{16,20},{20,16},{24,28},{28,24},{1,5},{5... | collective-permute-start | bytes 663560 | tf_op jit(solution)/shard_map/ppermute | solution.py:828
  24.2 0.0 copy-done.2
  24.2 0.7 %collective-permute-start.4 = (bf16[3,12,24,128]{3,2,1,0:T(8,128)(2,1)S(1)}, bf16[3,12,24,128]{3,2,1,0:T(8,128)(2,1)S(1)}, u32[]{:S(2)}, u32[]{:S(2)}) collective-permute-start(bf16[3,12,24,128]{3,2,1,0:T(8,128)(2,1)S(1)} %copy-done.2), channel_id=1, source_target_pairs={{4,8},{12,16},{20,24},{8,4},{16,12},{24,20},{5,9},{13,17},{21,25},... | collective-permute-start | bytes 663560 | tf_op jit(solution)/shard_map/ppermute | solution.py:830
  24.8 1.8 %all-to-all-done.pencil = bf16[8,5,16,128]{3,2,1,0:T(8,128)(2,1)S(1)} async-done(((bf16[8,5,16,128]{3,2,1,0:T(8,128)(2,1)}), bf16[8,5,16,128]{3,2,1,0:T(8,128)(2,1)S(1)}, u32[]{:S(2)}, u32[]{:S(2)}) %all-to-all-start) | async-done | bytes 163872 | tf_op jit(solution)/shard_map/all_to_all | solution.py:791
  26.6 5.0 %shard_map.157.after = bf16[8,5,16,128]{3,2,1,0:T(8,128)(2,1)} custom-call(bf16[8,5,16,128]{3,2,1,0:T(8,128)(2,1)S(1)} %all-to-all-done.pencil, bf16[1024,256]{1,0:T(8,128)(2,1)S(1)} %get-tuple-element.45.forward, bf16[2,2,20,16,128]{4,3,2,1,0:T(8,128)(2,1)} %get-tuple-element.46.packed_early, bf16[6,2,20,16,128]{4,3,2,1,0:T(8,128)(2,1)} %get-tuple-element.47.packed_late, ...), custom_call_target="tpu_custom_call" | custom-call | flops 1000000000 | bytes 1000000 | tf_op jit(solution)/shard_map/pallas_call | solution.py:132
  31.7 4.7 %all-to-all-start.1 = ((bf16[8,5,16,128]{3,2,1,0:T(8,128)(2,1)}), bf16[8,5,16,128]{3,2,1,0:T(8,128)(2,1)S(1)}, u32[]{:S(2)}, u32[]{:S(2)}) async-start(bf16[8,5,16,128]{3,2,1,0:T(8,128)(2,1)} %shard_map.157.after), calls=%async_computation.1 | async-start | bytes 327680 | tf_op jit(solution)/shard_map/all_to_all | solution.py:849
  36.4 0.0 collective-permute-done.3.near
  36.4 0.0 collective-permute-done.4.far
  36.4 5.9 %shard_map.158 = (f32[6,12,24,128]{3,2,1,0:T(8,128)S(1)}, bf16[128,256]{1,0:T(8,128)(2,1)S(1)}, bf16[128,128]{1,0:T(8,128)(2,1)S(1)}) custom-call(bf16[8,5,16,128]{3,2,1,0:T(8,128)(2,1)} %shard_map.157.after, bf16[3,12,24,128]{3,2,1,0:T(8,128)(2,1)S(1)} %collective-permute-done.3.near, bf16[3,12,24,128]{3,2,1,0:T(8,128)(2,1)S(1)} %collective-permute-done.4.far, ...), custom_call_target="tpu_custom_call" | custom-call | flops 6000000000 | bytes 1000000 | tf_op jit(solution)/shard_map/pallas_call | solution.py:132
  42.4 1.3 %all-to-all-done.1.line = bf16[8,5,16,128]{3,2,1,0:T(8,128)(2,1)S(1)} async-done(((bf16[8,5,16,128]{3,2,1,0:T(8,128)(2,1)}), bf16[8,5,16,128]{3,2,1,0:T(8,128)(2,1)S(1)}, u32[]{:S(2)}, u32[]{:S(2)}) %all-to-all-start.1) | async-done | bytes 163872 | tf_op jit(solution)/shard_map/all_to_all | solution.py:849
  43.6 0.4 shard_map.159
  44.0 1.7 %collective-permute-start.5 = (bf16[160,128]{1,0:T(8,128)(2,1)S(1)}, bf16[160,128]{1,0:T(8,128)(2,1)S(1)}, u32[]{:S(2)}, u32[]{:S(2)}) collective-permute-start(bf16[160,128]{1,0:T(8,128)(2,1)S(1)} %get-tuple-element.64), channel_id=1, source_target_pairs={{0,1},{1,2},{2,3},{3,0},{4,5},{5,6},{6,7},{7,4},{8,9},{9,10},{10,1... | collective-permute-start | bytes 122888 | tf_op jit(solution)/shard_map/ppermute | solution.py:728
  45.7 0.9 %collective-permute-start.6 = (bf16[160,128]{1,0:T(8,128)(2,1)S(1)}, bf16[160,128]{1,0:T(8,128)(2,1)S(1)}, u32[]{:S(2)}, u32[]{:S(2)}) collective-permute-start(bf16[160,128]{1,0:T(8,128)(2,1)S(1)} %get-tuple-element.65), channel_id=1, source_target_pairs={{0,2},{1,3},{2,0},{3,1},{4,6},{5,7},{6,4},{7,5},{8,10},{9,11},{10,... | collective-permute-start | bytes 122888 | tf_op jit(solution)/shard_map/ppermute | solution.py:728
  46.7 1.5 %collective-permute-start.7 = (bf16[160,128]{1,0:T(8,128)(2,1)S(1)}, bf16[160,128]{1,0:T(8,128)(2,1)S(1)}, u32[]{:S(2)}, u32[]{:S(2)}) collective-permute-start(bf16[160,128]{1,0:T(8,128)(2,1)S(1)} %get-tuple-element.66), channel_id=1, source_target_pairs={{0,3},{1,0},{2,1},{3,2},{4,7},{5,4},{6,5},{7,6},{8,11},{9,8},{10,9... | collective-permute-start | bytes 122888 | tf_op jit(solution)/shard_map/ppermute | solution.py:728
  48.2 2.2 %shard_map.160 = (bf16[4,16,24,128]{3,2,1,0:T(8,128)(2,1)S(1)}, bf16[20,8,32,128]{3,2,1,0:T(8,128)(2,1)S(1)}, bf16[320,512]{1,0:T(8,128)(2,1)S(1)}, bf16[512,512]{1,0:T(8,128)(2,1)S(1)}, bf16[128,1024]{1,0:T(8,128)(2,1)S(1)}) custom-call(bf16[160,128]{1,0:T(8,128)(2,1)S(1)} %get-tuple-element.56.after.own, f32[6,12,24,128]{3,2,1,0:T(8,128)S(1)} %get-tuple-element.57.second, ...), custom_call_target="tpu_custom_call" | custom-call | flops 3000000000 | bytes 1000000 | tf_op jit(solution)/shard_map/pallas_call | solution.py:132
  50.4 0.0 collective-permute-done.5.rest_0_
  50.4 0.0 collective-permute-done.6.rest_1_
  50.4 0.3 collective-permute-done.7.rest_2_
  50.7 3.3 %shard_map.161 = bf16[20,8,32,128]{3,2,1,0:T(8,128)(2,1)} custom-call(bf16[20,8,32,128]{3,2,1,0:T(8,128)(2,1)S(1)} %get-tuple-element.59.field, bf16[4,16,24,128]{3,2,1,0:T(8,128)(2,1)S(1)} %get-tuple-element.60.third, bf16[320,512]{1,0:T(8,128)(2,1)S(1)} %get-tuple-element.61.lift, bf16[512,512]{1,0:T(8,128)(2,1)S(1)} %get-tuple-element.62.regroup, ...), custom_call_target="tpu_custom_call" | custom-call | flops 1000000000 | bytes 1000000 | tf_op jit(solution)/shard_map/pallas_call | solution.py:132
Async XLA Ops:
  0.0 10.6 %copy-start = (bf16[3,27,20,20]{1,3,2,0:T(8,128)(2,1)S(1)}, bf16[3,27,20,20]{1,3,2,0:T(8,128)(2,1)}, u32[]{:S(2)}) copy-start(bf16[3,27,20,20]{1,3,2,0:T(8,128)(2,1)} %param.18) | copy-start | bytes 194404
  4.7 8.0 %collective-permute-start = (bf16[352,128]{1,0:T(8,128)(2,1)S(1)}, bf16[352,128]{1,0:T(8,128)(2,1)S(1)}, u32[]{:S(2)}, u32[]{:S(2)}) collective-permute-start(bf16[352,128]{1,0:T(8,128)(2,1)S(1)} %get-tuple-element.37), channel_id=1, source_target_pairs={{0,1},{1,2},{2,3},{3,0},{4,5},{5,6},{6,7},{7,4},{8,9},{9,10},{10,1... | collective-permute-start | bytes 270344 | tf_op jit(solution)/shard_map/ppermute | solution.py:728
  7.7 5.8 %collective-permute-start.1 = (bf16[352,128]{1,0:T(8,128)(2,1)S(1)}, bf16[352,128]{1,0:T(8,128)(2,1)S(1)}, u32[]{:S(2)}, u32[]{:S(2)}) collective-permute-start(bf16[352,128]{1,0:T(8,128)(2,1)S(1)} %get-tuple-element.38), channel_id=1, source_target_pairs={{0,3},{1,0},{2,1},{3,2},{4,7},{5,4},{6,5},{7,6},{8,11},{9,8},{10,9... | collective-permute-start | bytes 270344 | tf_op jit(solution)/shard_map/ppermute | solution.py:728
  8.7 4.0 %collective-permute-start.2 = (bf16[160,128]{1,0:T(8,128)(2,1)S(1)}, bf16[160,128]{1,0:T(8,128)(2,1)S(1)}, u32[]{:S(2)}, u32[]{:S(2)}) collective-permute-start(bf16[160,128]{1,0:T(8,128)(2,1)S(1)} %get-tuple-element.39), channel_id=1, source_target_pairs={{0,2},{1,3},{2,0},{3,1},{4,6},{5,7},{6,4},{7,5},{8,10},{9,11},{10,... | collective-permute-start | bytes 122888 | tf_op jit(solution)/shard_map/ppermute | solution.py:728
  11.3 0.8 %copy-start.1 = (bf16[20,20]{1,0:T(8,128)(2,1)S(1)}, bf16[20,20]{1,0:T(8,128)(2,1)}, u32[]{:S(2)}) copy-start(bf16[20,20]{1,0:T(8,128)(2,1)} %param.19) | copy-start | bytes 2404
  14.5 12.1 %all-to-all-start = ((bf16[8,5,16,128]{3,2,1,0:T(8,128)(2,1)}), bf16[8,5,16,128]{3,2,1,0:T(8,128)(2,1)S(1)}, u32[]{:S(2)}, u32[]{:S(2)}) async-start(bf16[8,5,16,128]{3,2,1,0:T(8,128)(2,1)} %get-tuple-element.43.after), calls=%async_computation | async-start | bytes 327680 | tf_op jit(solution)/shard_map/all_to_all | solution.py:791
  19.4 4.2 %copy-start.3 = (bf16[3,12,24,128]{3,2,1,0:T(8,128)(2,1)S(1)}, bf16[3,12,24,128]{3,2,1,0:T(8,128)(2,1)}, u32[]{:S(2)}) copy-start(bf16[3,12,24,128]{3,2,1,0:T(8,128)(2,1)} %get-tuple-element.52) | copy-start | bytes 663556
  19.4 4.7 %copy-start.2 = (bf16[3,12,24,128]{3,2,1,0:T(8,128)(2,1)S(1)}, bf16[3,12,24,128]{3,2,1,0:T(8,128)(2,1)}, u32[]{:S(2)}) copy-start(bf16[3,12,24,128]{3,2,1,0:T(8,128)(2,1)} %get-tuple-element.53) | copy-start | bytes 663556
  23.6 12.8 %collective-permute-start.3 = (bf16[3,12,24,128]{3,2,1,0:T(8,128)(2,1)S(1)}, bf16[3,12,24,128]{3,2,1,0:T(8,128)(2,1)S(1)}, u32[]{:S(2)}, u32[]{:S(2)}) collective-permute-start(bf16[3,12,24,128]{3,2,1,0:T(8,128)(2,1)S(1)} %copy-done.3), channel_id=1, source_target_pairs={{0,4},{4,0},{8,12},{12,8},{16,20},{20,16},{24,28},{28,24},{1,5},{5... | collective-permute-start | bytes 663560 | tf_op jit(solution)/shard_map/ppermute | solution.py:828
  24.2 12.3 %collective-permute-start.4 = (bf16[3,12,24,128]{3,2,1,0:T(8,128)(2,1)S(1)}, bf16[3,12,24,128]{3,2,1,0:T(8,128)(2,1)S(1)}, u32[]{:S(2)}, u32[]{:S(2)}) collective-permute-start(bf16[3,12,24,128]{3,2,1,0:T(8,128)(2,1)S(1)} %copy-done.2), channel_id=1, source_target_pairs={{4,8},{12,16},{20,24},{8,4},{16,12},{24,20},{5,9},{13,17},{21,25},... | collective-permute-start | bytes 663560 | tf_op jit(solution)/shard_map/ppermute | solution.py:830
  31.7 12.0 %all-to-all-start.1 = ((bf16[8,5,16,128]{3,2,1,0:T(8,128)(2,1)}), bf16[8,5,16,128]{3,2,1,0:T(8,128)(2,1)S(1)}, u32[]{:S(2)}, u32[]{:S(2)}) async-start(bf16[8,5,16,128]{3,2,1,0:T(8,128)(2,1)} %shard_map.157.after), calls=%async_computation.1 | async-start | bytes 327680 | tf_op jit(solution)/shard_map/all_to_all | solution.py:849
  44.0 6.4 %collective-permute-start.5 = (bf16[160,128]{1,0:T(8,128)(2,1)S(1)}, bf16[160,128]{1,0:T(8,128)(2,1)S(1)}, u32[]{:S(2)}, u32[]{:S(2)}) collective-permute-start(bf16[160,128]{1,0:T(8,128)(2,1)S(1)} %get-tuple-element.64), channel_id=1, source_target_pairs={{0,1},{1,2},{2,3},{3,0},{4,5},{5,6},{6,7},{7,4},{8,9},{9,10},{10,1... | collective-permute-start | bytes 122888 | tf_op jit(solution)/shard_map/ppermute | solution.py:728
  45.7 4.7 %collective-permute-start.6 = (bf16[160,128]{1,0:T(8,128)(2,1)S(1)}, bf16[160,128]{1,0:T(8,128)(2,1)S(1)}, u32[]{:S(2)}, u32[]{:S(2)}) collective-permute-start(bf16[160,128]{1,0:T(8,128)(2,1)S(1)} %get-tuple-element.65), channel_id=1, source_target_pairs={{0,2},{1,3},{2,0},{3,1},{4,6},{5,7},{6,4},{7,5},{8,10},{9,11},{10,... | collective-permute-start | bytes 122888 | tf_op jit(solution)/shard_map/ppermute | solution.py:728
  46.7 4.0 %collective-permute-start.7 = (bf16[160,128]{1,0:T(8,128)(2,1)S(1)}, bf16[160,128]{1,0:T(8,128)(2,1)S(1)}, u32[]{:S(2)}, u32[]{:S(2)}) collective-permute-start(bf16[160,128]{1,0:T(8,128)(2,1)S(1)} %get-tuple-element.66), channel_id=1, source_target_pairs={{0,3},{1,0},{2,1},{3,2},{4,7},{5,4},{6,5},{7,6},{8,11},{9,8},{10,9... | collective-permute-start | bytes 122888 | tf_op jit(solution)/shard_map/ppermute | solution.py:728

commit v3 on v2

--- a/solution.py
+++ b/solution.py
@@ -151,31 +151,37 @@
 def first_body(
     plan, field_in, table_in, regroup_in, rows_in, pair_in, ytable_in, swap_in, *rest
 ):
-    weight = held = None
-    if len(rest) > plan.dy + 11:
-        weight, *rest, held, held_sems = rest
-        packed = rest.pop(plan.dy + 3)
     own, low_message, high_message, *rest = rest
     middle = rest[: plan.dy - 3]
     coarse, ytable, swap, field, table, regroup, rows_table, pair_table, chunks, sems = rest[
         plan.dy - 3 :
     ]
-    sources = (field_in, table_in, regroup_in, rows_in, pair_in, ytable_in, swap_in)
-    targets = (field, table, regroup, rows_table, pair_table, ytable, swap)
+    middle_channel = plan.channels // 2
+    lower = pl.ds(0, middle_channel)
+    upper = pl.ds(middle_channel, plan.channels - middle_channel)
+    sources = (
+        table_in, field_in.at[lower], field_in.at[upper],
+        regroup_in, rows_in, pair_in, ytable_in, swap_in,
+    )
+    targets = (
+        table, field.at[lower], field.at[upper], regroup, rows_table, pair_table, ytable, swap
+    )
     copies = [
         pltpu.make_async_copy(s, t, sems.at[n]) for n, (s, t) in enumerate(zip(sources, targets))
     ]
     for copy in copies:
         copy.start()
-    if held is not None:
-        start_weights(weight, held, held_sems, 0)
-    for copy in copies[:3]:
-        copy.wait()
-    rows = plan.channels * plan.cy
-    lhs = jnp.concatenate(
-        [field[:, x].reshape(rows, plan.cz) for x in range(plan.cx)], axis=1
-    )
-    modes = dot(lhs, table[...]).astype(BF16)
+    copies[0].wait()
+    pieces = []
+    for n, (low, high) in enumerate(((0, middle_channel), (middle_channel, plan.channels))):
+        copies[1 + n].wait()
+        rows = (high - low) * plan.cy
+        lhs = jnp.concatenate(
+            [field[low:high, x].reshape(rows, plan.cz) for x in range(plan.cx)], axis=1
+        )
+        pieces.append(dot(lhs, table[...]).astype(BF16))
+    modes = jnp.concatenate(pieces, axis=0)
+    copies[3].wait()
     part = plan.cg * plan.cy
     lanes = jnp.concatenate(
         [modes[g * part : (g + 1) * part] for g in range(plan.groups)], axis=1
@@ -183,7 +189,7 @@
     result = dot(lanes, regroup[...]).astype(BF16)
     for d in range(plan.dy):
         chunks[d] = result[:, d * LANES : (d + 1) * LANES]
-    for copy in copies[3:]:
+    for copy in copies[4:]:
         copy.wait()
     pool_body(plan, field, rows_table, pair_table, coarse)
     here = lax.axis_index("gy")
@@ -200,8 +206,6 @@
             low_message[at] = coarse[x, tiles - 2 + j]
             high_message[at] = coarse[x, j]
             index += 1
-    if held is not None:
-        pack_weights(plan, weight, held, held_sems, 0, packed)
 
 
 def y_transform(plan, line, table, swap):
@@ -313,6 +317,11 @@
         return carry
 
     lax.fori_loop(0, held.shape[0], one, 0)
+
+
+def early_body(plan, after, weight, packed, held, sems):
+    start_weights(weight, held, sems, 0)
+    pack_weights(plan, weight, held, sems, 0, packed)
 
 
 def window_body(
@@ -698,18 +707,19 @@
     columns = []
     for e in range(2):
         for h in range(2):
-            cols = third[0, h * (half // 2) : (h + 1) * (half // 2)]
+            cols = third[step, h * (half // 2) : (h + 1) * (half // 2)]
             columns.append(
                 jnp.concatenate(
                     [
-                        field[:, e, h * half : (h + 1) * half].reshape(cells, plan.cz),
+                        field[:, 2 * step + e, h * half : (h + 1) * half].reshape(cells, plan.cz),
                         cols.astype(F32).reshape(half // 2 * CP, plan.cz).astype(BF16),
                     ],
                     axis=0,
                 )
             )
     local = dot(lift[...], jnp.concatenate(columns, axis=1))
-    spectral = dot(lanes[...], inverse[...]).reshape(plan.channels, plan.cy, 2 * plan.cz)
+    at = pl.multiple_of(step * 2 * plan.cz, 2 * plan.cz)
+    spectral = dot(lanes[...], inverse[:, pl.ds(at, 2 * plan.cz)]).reshape(plan.channels, plan.cy, 2 * plan.cz)
     for e in range(2):
         for h in range(2):
             index = e * 2 + h
@@ -750,32 +760,39 @@
     outs = [chunk, message, message] + [chunk] * (devices_y - 3)
     outs += [shape((nx, ny, CP, cz), BF16)] + [shape(t.shape, BF16) for t in tables[4:]]
     if split:
-        early, late = channels // 10, 3 * channels // 10
+        early, late = channels // 6, channels // 4
         pack = lambda n: shape((n, 2, channels, plan.ky, LANES), BF16)
         hold = lambda n: [
             pltpu.VMEM((n, 2) + spectral_weight.shape[2:], F32), pltpu.SemaphoreType.DMA((n,))
         ]
-    packs = [pack(early)] if split else []
     first = call(
         functools.partial(first_body, plan),
-        outs + packs,
-        (features,) + tables + ((spectral_weight,) if split else ()),
-        out_specs=[VMEM] * len(outs) + [FAR] * len(packs),
+        outs,
+        (features,) + tables,
         scratch=[pltpu.VMEM(features.shape, BF16)]
         + [pltpu.VMEM(t.shape, BF16) for t in tables[:4]]
-        + [pltpu.VMEM((devices_y, part, LANES), BF16), pltpu.SemaphoreType.DMA((7,))]
-        + (hold(early) if split else []),
-        specs=[HBM] * (7 + len(packs)),
+        + [pltpu.VMEM((devices_y, part, LANES), BF16), pltpu.SemaphoreType.DMA((8,))],
+        specs=[HBM] * 7,
         vmem=16,
     )
-    packed_early = first[-1]
-    first = first[: len(outs)]
     own, to_up, to_down = first[:3]
     middle = first[3:-3]
     coarse, y_table, y_swap = first[-3:]
     low_message = ring(to_up, "gy", 1)
     high_message = ring(to_down, "gy", -1)
     middle = [ring(m, "gy", s + 2) for s, m in enumerate(middle)]
+
+    if split:
+        packed_early = call(
+            functools.partial(early_body, plan),
+            pack(early),
+            (own, spectral_weight),
+            specs=[ANY, HBM],
+            out_specs=[FAR],
+            scratch=hold(early),
+            moved=2e6,
+        )
+        own = after(own, packed_early)
 
     y_out = (devices_x, cg, plan.ky) if split else (1, cg, plan.my)
     planes = shape((3, ny + 4, CP, LANES), BF16)
@@ -887,21 +904,13 @@
     near = lambda array: pltpu.with_memory_space_constraint(array, pltpu.VMEM)
     field, lift, regroup, inverse_z = (near(t) for t in tables)
 
-    full = lambda array: pl.BlockSpec(array.shape, lambda s: (0,) * array.ndim)
     return call(
         functools.partial(final_body, plan),
         shape(features.shape, BF16),
         (field, third, lift, regroup, inverse_z, own, *arrived),
         pin=False,
         grid=(nx,),
-        specs=[
-            pl.BlockSpec((channels, 2, cy, cz), lambda s: (0, s, 0, 0)),
-            pl.BlockSpec((1, cy // 2, CP, cz), lambda s: (s, 0, 0, 0)),
-            full(lift),
-            full(regroup),
-            pl.BlockSpec((devices_y * plan.unit, 2 * cz), lambda s: (0, s)),
-        ]
-        + [full(own)] * devices_y,
+        specs=[VMEM] * (5 + devices_y),
         out_specs=[pl.BlockSpec((channels, 2, cy, cz), lambda s: (0, s, 0, 0))],
         scratch=[
             pltpu.VMEM((devices_y, part, LANES), BF16),

time: 54.3 us -> 53 us (0.976)
  waiting for transfers between devices: 4.51 us -> 3.34 us
  starting transfers between devices: 21 us -> 20 us
  Pallas kernels: 26.7 us -> 27.5 us
    ppermute x6, waiting for transfers between devices: 1.43 us -> 0.02 us  [ring(): lax.ppermute(value, axis, [(i, (i + shift) % count) for i in range(count)])]
    pallas_call x8 -> x9, Pallas kernels: 26.7 us -> 27.5 us  [call(): pl.pallas_call(body, out_shape=outs, in_specs=specs, out_specs=out_specs,...]
    ppermute x6, starting transfers between devices: 10.1 us -> 9.43 us  [ring(): lax.ppermute(value, axis, [(i, (i + shift) % count) for i in range(count)])]
  transfers between devices with their start and end apart: 10 -> 10, of which waited for: 5 -> 2; matrix products, arithmetic and copies ran while one was open for 3% -> 3% of each run, Pallas kernels for 32% -> 37%
where the time goes in v3:
time: 53 us; the launch traced here: 52.6 us
  Pallas kernels  27.5 us (52%)
  starting transfers between devices  20 us (38%)
  waiting for transfers between devices  3.34 us (6%)
  local copies, waits for them, and re-layouts  1.62 us (3%)
    pallas_call x9, Pallas kernels, call(): pl.pallas_call(body, out_shape=outs, in_specs=specs, out_specs=out_specs,...  27.5 us
    ppermute x6, starting transfers between devices, ring(): lax.ppermute(value, axis, [(i, (i + shift) % count) for i in range(count)])  9.43 us
    all_to_all x1, starting transfers between devices, on_device(): pencil = lax.all_to_all(y_spec, 'gx', 0, 0, tiled=True)  4.88 us
    all_to_all x1, starting transfers between devices, on_device(): line = lax.all_to_all(back, 'gx', 0, 0, tiled=True)  4.5 us
    all_to_all x1, waiting for transfers between devices, on_device(): pencil = lax.all_to_all(y_spec, 'gx', 0, 0, tiled=True)  2.05 us
    all_to_all x1, waiting for transfers between devices, on_device(): line = lax.all_to_all(back, 'gx', 0, 0, tiled=True)  1.27 us
  transfers between devices with their start and end apart: 10, of which 2 were waited for; matrix products, arithmetic and copies ran while one was open for 3% of the time, Pallas kernels for 37%

profile of v3, /device:TPU:0, one launch (start us, length us, event | category | flops | bytes accessed | tf_op | source)
XLA Modules:
  0.0 52.6 jit_solution(11128374295218051460)
XLA Ops:
  0.0 0.0 copy-start
  0.0 3.4 %shard_map.154 = (bf16[160,128]{1,0:T(8,128)(2,1)S(1)}, bf16[352,128]{1,0:T(8,128)(2,1)S(1)}, bf16[352,128]{1,0:T(8,128)(2,1)S(1)}, bf16[160,128]{1,0:T(8,128)(2...) custom-call(bf16[20,8,32,128]{3,2,1,0:T(8,128)(2,1)} %rest_0_.1, ...), custom_call_target="tpu_custom_call" | custom-call | flops 1000000000 | bytes 1000000 | tf_op jit(solution)/shard_map/pallas_call | solution.py:132
  3.4 3.0 %collective-permute-start = (bf16[352,128]{1,0:T(8,128)(2,1)S(1)}, bf16[352,128]{1,0:T(8,128)(2,1)S(1)}, u32[]{:S(2)}, u32[]{:S(2)}) collective-permute-start(bf16[352,128]{1,0:T(8,128)(2,1)S(1)} %get-tuple-element.38), channel_id=1, source_target_pairs={{0,1},{1,2},{2,3},{3,0},{4,5},{5,6},{6,7},{7,4},{8,9},{9,10},{10,1... | collective-permute-start | bytes 270344 | tf_op jit(solution)/shard_map/ppermute | solution.py:738
  6.4 1.0 %collective-permute-start.1 = (bf16[352,128]{1,0:T(8,128)(2,1)S(1)}, bf16[352,128]{1,0:T(8,128)(2,1)S(1)}, u32[]{:S(2)}, u32[]{:S(2)}) collective-permute-start(bf16[352,128]{1,0:T(8,128)(2,1)S(1)} %get-tuple-element.39), channel_id=1, source_target_pairs={{0,3},{1,0},{2,1},{3,2},{4,7},{5,4},{6,5},{7,6},{8,11},{9,8},{10,9... | collective-permute-start | bytes 270344 | tf_op jit(solution)/shard_map/ppermute | solution.py:738
  7.4 1.9 %collective-permute-start.2 = (bf16[160,128]{1,0:T(8,128)(2,1)S(1)}, bf16[160,128]{1,0:T(8,128)(2,1)S(1)}, u32[]{:S(2)}, u32[]{:S(2)}) collective-permute-start(bf16[160,128]{1,0:T(8,128)(2,1)S(1)} %get-tuple-element.40), channel_id=1, source_target_pairs={{0,2},{1,3},{2,0},{3,1},{4,6},{5,7},{6,4},{7,5},{8,10},{9,11},{10,... | collective-permute-start | bytes 122888 | tf_op jit(solution)/shard_map/ppermute | solution.py:738
  9.3 0.0 copy-done
  9.3 0.6 %copy.19 = bf16[3,27,20,20]{3,2,1,0:T(8,128)(2,1)S(1)} copy(bf16[3,27,20,20]{1,3,2,0:T(8,128)(2,1)S(1)} %copy-done) | data formatting | bytes 129600 | tf_op args[2]
  9.9 0.1 pad_bitcast_fusion
  10.1 2.4 %shard_map.155.packed_early = bf16[3,2,20,16,128]{4,3,2,1,0:T(8,128)(2,1)} custom-call(bf16[160,128]{1,0:T(8,128)(2,1)S(1)} %get-tuple-element.37.after.own, f32[2,20,20,2,16,64]{5,4,3,2,1,0:T(8,128)} %weight.5), custom_call_target="tpu_custom_call" | custom-call | flops 1000000000 | bytes 2000000 | tf_op jit(solution)/shard_map/pallas_call | solution.py:132
  12.5 0.0 copy-start.1
  12.5 0.2 copy.25
  12.7 0.6 %reshape.8.filters = bf16[3,72,216]{2,1,0:T(8,128)(2,1)S(1)} reshape(bf16[3,3,24,9,24]{4,3,2,1,0:T(8,128)(2,1)S(1)} %copy.25) | data formatting | bytes 186624 | tf_op jit(solution)/shard_map/reshape | solution.py:814
  13.3 0.0 copy-done.1
  13.3 0.1 copy.21
  13.4 0.0 collective-permute-done.2.rest_0_
  13.4 0.0 collective-permute-done.low_message
  13.4 0.0 collective-permute-done.1.high_message
  13.4 1.1 %shard_map.156 = (bf16[8,5,16,128]{3,2,1,0:T(8,128)(2,1)}, bf16[3,12,24,128]{3,2,1,0:T(8,128)(2,1)}, bf16[3,12,24,128]{3,2,1,0:T(8,128)(2,1)}, bf16[4,12,24,128]{3,2,1,0:T(8,128)(2,1)S(1)}) custom-call(bf16[160,128]{1,0:T(8,128)(2,1)S(1)} %get-tuple-element.37.after.own, bf16[352,128]{1,0:T(8,128)(2,1)S(1)} %collective-permute-done.low_message, ...), custom_call_target="tpu_custom_call" | custom-call | flops 1000000000 | bytes 1000000 | tf_op jit(solution)/shard_map/pallas_call | solution.py:132
  14.5 4.9 %all-to-all-start = ((bf16[8,5,16,128]{3,2,1,0:T(8,128)(2,1)}), bf16[8,5,16,128]{3,2,1,0:T(8,128)(2,1)S(1)}, u32[]{:S(2)}, u32[]{:S(2)}) async-start(bf16[8,5,16,128]{3,2,1,0:T(8,128)(2,1)} %get-tuple-element.44.after), calls=%async_computation | async-start | bytes 327680 | tf_op jit(solution)/shard_map/all_to_all | solution.py:808
  19.4 0.0 copy-start.3
  19.4 0.0 copy-start.2
  19.4 3.9 %shard_map.157 = (bf16[5,2,20,16,128]{4,3,2,1,0:T(8,128)(2,1)}, f32[4,72,1280]{2,1,0:T(8,128)}, bf16[320,512]{1,0:T(8,128)(2,1)}, bf16[1024,256]{1,0:T(8,128)(2,1)S(1)}, bf16[256,1024]{1,0:T(8,128)(2,1)S(1)}) custom-call(bf16[8,5,16,128]{3,2,1,0:T(8,128)(2,1)} %get-tuple-element.44.after, bf16[4,12,24,128]{3,2,1,0:T(8,128)(2,1)S(1)} %get-tuple-element.45.volume, ...), custom_call_target="tpu_custom_call" | custom-call | flops 4000000000 | bytes 8000000 | tf_op jit(solution)/shard_map/pallas_call | solution.py:132
  23.3 0.0 copy-done.3
  23.3 0.6 %collective-permute-start.3 = (bf16[3,12,24,128]{3,2,1,0:T(8,128)(2,1)S(1)}, bf16[3,12,24,128]{3,2,1,0:T(8,128)(2,1)S(1)}, u32[]{:S(2)}, u32[]{:S(2)}) collective-permute-start(bf16[3,12,24,128]{3,2,1,0:T(8,128)(2,1)S(1)} %copy-done.3), channel_id=1, source_target_pairs={{0,4},{4,0},{8,12},{12,8},{16,20},{20,16},{24,28},{28,24},{1,5},{5... | collective-permute-start | bytes 663560 | tf_op jit(solution)/shard_map/ppermute | solution.py:845
  23.9 0.0 copy-done.2
  23.9 0.7 %collective-permute-start.4 = (bf16[3,12,24,128]{3,2,1,0:T(8,128)(2,1)S(1)}, bf16[3,12,24,128]{3,2,1,0:T(8,128)(2,1)S(1)}, u32[]{:S(2)}, u32[]{:S(2)}) collective-permute-start(bf16[3,12,24,128]{3,2,1,0:T(8,128)(2,1)S(1)} %copy-done.2), channel_id=1, source_target_pairs={{4,8},{12,16},{20,24},{8,4},{16,12},{24,20},{5,9},{13,17},{21,25},... | collective-permute-start | bytes 663560 | tf_op jit(solution)/shard_map/ppermute | solution.py:847
  24.6 2.0 %all-to-all-done.pencil = bf16[8,5,16,128]{3,2,1,0:T(8,128)(2,1)S(1)} async-done(((bf16[8,5,16,128]{3,2,1,0:T(8,128)(2,1)}), bf16[8,5,16,128]{3,2,1,0:T(8,128)(2,1)S(1)}, u32[]{:S(2)}, u32[]{:S(2)}) %all-to-all-start) | async-done | bytes 163872 | tf_op jit(solution)/shard_map/all_to_all | solution.py:808
  26.6 5.0 %shard_map.158.after = bf16[8,5,16,128]{3,2,1,0:T(8,128)(2,1)} custom-call(bf16[8,5,16,128]{3,2,1,0:T(8,128)(2,1)S(1)} %all-to-all-done.pencil, bf16[1024,256]{1,0:T(8,128)(2,1)S(1)} %get-tuple-element.46.forward, bf16[3,2,20,16,128]{4,3,2,1,0:T(8,128)(2,1)} %shard_map.155.packed_early, bf16[5,2,20,16,128]{4,3,2,1,0:T(8,128)(2,1)} %get-tuple-element.47.packed_late, ...), custom_call_target="tpu_custom_call" | custom-call | flops 1000000000 | bytes 1000000 | tf_op jit(solution)/shard_map/pallas_call | solution.py:132
  31.7 4.5 %all-to-all-start.1 = ((bf16[8,5,16,128]{3,2,1,0:T(8,128)(2,1)}), bf16[8,5,16,128]{3,2,1,0:T(8,128)(2,1)S(1)}, u32[]{:S(2)}, u32[]{:S(2)}) async-start(bf16[8,5,16,128]{3,2,1,0:T(8,128)(2,1)} %shard_map.158.after), calls=%async_computation.1 | async-start | bytes 327680 | tf_op jit(solution)/shard_map/all_to_all | solution.py:866
  36.2 0.0 collective-permute-done.3.near
  36.2 0.0 collective-permute-done.4.far
  36.2 5.9 %shard_map.159 = (f32[6,12,24,128]{3,2,1,0:T(8,128)S(1)}, bf16[128,256]{1,0:T(8,128)(2,1)S(1)}, bf16[128,128]{1,0:T(8,128)(2,1)S(1)}) custom-call(bf16[8,5,16,128]{3,2,1,0:T(8,128)(2,1)} %shard_map.158.after, bf16[3,12,24,128]{3,2,1,0:T(8,128)(2,1)S(1)} %collective-permute-done.3.near, bf16[3,12,24,128]{3,2,1,0:T(8,128)(2,1)S(1)} %collective-permute-done.4.far, ...), custom_call_target="tpu_custom_call" | custom-call | flops 6000000000 | bytes 1000000 | tf_op jit(solution)/shard_map/pallas_call | solution.py:132
  42.1 1.3 %all-to-all-done.1.line = bf16[8,5,16,128]{3,2,1,0:T(8,128)(2,1)S(1)} async-done(((bf16[8,5,16,128]{3,2,1,0:T(8,128)(2,1)}), bf16[8,5,16,128]{3,2,1,0:T(8,128)(2,1)S(1)}, u32[]{:S(2)}, u32[]{:S(2)}) %all-to-all-start.1) | async-done | bytes 163872 | tf_op jit(solution)/shard_map/all_to_all | solution.py:866
  43.4 0.4 shard_map.160
  43.7 0.6 %collective-permute-start.5 = (bf16[160,128]{1,0:T(8,128)(2,1)S(1)}, bf16[160,128]{1,0:T(8,128)(2,1)S(1)}, u32[]{:S(2)}, u32[]{:S(2)}) collective-permute-start(bf16[160,128]{1,0:T(8,128)(2,1)S(1)} %get-tuple-element.64), channel_id=1, source_target_pairs={{0,1},{1,2},{2,3},{3,0},{4,5},{5,6},{6,7},{7,4},{8,9},{9,10},{10,1... | collective-permute-start | bytes 122888 | tf_op jit(solution)/shard_map/ppermute | solution.py:738
  44.4 0.7 %collective-permute-start.6 = (bf16[160,128]{1,0:T(8,128)(2,1)S(1)}, bf16[160,128]{1,0:T(8,128)(2,1)S(1)}, u32[]{:S(2)}, u32[]{:S(2)}) collective-permute-start(bf16[160,128]{1,0:T(8,128)(2,1)S(1)} %get-tuple-element.65), channel_id=1, source_target_pairs={{0,2},{1,3},{2,0},{3,1},{4,6},{5,7},{6,4},{7,5},{8,10},{9,11},{10,... | collective-permute-start | bytes 122888 | tf_op jit(solution)/shard_map/ppermute | solution.py:738
  45.1 2.1 %collective-permute-start.7 = (bf16[160,128]{1,0:T(8,128)(2,1)S(1)}, bf16[160,128]{1,0:T(8,128)(2,1)S(1)}, u32[]{:S(2)}, u32[]{:S(2)}) collective-permute-start(bf16[160,128]{1,0:T(8,128)(2,1)S(1)} %get-tuple-element.66), channel_id=1, source_target_pairs={{0,3},{1,0},{2,1},{3,2},{4,7},{5,4},{6,5},{7,6},{8,11},{9,8},{10,9... | collective-permute-start | bytes 122888 | tf_op jit(solution)/shard_map/ppermute | solution.py:738
  47.2 2.2 %shard_map.161 = (bf16[4,16,24,128]{3,2,1,0:T(8,128)(2,1)S(1)}, bf16[20,8,32,128]{3,2,1,0:T(8,128)(2,1)S(1)}, bf16[320,512]{1,0:T(8,128)(2,1)S(1)}, bf16[512,512]{1,0:T(8,128)(2,1)S(1)}, bf16[128,1024]{1,0:T(8,128)(2,1)S(1)}) custom-call(bf16[160,128]{1,0:T(8,128)(2,1)S(1)} %get-tuple-element.56.after.own, f32[6,12,24,128]{3,2,1,0:T(8,128)S(1)} %get-tuple-element.57.second, ...), custom_call_target="tpu_custom_call" | custom-call | flops 3000000000 | bytes 1000000 | tf_op jit(solution)/shard_map/pallas_call | solution.py:132
  49.4 0.0 collective-permute-done.5.rest_0_
  49.4 0.0 collective-permute-done.6.rest_1_
  49.4 0.0 collective-permute-done.7.rest_2_
  49.5 3.1 %shard_map.162 = bf16[20,8,32,128]{3,2,1,0:T(8,128)(2,1)} custom-call(bf16[20,8,32,128]{3,2,1,0:T(8,128)(2,1)S(1)} %get-tuple-element.59.field, bf16[4,16,24,128]{3,2,1,0:T(8,128)(2,1)S(1)} %get-tuple-element.60.third, bf16[320,512]{1,0:T(8,128)(2,1)S(1)} %get-tuple-element.61.lift, bf16[512,512]{1,0:T(8,128)(2,1)S(1)} %get-tuple-element.62.regroup, ...), custom_call_target="tpu_custom_call" | custom-call | flops 1000000000 | bytes 1000000 | tf_op jit(solution)/shard_map/pallas_call | solution.py:132
Async XLA Ops:
  0.0 9.3 %copy-start = (bf16[3,27,20,20]{1,3,2,0:T(8,128)(2,1)S(1)}, bf16[3,27,20,20]{1,3,2,0:T(8,128)(2,1)}, u32[]{:S(2)}) copy-start(bf16[3,27,20,20]{1,3,2,0:T(8,128)(2,1)} %param.18) | copy-start | bytes 194404
  3.4 10.0 %collective-permute-start = (bf16[352,128]{1,0:T(8,128)(2,1)S(1)}, bf16[352,128]{1,0:T(8,128)(2,1)S(1)}, u32[]{:S(2)}, u32[]{:S(2)}) collective-permute-start(bf16[352,128]{1,0:T(8,128)(2,1)S(1)} %get-tuple-element.38), channel_id=1, source_target_pairs={{0,1},{1,2},{2,3},{3,0},{4,5},{5,6},{6,7},{7,4},{8,9},{9,10},{10,1... | collective-permute-start | bytes 270344 | tf_op jit(solution)/shard_map/ppermute | solution.py:738
  6.4 7.0 %collective-permute-start.1 = (bf16[352,128]{1,0:T(8,128)(2,1)S(1)}, bf16[352,128]{1,0:T(8,128)(2,1)S(1)}, u32[]{:S(2)}, u32[]{:S(2)}) collective-permute-start(bf16[352,128]{1,0:T(8,128)(2,1)S(1)} %get-tuple-element.39), channel_id=1, source_target_pairs={{0,3},{1,0},{2,1},{3,2},{4,7},{5,4},{6,5},{7,6},{8,11},{9,8},{10,9... | collective-permute-start | bytes 270344 | tf_op jit(solution)/shard_map/ppermute | solution.py:738
  7.4 6.0 %collective-permute-start.2 = (bf16[160,128]{1,0:T(8,128)(2,1)S(1)}, bf16[160,128]{1,0:T(8,128)(2,1)S(1)}, u32[]{:S(2)}, u32[]{:S(2)}) collective-permute-start(bf16[160,128]{1,0:T(8,128)(2,1)S(1)} %get-tuple-element.40), channel_id=1, source_target_pairs={{0,2},{1,3},{2,0},{3,1},{4,6},{5,7},{6,4},{7,5},{8,10},{9,11},{10,... | collective-permute-start | bytes 122888 | tf_op jit(solution)/shard_map/ppermute | solution.py:738
  12.5 0.8 %copy-start.1 = (bf16[20,20]{1,0:T(8,128)(2,1)S(1)}, bf16[20,20]{1,0:T(8,128)(2,1)}, u32[]{:S(2)}) copy-start(bf16[20,20]{1,0:T(8,128)(2,1)} %param.19) | copy-start | bytes 2404
  14.5 12.1 %all-to-all-start = ((bf16[8,5,16,128]{3,2,1,0:T(8,128)(2,1)}), bf16[8,5,16,128]{3,2,1,0:T(8,128)(2,1)S(1)}, u32[]{:S(2)}, u32[]{:S(2)}) async-start(bf16[8,5,16,128]{3,2,1,0:T(8,128)(2,1)} %get-tuple-element.44.after), calls=%async_computation | async-start | bytes 327680 | tf_op jit(solution)/shard_map/all_to_all | solution.py:808
  19.4 3.9 %copy-start.3 = (bf16[3,12,24,128]{3,2,1,0:T(8,128)(2,1)S(1)}, bf16[3,12,24,128]{3,2,1,0:T(8,128)(2,1)}, u32[]{:S(2)}) copy-start(bf16[3,12,24,128]{3,2,1,0:T(8,128)(2,1)} %get-tuple-element.52) | copy-start | bytes 663556
  19.4 4.5 %copy-start.2 = (bf16[3,12,24,128]{3,2,1,0:T(8,128)(2,1)S(1)}, bf16[3,12,24,128]{3,2,1,0:T(8,128)(2,1)}, u32[]{:S(2)}) copy-start(bf16[3,12,24,128]{3,2,1,0:T(8,128)(2,1)} %get-tuple-element.53) | copy-start | bytes 663556
  23.3 12.8 %collective-permute-start.3 = (bf16[3,12,24,128]{3,2,1,0:T(8,128)(2,1)S(1)}, bf16[3,12,24,128]{3,2,1,0:T(8,128)(2,1)S(1)}, u32[]{:S(2)}, u32[]{:S(2)}) collective-permute-start(bf16[3,12,24,128]{3,2,1,0:T(8,128)(2,1)S(1)} %copy-done.3), channel_id=1, source_target_pairs={{0,4},{4,0},{8,12},{12,8},{16,20},{20,16},{24,28},{28,24},{1,5},{5... | collective-permute-start | bytes 663560 | tf_op jit(solution)/shard_map/ppermute | solution.py:845
  23.9 12.3 %collective-permute-start.4 = (bf16[3,12,24,128]{3,2,1,0:T(8,128)(2,1)S(1)}, bf16[3,12,24,128]{3,2,1,0:T(8,128)(2,1)S(1)}, u32[]{:S(2)}, u32[]{:S(2)}) collective-permute-start(bf16[3,12,24,128]{3,2,1,0:T(8,128)(2,1)S(1)} %copy-done.2), channel_id=1, source_target_pairs={{4,8},{12,16},{20,24},{8,4},{16,12},{24,20},{5,9},{13,17},{21,25},... | collective-permute-start | bytes 663560 | tf_op jit(solution)/shard_map/ppermute | solution.py:847
  31.7 11.7 %all-to-all-start.1 = ((bf16[8,5,16,128]{3,2,1,0:T(8,128)(2,1)}), bf16[8,5,16,128]{3,2,1,0:T(8,128)(2,1)S(1)}, u32[]{:S(2)}, u32[]{:S(2)}) async-start(bf16[8,5,16,128]{3,2,1,0:T(8,128)(2,1)} %shard_map.158.after), calls=%async_computation.1 | async-start | bytes 327680 | tf_op jit(solution)/shard_map/all_to_all | solution.py:866
  43.7 5.7 %collective-permute-start.5 = (bf16[160,128]{1,0:T(8,128)(2,1)S(1)}, bf16[160,128]{1,0:T(8,128)(2,1)S(1)}, u32[]{:S(2)}, u32[]{:S(2)}) collective-permute-start(bf16[160,128]{1,0:T(8,128)(2,1)S(1)} %get-tuple-element.64), channel_id=1, source_target_pairs={{0,1},{1,2},{2,3},{3,0},{4,5},{5,6},{6,7},{7,4},{8,9},{9,10},{10,1... | collective-permute-start | bytes 122888 | tf_op jit(solution)/shard_map/ppermute | solution.py:738
  44.4 5.1 %collective-permute-start.6 = (bf16[160,128]{1,0:T(8,128)(2,1)S(1)}, bf16[160,128]{1,0:T(8,128)(2,1)S(1)}, u32[]{:S(2)}, u32[]{:S(2)}) collective-permute-start(bf16[160,128]{1,0:T(8,128)(2,1)S(1)} %get-tuple-element.65), channel_id=1, source_target_pairs={{0,2},{1,3},{2,0},{3,1},{4,6},{5,7},{6,4},{7,5},{8,10},{9,11},{10,... | collective-permute-start | bytes 122888 | tf_op jit(solution)/shard_map/ppermute | solution.py:738
  45.1 4.3 %collective-permute-start.7 = (bf16[160,128]{1,0:T(8,128)(2,1)S(1)}, bf16[160,128]{1,0:T(8,128)(2,1)S(1)}, u32[]{:S(2)}, u32[]{:S(2)}) collective-permute-start(bf16[160,128]{1,0:T(8,128)(2,1)S(1)} %get-tuple-element.66), channel_id=1, source_target_pairs={{0,3},{1,0},{2,1},{3,2},{4,7},{5,4},{6,5},{7,6},{8,11},{9,8},{10,9... | collective-permute-start | bytes 122888 | tf_op jit(solution)/shard_map/ppermute | solution.py:738

commit v4 on v3

--- a/solution.py
+++ b/solution.py
@@ -705,22 +705,25 @@
 
     cells = plan.channels * half
     columns = []
-    for e in range(2):
+    planes = out.shape[1]
+    for e in range(planes):
         for h in range(2):
-            cols = third[step, h * (half // 2) : (h + 1) * (half // 2)]
+            cols = third[step * (planes // 2) + e // 2, h * (half // 2) : (h + 1) * (half // 2)]
             columns.append(
                 jnp.concatenate(
                     [
-                        field[:, 2 * step + e, h * half : (h + 1) * half].reshape(cells, plan.cz),
+                        field[:, planes * step + e, h * half : (h + 1) * half].reshape(cells, plan.cz),
                         cols.astype(F32).reshape(half // 2 * CP, plan.cz).astype(BF16),
                     ],
                     axis=0,
                 )
             )
     local = dot(lift[...], jnp.concatenate(columns, axis=1))
-    at = pl.multiple_of(step * 2 * plan.cz, 2 * plan.cz)
-    spectral = dot(lanes[...], inverse[:, pl.ds(at, 2 * plan.cz)]).reshape(plan.channels, plan.cy, 2 * plan.cz)
-    for e in range(2):
+    at = pl.multiple_of(step * planes * plan.cz, planes * plan.cz)
+    spectral = dot(lanes[...], inverse[:, pl.ds(at, planes * plan.cz)]).reshape(
+        plan.channels, plan.cy, planes * plan.cz
+    )
+    for e in range(planes):
         for h in range(2):
             index = e * 2 + h
             total = local[:, index * plan.cz : (index + 1) * plan.cz].reshape(
@@ -909,9 +912,9 @@
         shape(features.shape, BF16),
         (field, third, lift, regroup, inverse_z, own, *arrived),
         pin=False,
-        grid=(nx,),
+        grid=(nx // 2,),
         specs=[VMEM] * (5 + devices_y),
-        out_specs=[pl.BlockSpec((channels, 2, cy, cz), lambda s: (0, s, 0, 0))],
+        out_specs=[pl.BlockSpec((channels, 4, cy, cz), lambda s: (0, s, 0, 0))],
         scratch=[
             pltpu.VMEM((devices_y, part, LANES), BF16),
             pltpu.VMEM((channels * cy, devices_y * plan.unit), BF16),

time: 53 us -> 52.6 us (level)
  no operation moved by 1% of the time
where the time goes in v4:
time: 52.6 us; the launch traced here: 52.2 us
  Pallas kernels  27.1 us (52%)
  starting transfers between devices  20 us (38%)
  waiting for transfers between devices  3.34 us (6%)
  local copies, waits for them, and re-layouts  1.62 us (3%)
    pallas_call x9, Pallas kernels, call(): pl.pallas_call(body, out_shape=outs, in_specs=specs, out_specs=out_specs,...  27.1 us
    ppermute x6, starting transfers between devices, ring(): lax.ppermute(value, axis, [(i, (i + shift) % count) for i in range(count)])  9.43 us
    all_to_all x1, starting transfers between devices, on_device(): pencil = lax.all_to_all(y_spec, 'gx', 0, 0, tiled=True)  4.88 us
    all_to_all x1, starting transfers between devices, on_device(): line = lax.all_to_all(back, 'gx', 0, 0, tiled=True)  4.5 us
    all_to_all x1, waiting for transfers between devices, on_device(): pencil = lax.all_to_all(y_spec, 'gx', 0, 0, tiled=True)  2.05 us
    all_to_all x1, waiting for transfers between devices, on_device(): line = lax.all_to_all(back, 'gx', 0, 0, tiled=True)  1.27 us
  transfers between devices with their start and end apart: 10, of which 2 were waited for; matrix products, arithmetic and copies ran while one was open for 3% of the time, Pallas kernels for 37%

profile of v4, /device:TPU:0, one launch (start us, length us, event | category | flops | bytes accessed | tf_op | source)
XLA Modules:
  0.0 52.2 jit_solution(1960387801294671104)
XLA Ops:
  0.0 0.0 copy-start
  0.0 3.4 %shard_map.154 = (bf16[160,128]{1,0:T(8,128)(2,1)S(1)}, bf16[352,128]{1,0:T(8,128)(2,1)S(1)}, bf16[352,128]{1,0:T(8,128)(2,1)S(1)}, bf16[160,128]{1,0:T(8,128)(2...) custom-call(bf16[20,8,32,128]{3,2,1,0:T(8,128)(2,1)} %rest_0_.1, ...), custom_call_target="tpu_custom_call" | custom-call | flops 1000000000 | bytes 1000000 | tf_op jit(solution)/shard_map/pallas_call | solution.py:132
  3.4 3.0 %collective-permute-start = (bf16[352,128]{1,0:T(8,128)(2,1)S(1)}, bf16[352,128]{1,0:T(8,128)(2,1)S(1)}, u32[]{:S(2)}, u32[]{:S(2)}) collective-permute-start(bf16[352,128]{1,0:T(8,128)(2,1)S(1)} %get-tuple-element.38), channel_id=1, source_target_pairs={{0,1},{1,2},{2,3},{3,0},{4,5},{5,6},{6,7},{7,4},{8,9},{9,10},{10,1... | collective-permute-start | bytes 270344 | tf_op jit(solution)/shard_map/ppermute | solution.py:741
  6.4 1.0 %collective-permute-start.1 = (bf16[352,128]{1,0:T(8,128)(2,1)S(1)}, bf16[352,128]{1,0:T(8,128)(2,1)S(1)}, u32[]{:S(2)}, u32[]{:S(2)}) collective-permute-start(bf16[352,128]{1,0:T(8,128)(2,1)S(1)} %get-tuple-element.39), channel_id=1, source_target_pairs={{0,3},{1,0},{2,1},{3,2},{4,7},{5,4},{6,5},{7,6},{8,11},{9,8},{10,9... | collective-permute-start | bytes 270344 | tf_op jit(solution)/shard_map/ppermute | solution.py:741
  7.4 1.9 %collective-permute-start.2 = (bf16[160,128]{1,0:T(8,128)(2,1)S(1)}, bf16[160,128]{1,0:T(8,128)(2,1)S(1)}, u32[]{:S(2)}, u32[]{:S(2)}) collective-permute-start(bf16[160,128]{1,0:T(8,128)(2,1)S(1)} %get-tuple-element.40), channel_id=1, source_target_pairs={{0,2},{1,3},{2,0},{3,1},{4,6},{5,7},{6,4},{7,5},{8,10},{9,11},{10,... | collective-permute-start | bytes 122888 | tf_op jit(solution)/shard_map/ppermute | solution.py:741
  9.3 0.0 copy-done
  9.3 0.6 %copy.19 = bf16[3,27,20,20]{3,2,1,0:T(8,128)(2,1)S(1)} copy(bf16[3,27,20,20]{1,3,2,0:T(8,128)(2,1)S(1)} %copy-done) | data formatting | bytes 129600 | tf_op args[2]
  9.9 0.1 pad_bitcast_fusion
  10.1 2.4 %shard_map.155.packed_early = bf16[3,2,20,16,128]{4,3,2,1,0:T(8,128)(2,1)} custom-call(bf16[160,128]{1,0:T(8,128)(2,1)S(1)} %get-tuple-element.37.after.own, f32[2,20,20,2,16,64]{5,4,3,2,1,0:T(8,128)} %weight.5), custom_call_target="tpu_custom_call" | custom-call | flops 1000000000 | bytes 2000000 | tf_op jit(solution)/shard_map/pallas_call | solution.py:132
  12.5 0.0 copy-start.1
  12.5 0.2 copy.25
  12.7 0.6 %reshape.8.filters = bf16[3,72,216]{2,1,0:T(8,128)(2,1)S(1)} reshape(bf16[3,3,24,9,24]{4,3,2,1,0:T(8,128)(2,1)S(1)} %copy.25) | data formatting | bytes 186624 | tf_op jit(solution)/shard_map/reshape | solution.py:817
  13.3 0.0 copy-done.1
  13.3 0.1 copy.21
  13.4 0.0 collective-permute-done.2.rest_0_
  13.4 0.0 collective-permute-done.low_message
  13.4 0.0 collective-permute-done.1.high_message
  13.4 1.1 %shard_map.156 = (bf16[8,5,16,128]{3,2,1,0:T(8,128)(2,1)}, bf16[3,12,24,128]{3,2,1,0:T(8,128)(2,1)}, bf16[3,12,24,128]{3,2,1,0:T(8,128)(2,1)}, bf16[4,12,24,128]{3,2,1,0:T(8,128)(2,1)S(1)}) custom-call(bf16[160,128]{1,0:T(8,128)(2,1)S(1)} %get-tuple-element.37.after.own, bf16[352,128]{1,0:T(8,128)(2,1)S(1)} %collective-permute-done.low_message, ...), custom_call_target="tpu_custom_call" | custom-call | flops 1000000000 | bytes 1000000 | tf_op jit(solution)/shard_map/pallas_call | solution.py:132
  14.5 4.9 %all-to-all-start = ((bf16[8,5,16,128]{3,2,1,0:T(8,128)(2,1)}), bf16[8,5,16,128]{3,2,1,0:T(8,128)(2,1)S(1)}, u32[]{:S(2)}, u32[]{:S(2)}) async-start(bf16[8,5,16,128]{3,2,1,0:T(8,128)(2,1)} %get-tuple-element.44.after), calls=%async_computation | async-start | bytes 327680 | tf_op jit(solution)/shard_map/all_to_all | solution.py:811
  19.4 0.0 copy-start.3
  19.4 0.0 copy-start.2
  19.4 3.9 %shard_map.157 = (bf16[5,2,20,16,128]{4,3,2,1,0:T(8,128)(2,1)}, f32[4,72,1280]{2,1,0:T(8,128)}, bf16[320,512]{1,0:T(8,128)(2,1)}, bf16[1024,256]{1,0:T(8,128)(2,1)S(1)}, bf16[256,1024]{1,0:T(8,128)(2,1)S(1)}) custom-call(bf16[8,5,16,128]{3,2,1,0:T(8,128)(2,1)} %get-tuple-element.44.after, bf16[4,12,24,128]{3,2,1,0:T(8,128)(2,1)S(1)} %get-tuple-element.45.volume, ...), custom_call_target="tpu_custom_call" | custom-call | flops 4000000000 | bytes 8000000 | tf_op jit(solution)/shard_map/pallas_call | solution.py:132
  23.3 0.0 copy-done.3
  23.3 0.6 %collective-permute-start.3 = (bf16[3,12,24,128]{3,2,1,0:T(8,128)(2,1)S(1)}, bf16[3,12,24,128]{3,2,1,0:T(8,128)(2,1)S(1)}, u32[]{:S(2)}, u32[]{:S(2)}) collective-permute-start(bf16[3,12,24,128]{3,2,1,0:T(8,128)(2,1)S(1)} %copy-done.3), channel_id=1, source_target_pairs={{0,4},{4,0},{8,12},{12,8},{16,20},{20,16},{24,28},{28,24},{1,5},{5... | collective-permute-start | bytes 663560 | tf_op jit(solution)/shard_map/ppermute | solution.py:848
  23.9 0.0 copy-done.2
  23.9 0.7 %collective-permute-start.4 = (bf16[3,12,24,128]{3,2,1,0:T(8,128)(2,1)S(1)}, bf16[3,12,24,128]{3,2,1,0:T(8,128)(2,1)S(1)}, u32[]{:S(2)}, u32[]{:S(2)}) collective-permute-start(bf16[3,12,24,128]{3,2,1,0:T(8,128)(2,1)S(1)} %copy-done.2), channel_id=1, source_target_pairs={{4,8},{12,16},{20,24},{8,4},{16,12},{24,20},{5,9},{13,17},{21,25},... | collective-permute-start | bytes 663560 | tf_op jit(solution)/shard_map/ppermute | solution.py:850
  24.6 2.0 %all-to-all-done.pencil = bf16[8,5,16,128]{3,2,1,0:T(8,128)(2,1)S(1)} async-done(((bf16[8,5,16,128]{3,2,1,0:T(8,128)(2,1)}), bf16[8,5,16,128]{3,2,1,0:T(8,128)(2,1)S(1)}, u32[]{:S(2)}, u32[]{:S(2)}) %all-to-all-start) | async-done | bytes 163872 | tf_op jit(solution)/shard_map/all_to_all | solution.py:811
  26.6 5.0 %shard_map.158.after = bf16[8,5,16,128]{3,2,1,0:T(8,128)(2,1)} custom-call(bf16[8,5,16,128]{3,2,1,0:T(8,128)(2,1)S(1)} %all-to-all-done.pencil, bf16[1024,256]{1,0:T(8,128)(2,1)S(1)} %get-tuple-element.46.forward, bf16[3,2,20,16,128]{4,3,2,1,0:T(8,128)(2,1)} %shard_map.155.packed_early, bf16[5,2,20,16,128]{4,3,2,1,0:T(8,128)(2,1)} %get-tuple-element.47.packed_late, ...), custom_call_target="tpu_custom_call" | custom-call | flops 1000000000 | bytes 1000000 | tf_op jit(solution)/shard_map/pallas_call | solution.py:132
  31.7 4.5 %all-to-all-start.1 = ((bf16[8,5,16,128]{3,2,1,0:T(8,128)(2,1)}), bf16[8,5,16,128]{3,2,1,0:T(8,128)(2,1)S(1)}, u32[]{:S(2)}, u32[]{:S(2)}) async-start(bf16[8,5,16,128]{3,2,1,0:T(8,128)(2,1)} %shard_map.158.after), calls=%async_computation.1 | async-start | bytes 327680 | tf_op jit(solution)/shard_map/all_to_all | solution.py:869
  36.2 0.0 collective-permute-done.3.near
  36.2 0.0 collective-permute-done.4.far
  36.2 5.9 %shard_map.159 = (f32[6,12,24,128]{3,2,1,0:T(8,128)S(1)}, bf16[128,256]{1,0:T(8,128)(2,1)S(1)}, bf16[128,128]{1,0:T(8,128)(2,1)S(1)}) custom-call(bf16[8,5,16,128]{3,2,1,0:T(8,128)(2,1)} %shard_map.158.after, bf16[3,12,24,128]{3,2,1,0:T(8,128)(2,1)S(1)} %collective-permute-done.3.near, bf16[3,12,24,128]{3,2,1,0:T(8,128)(2,1)S(1)} %collective-permute-done.4.far, ...), custom_call_target="tpu_custom_call" | custom-call | flops 6000000000 | bytes 1000000 | tf_op jit(solution)/shard_map/pallas_call | solution.py:132
  42.1 1.3 %all-to-all-done.1.line = bf16[8,5,16,128]{3,2,1,0:T(8,128)(2,1)S(1)} async-done(((bf16[8,5,16,128]{3,2,1,0:T(8,128)(2,1)}), bf16[8,5,16,128]{3,2,1,0:T(8,128)(2,1)S(1)}, u32[]{:S(2)}, u32[]{:S(2)}) %all-to-all-start.1) | async-done | bytes 163872 | tf_op jit(solution)/shard_map/all_to_all | solution.py:869
  43.4 0.4 shard_map.160
  43.7 0.6 %collective-permute-start.5 = (bf16[160,128]{1,0:T(8,128)(2,1)S(1)}, bf16[160,128]{1,0:T(8,128)(2,1)S(1)}, u32[]{:S(2)}, u32[]{:S(2)}) collective-permute-start(bf16[160,128]{1,0:T(8,128)(2,1)S(1)} %get-tuple-element.64), channel_id=1, source_target_pairs={{0,1},{1,2},{2,3},{3,0},{4,5},{5,6},{6,7},{7,4},{8,9},{9,10},{10,1... | collective-permute-start | bytes 122888 | tf_op jit(solution)/shard_map/ppermute | solution.py:741
  44.4 0.7 %collective-permute-start.6 = (bf16[160,128]{1,0:T(8,128)(2,1)S(1)}, bf16[160,128]{1,0:T(8,128)(2,1)S(1)}, u32[]{:S(2)}, u32[]{:S(2)}) collective-permute-start(bf16[160,128]{1,0:T(8,128)(2,1)S(1)} %get-tuple-element.65), channel_id=1, source_target_pairs={{0,2},{1,3},{2,0},{3,1},{4,6},{5,7},{6,4},{7,5},{8,10},{9,11},{10,... | collective-permute-start | bytes 122888 | tf_op jit(solution)/shard_map/ppermute | solution.py:741
  45.1 2.1 %collective-permute-start.7 = (bf16[160,128]{1,0:T(8,128)(2,1)S(1)}, bf16[160,128]{1,0:T(8,128)(2,1)S(1)}, u32[]{:S(2)}, u32[]{:S(2)}) collective-permute-start(bf16[160,128]{1,0:T(8,128)(2,1)S(1)} %get-tuple-element.66), channel_id=1, source_target_pairs={{0,3},{1,0},{2,1},{3,2},{4,7},{5,4},{6,5},{7,6},{8,11},{9,8},{10,9... | collective-permute-start | bytes 122888 | tf_op jit(solution)/shard_map/ppermute | solution.py:741
  47.2 2.2 %shard_map.161 = (bf16[4,16,24,128]{3,2,1,0:T(8,128)(2,1)S(1)}, bf16[20,8,32,128]{3,2,1,0:T(8,128)(2,1)S(1)}, bf16[320,512]{1,0:T(8,128)(2,1)S(1)}, bf16[512,512]{1,0:T(8,128)(2,1)S(1)}, bf16[128,1024]{1,0:T(8,128)(2,1)S(1)}) custom-call(bf16[160,128]{1,0:T(8,128)(2,1)S(1)} %get-tuple-element.56.after.own, f32[6,12,24,128]{3,2,1,0:T(8,128)S(1)} %get-tuple-element.57.second, ...), custom_call_target="tpu_custom_call" | custom-call | flops 3000000000 | bytes 1000000 | tf_op jit(solution)/shard_map/pallas_call | solution.py:132
  49.4 0.0 collective-permute-done.5.rest_0_
  49.4 0.0 collective-permute-done.6.rest_1_
  49.4 0.0 collective-permute-done.7.rest_2_
  49.5 2.7 %shard_map.162 = bf16[20,8,32,128]{3,2,1,0:T(8,128)(2,1)} custom-call(bf16[20,8,32,128]{3,2,1,0:T(8,128)(2,1)S(1)} %get-tuple-element.59.field, bf16[4,16,24,128]{3,2,1,0:T(8,128)(2,1)S(1)} %get-tuple-element.60.third, bf16[320,512]{1,0:T(8,128)(2,1)S(1)} %get-tuple-element.61.lift, bf16[512,512]{1,0:T(8,128)(2,1)S(1)} %get-tuple-element.62.regroup, ...), custom_call_target="tpu_custom_call" | custom-call | flops 1000000000 | bytes 1000000 | tf_op jit(solution)/shard_map/pallas_call | solution.py:132
Async XLA Ops:
  0.0 9.3 %copy-start = (bf16[3,27,20,20]{1,3,2,0:T(8,128)(2,1)S(1)}, bf16[3,27,20,20]{1,3,2,0:T(8,128)(2,1)}, u32[]{:S(2)}) copy-start(bf16[3,27,20,20]{1,3,2,0:T(8,128)(2,1)} %param.18) | copy-start | bytes 194404
  3.4 10.0 %collective-permute-start = (bf16[352,128]{1,0:T(8,128)(2,1)S(1)}, bf16[352,128]{1,0:T(8,128)(2,1)S(1)}, u32[]{:S(2)}, u32[]{:S(2)}) collective-permute-start(bf16[352,128]{1,0:T(8,128)(2,1)S(1)} %get-tuple-element.38), channel_id=1, source_target_pairs={{0,1},{1,2},{2,3},{3,0},{4,5},{5,6},{6,7},{7,4},{8,9},{9,10},{10,1... | collective-permute-start | bytes 270344 | tf_op jit(solution)/shard_map/ppermute | solution.py:741
  6.4 7.0 %collective-permute-start.1 = (bf16[352,128]{1,0:T(8,128)(2,1)S(1)}, bf16[352,128]{1,0:T(8,128)(2,1)S(1)}, u32[]{:S(2)}, u32[]{:S(2)}) collective-permute-start(bf16[352,128]{1,0:T(8,128)(2,1)S(1)} %get-tuple-element.39), channel_id=1, source_target_pairs={{0,3},{1,0},{2,1},{3,2},{4,7},{5,4},{6,5},{7,6},{8,11},{9,8},{10,9... | collective-permute-start | bytes 270344 | tf_op jit(solution)/shard_map/ppermute | solution.py:741
  7.4 6.0 %collective-permute-start.2 = (bf16[160,128]{1,0:T(8,128)(2,1)S(1)}, bf16[160,128]{1,0:T(8,128)(2,1)S(1)}, u32[]{:S(2)}, u32[]{:S(2)}) collective-permute-start(bf16[160,128]{1,0:T(8,128)(2,1)S(1)} %get-tuple-element.40), channel_id=1, source_target_pairs={{0,2},{1,3},{2,0},{3,1},{4,6},{5,7},{6,4},{7,5},{8,10},{9,11},{10,... | collective-permute-start | bytes 122888 | tf_op jit(solution)/shard_map/ppermute | solution.py:741
  12.5 0.8 %copy-start.1 = (bf16[20,20]{1,0:T(8,128)(2,1)S(1)}, bf16[20,20]{1,0:T(8,128)(2,1)}, u32[]{:S(2)}) copy-start(bf16[20,20]{1,0:T(8,128)(2,1)} %param.19) | copy-start | bytes 2404
  14.5 12.1 %all-to-all-start = ((bf16[8,5,16,128]{3,2,1,0:T(8,128)(2,1)}), bf16[8,5,16,128]{3,2,1,0:T(8,128)(2,1)S(1)}, u32[]{:S(2)}, u32[]{:S(2)}) async-start(bf16[8,5,16,128]{3,2,1,0:T(8,128)(2,1)} %get-tuple-element.44.after), calls=%async_computation | async-start | bytes 327680 | tf_op jit(solution)/shard_map/all_to_all | solution.py:811
  19.4 3.9 %copy-start.3 = (bf16[3,12,24,128]{3,2,1,0:T(8,128)(2,1)S(1)}, bf16[3,12,24,128]{3,2,1,0:T(8,128)(2,1)}, u32[]{:S(2)}) copy-start(bf16[3,12,24,128]{3,2,1,0:T(8,128)(2,1)} %get-tuple-element.52) | copy-start | bytes 663556
  19.4 4.5 %copy-start.2 = (bf16[3,12,24,128]{3,2,1,0:T(8,128)(2,1)S(1)}, bf16[3,12,24,128]{3,2,1,0:T(8,128)(2,1)}, u32[]{:S(2)}) copy-start(bf16[3,12,24,128]{3,2,1,0:T(8,128)(2,1)} %get-tuple-element.53) | copy-start | bytes 663556
  23.3 12.8 %collective-permute-start.3 = (bf16[3,12,24,128]{3,2,1,0:T(8,128)(2,1)S(1)}, bf16[3,12,24,128]{3,2,1,0:T(8,128)(2,1)S(1)}, u32[]{:S(2)}, u32[]{:S(2)}) collective-permute-start(bf16[3,12,24,128]{3,2,1,0:T(8,128)(2,1)S(1)} %copy-done.3), channel_id=1, source_target_pairs={{0,4},{4,0},{8,12},{12,8},{16,20},{20,16},{24,28},{28,24},{1,5},{5... | collective-permute-start | bytes 663560 | tf_op jit(solution)/shard_map/ppermute | solution.py:848
  23.9 12.3 %collective-permute-start.4 = (bf16[3,12,24,128]{3,2,1,0:T(8,128)(2,1)S(1)}, bf16[3,12,24,128]{3,2,1,0:T(8,128)(2,1)S(1)}, u32[]{:S(2)}, u32[]{:S(2)}) collective-permute-start(bf16[3,12,24,128]{3,2,1,0:T(8,128)(2,1)S(1)} %copy-done.2), channel_id=1, source_target_pairs={{4,8},{12,16},{20,24},{8,4},{16,12},{24,20},{5,9},{13,17},{21,25},... | collective-permute-start | bytes 663560 | tf_op jit(solution)/shard_map/ppermute | solution.py:850
  31.7 11.7 %all-to-all-start.1 = ((bf16[8,5,16,128]{3,2,1,0:T(8,128)(2,1)}), bf16[8,5,16,128]{3,2,1,0:T(8,128)(2,1)S(1)}, u32[]{:S(2)}, u32[]{:S(2)}) async-start(bf16[8,5,16,128]{3,2,1,0:T(8,128)(2,1)} %shard_map.158.after), calls=%async_computation.1 | async-start | bytes 327680 | tf_op jit(solution)/shard_map/all_to_all | solution.py:869
  43.7 5.7 %collective-permute-start.5 = (bf16[160,128]{1,0:T(8,128)(2,1)S(1)}, bf16[160,128]{1,0:T(8,128)(2,1)S(1)}, u32[]{:S(2)}, u32[]{:S(2)}) collective-permute-start(bf16[160,128]{1,0:T(8,128)(2,1)S(1)} %get-tuple-element.64), channel_id=1, source_target_pairs={{0,1},{1,2},{2,3},{3,0},{4,5},{5,6},{6,7},{7,4},{8,9},{9,10},{10,1... | collective-permute-start | bytes 122888 | tf_op jit(solution)/shard_map/ppermute | solution.py:741
  44.4 5.1 %collective-permute-start.6 = (bf16[160,128]{1,0:T(8,128)(2,1)S(1)}, bf16[160,128]{1,0:T(8,128)(2,1)S(1)}, u32[]{:S(2)}, u32[]{:S(2)}) collective-permute-start(bf16[160,128]{1,0:T(8,128)(2,1)S(1)} %get-tuple-element.65), channel_id=1, source_target_pairs={{0,2},{1,3},{2,0},{3,1},{4,6},{5,7},{6,4},{7,5},{8,10},{9,11},{10,... | collective-permute-start | bytes 122888 | tf_op jit(solution)/shard_map/ppermute | solution.py:741
  45.1 4.3 %collective-permute-start.7 = (bf16[160,128]{1,0:T(8,128)(2,1)S(1)}, bf16[160,128]{1,0:T(8,128)(2,1)S(1)}, u32[]{:S(2)}, u32[]{:S(2)}) collective-permute-start(bf16[160,128]{1,0:T(8,128)(2,1)S(1)} %get-tuple-element.66), channel_id=1, source_target_pairs={{0,3},{1,0},{2,1},{3,2},{4,7},{5,4},{6,5},{7,6},{8,11},{9,8},{10,9... | collective-permute-start | bytes 122888 | tf_op jit(solution)/shard_map/ppermute | solution.py:741

commit v5 on v4

--- a/solution.py
+++ b/solution.py
@@ -11,6 +11,7 @@
 
 LANES = 128
 CP = 24
+TALL = 32
 BF16 = jnp.bfloat16
 F32 = jnp.float32
 MIB = 1024 * 1024
@@ -148,6 +149,11 @@
     return lax.rem(index + shift + count, count)
 
 
+def taller(tile):
+    none = jnp.zeros((TALL - CP, LANES), F32)
+    return jnp.concatenate([tile.astype(F32), none], axis=0).astype(BF16)
+
+
 def first_body(
     plan, field_in, table_in, regroup_in, rows_in, pair_in, ytable_in, swap_in, *rest
 ):
@@ -202,9 +208,9 @@
     index = 0
     for x in range(plan.cx // 2):
         for j in range(2):
-            at = slice(part + index * CP, part + (index + 1) * CP)
-            low_message[at] = coarse[x, tiles - 2 + j]
-            high_message[at] = coarse[x, j]
+            at = slice(part + index * TALL, part + (index + 1) * TALL)
+            low_message[at] = taller(coarse[x, tiles - 2 + j])
+            high_message[at] = taller(coarse[x, j])
             index += 1
 
 
@@ -243,10 +249,11 @@
     tiles = plan.cy // 4
     for x in range(nx):
         for j in range(2):
-            at = slice(part + (x * 2 + j) * CP, part + (x * 2 + j + 1) * CP)
-            none = jnp.zeros((CP, LANES), BF16)
-            volume[x, j] = jnp.where(here > 0, low_message[at], none)
-            volume[x, 2 + tiles + j] = jnp.where(here < plan.dy - 1, high_message[at], none)
+            at = slice(part + (x * 2 + j) * TALL, part + (x * 2 + j + 1) * TALL)
+            low = low_message[at].astype(F32)[:CP]
+            high = high_message[at].astype(F32)[:CP]
+            volume[x, j] = jnp.where(here > 0, low, 0.0).astype(BF16)
+            volume[x, 2 + tiles + j] = jnp.where(here < plan.dy - 1, high, 0.0).astype(BF16)
         for j in range(tiles):
             volume[x, 2 + j] = coarse[x, j]
     even = lax.rem(lax.axis_index("gx"), 2) == 0
@@ -759,7 +766,7 @@
         plan.forward_y(), plan.swap(1.0),
     )
     chunk = shape((part, LANES), BF16)
-    message = shape((part + nx * 2 * CP, LANES), BF16)
+    message = shape((part + nx * 2 * TALL, LANES), BF16)
     outs = [chunk, message, message] + [chunk] * (devices_y - 3)
     outs += [shape((nx, ny, CP, cz), BF16)] + [shape(t.shape, BF16) for t in tables[4:]]
     if split:

time: 52.6 us -> 52.7 us (level)
  transfers between devices with their start and end apart: 10 -> 10, of which waited for: 2 -> 3; matrix products, arithmetic and copies ran while one was open for 3% -> 3% of each run, Pallas kernels for 37% -> 37%
where the time goes in v5:
time: 52.7 us; the launch traced here: 52.3 us
  Pallas kernels  27 us (51%)
  starting transfers between devices  20 us (38%)
  waiting for transfers between devices  3.46 us (7%)
  local copies, waits for them, and re-layouts  1.62 us (3%)
    pallas_call x9, Pallas kernels, call(): pl.pallas_call(body, out_shape=outs, in_specs=specs, out_specs=out_specs,...  27 us
    ppermute x6, starting transfers between devices, ring(): lax.ppermute(value, axis, [(i, (i + shift) % count) for i in range(count)])  9.43 us
    all_to_all x1, starting transfers between devices, on_device(): pencil = lax.all_to_all(y_spec, 'gx', 0, 0, tiled=True)  4.88 us
    all_to_all x1, starting transfers between devices, on_device(): line = lax.all_to_all(back, 'gx', 0, 0, tiled=True)  4.5 us
    all_to_all x1, waiting for transfers between devices, on_device(): pencil = lax.all_to_all(y_spec, 'gx', 0, 0, tiled=True)  2.05 us
    all_to_all x1, waiting for transfers between devices, on_device(): line = lax.all_to_all(back, 'gx', 0, 0, tiled=True)  1.28 us
  transfers between devices with their start and end apart: 10, of which 3 were waited for; matrix products, arithmetic and copies ran while one was open for 3% of the time, Pallas kernels for 37%

profile of v5, /device:TPU:0, one launch (start us, length us, event | category | flops | bytes accessed | tf_op | source)
XLA Modules:
  0.0 52.3 jit_solution(10064913554176004662)
XLA Ops:
  0.0 0.0 copy-start
  0.0 3.4 %shard_map.154 = (bf16[160,128]{1,0:T(8,128)(2,1)S(1)}, bf16[416,128]{1,0:T(8,128)(2,1)S(1)}, bf16[416,128]{1,0:T(8,128)(2,1)S(1)}, bf16[160,128]{1,0:T(8,128)(2...) custom-call(bf16[20,8,32,128]{3,2,1,0:T(8,128)(2,1)} %rest_0_.1, ...), custom_call_target="tpu_custom_call" | custom-call | flops 1000000000 | bytes 1000000 | tf_op jit(solution)/shard_map/pallas_call | solution.py:133
  3.4 3.0 %collective-permute-start = (bf16[416,128]{1,0:T(8,128)(2,1)S(1)}, bf16[416,128]{1,0:T(8,128)(2,1)S(1)}, u32[]{:S(2)}, u32[]{:S(2)}) collective-permute-start(bf16[416,128]{1,0:T(8,128)(2,1)S(1)} %get-tuple-element.38), channel_id=1, source_target_pairs={{0,1},{1,2},{2,3},{3,0},{4,5},{5,6},{6,7},{7,4},{8,9},{9,10},{10,1... | collective-permute-start | bytes 319496 | tf_op jit(solution)/shard_map/ppermute | solution.py:748
  6.4 1.0 %collective-permute-start.1 = (bf16[416,128]{1,0:T(8,128)(2,1)S(1)}, bf16[416,128]{1,0:T(8,128)(2,1)S(1)}, u32[]{:S(2)}, u32[]{:S(2)}) collective-permute-start(bf16[416,128]{1,0:T(8,128)(2,1)S(1)} %get-tuple-element.39), channel_id=1, source_target_pairs={{0,3},{1,0},{2,1},{3,2},{4,7},{5,4},{6,5},{7,6},{8,11},{9,8},{10,9... | collective-permute-start | bytes 319496 | tf_op jit(solution)/shard_map/ppermute | solution.py:748
  7.4 1.9 %collective-permute-start.2 = (bf16[160,128]{1,0:T(8,128)(2,1)S(1)}, bf16[160,128]{1,0:T(8,128)(2,1)S(1)}, u32[]{:S(2)}, u32[]{:S(2)}) collective-permute-start(bf16[160,128]{1,0:T(8,128)(2,1)S(1)} %get-tuple-element.40), channel_id=1, source_target_pairs={{0,2},{1,3},{2,0},{3,1},{4,6},{5,7},{6,4},{7,5},{8,10},{9,11},{10,... | collective-permute-start | bytes 122888 | tf_op jit(solution)/shard_map/ppermute | solution.py:748
  9.3 0.0 copy-done
  9.3 0.6 %copy.19 = bf16[3,27,20,20]{3,2,1,0:T(8,128)(2,1)S(1)} copy(bf16[3,27,20,20]{1,3,2,0:T(8,128)(2,1)S(1)} %copy-done) | data formatting | bytes 129600 | tf_op args[2]
  9.9 0.1 pad_bitcast_fusion
  10.1 2.4 %shard_map.155.packed_early = bf16[3,2,20,16,128]{4,3,2,1,0:T(8,128)(2,1)} custom-call(bf16[160,128]{1,0:T(8,128)(2,1)S(1)} %get-tuple-element.37.after.own, f32[2,20,20,2,16,64]{5,4,3,2,1,0:T(8,128)} %weight.5), custom_call_target="tpu_custom_call" | custom-call | flops 1000000000 | bytes 2000000 | tf_op jit(solution)/shard_map/pallas_call | solution.py:133
  12.5 0.0 copy-start.1
  12.5 0.2 copy.25
  12.7 0.6 %reshape.8.filters = bf16[3,72,216]{2,1,0:T(8,128)(2,1)S(1)} reshape(bf16[3,3,24,9,24]{4,3,2,1,0:T(8,128)(2,1)S(1)} %copy.25) | data formatting | bytes 186624 | tf_op jit(solution)/shard_map/reshape | solution.py:824
  13.3 0.0 copy-done.1
  13.3 0.1 copy.21
  13.4 0.0 collective-permute-done.2.rest_0_
  13.4 0.0 collective-permute-done.low_message
  13.4 0.0 collective-permute-done.1.high_message
  13.4 1.1 %shard_map.156 = (bf16[8,5,16,128]{3,2,1,0:T(8,128)(2,1)}, bf16[3,12,24,128]{3,2,1,0:T(8,128)(2,1)}, bf16[3,12,24,128]{3,2,1,0:T(8,128)(2,1)}, bf16[4,12,24,128]{3,2,1,0:T(8,128)(2,1)S(1)}) custom-call(bf16[160,128]{1,0:T(8,128)(2,1)S(1)} %get-tuple-element.37.after.own, bf16[416,128]{1,0:T(8,128)(2,1)S(1)} %collective-permute-done.low_message, ...), custom_call_target="tpu_custom_call" | custom-call | flops 1000000000 | bytes 1000000 | tf_op jit(solution)/shard_map/pallas_call | solution.py:133
  14.5 4.9 %all-to-all-start = ((bf16[8,5,16,128]{3,2,1,0:T(8,128)(2,1)}), bf16[8,5,16,128]{3,2,1,0:T(8,128)(2,1)S(1)}, u32[]{:S(2)}, u32[]{:S(2)}) async-start(bf16[8,5,16,128]{3,2,1,0:T(8,128)(2,1)} %get-tuple-element.44.after), calls=%async_computation | async-start | bytes 327680 | tf_op jit(solution)/shard_map/all_to_all | solution.py:818
  19.4 0.0 copy-start.3
  19.4 0.0 copy-start.2
  19.4 3.9 %shard_map.157 = (bf16[5,2,20,16,128]{4,3,2,1,0:T(8,128)(2,1)}, f32[4,72,1280]{2,1,0:T(8,128)}, bf16[320,512]{1,0:T(8,128)(2,1)}, bf16[1024,256]{1,0:T(8,128)(2,1)S(1)}, bf16[256,1024]{1,0:T(8,128)(2,1)S(1)}) custom-call(bf16[8,5,16,128]{3,2,1,0:T(8,128)(2,1)} %get-tuple-element.44.after, bf16[4,12,24,128]{3,2,1,0:T(8,128)(2,1)S(1)} %get-tuple-element.45.volume, ...), custom_call_target="tpu_custom_call" | custom-call | flops 4000000000 | bytes 8000000 | tf_op jit(solution)/shard_map/pallas_call | solution.py:133
  23.3 0.0 copy-done.3
  23.3 0.6 %collective-permute-start.3 = (bf16[3,12,24,128]{3,2,1,0:T(8,128)(2,1)S(1)}, bf16[3,12,24,128]{3,2,1,0:T(8,128)(2,1)S(1)}, u32[]{:S(2)}, u32[]{:S(2)}) collective-permute-start(bf16[3,12,24,128]{3,2,1,0:T(8,128)(2,1)S(1)} %copy-done.3), channel_id=1, source_target_pairs={{0,4},{4,0},{8,12},{12,8},{16,20},{20,16},{24,28},{28,24},{1,5},{5... | collective-permute-start | bytes 663560 | tf_op jit(solution)/shard_map/ppermute | solution.py:855
  23.9 0.0 copy-done.2
  23.9 0.7 %collective-permute-start.4 = (bf16[3,12,24,128]{3,2,1,0:T(8,128)(2,1)S(1)}, bf16[3,12,24,128]{3,2,1,0:T(8,128)(2,1)S(1)}, u32[]{:S(2)}, u32[]{:S(2)}) collective-permute-start(bf16[3,12,24,128]{3,2,1,0:T(8,128)(2,1)S(1)} %copy-done.2), channel_id=1, source_target_pairs={{4,8},{12,16},{20,24},{8,4},{16,12},{24,20},{5,9},{13,17},{21,25},... | collective-permute-start | bytes 663560 | tf_op jit(solution)/shard_map/ppermute | solution.py:857
  24.6 2.0 %all-to-all-done.pencil = bf16[8,5,16,128]{3,2,1,0:T(8,128)(2,1)S(1)} async-done(((bf16[8,5,16,128]{3,2,1,0:T(8,128)(2,1)}), bf16[8,5,16,128]{3,2,1,0:T(8,128)(2,1)S(1)}, u32[]{:S(2)}, u32[]{:S(2)}) %all-to-all-start) | async-done | bytes 163872 | tf_op jit(solution)/shard_map/all_to_all | solution.py:818
  26.6 5.0 %shard_map.158.after = bf16[8,5,16,128]{3,2,1,0:T(8,128)(2,1)} custom-call(bf16[8,5,16,128]{3,2,1,0:T(8,128)(2,1)S(1)} %all-to-all-done.pencil, bf16[1024,256]{1,0:T(8,128)(2,1)S(1)} %get-tuple-element.46.forward, bf16[3,2,20,16,128]{4,3,2,1,0:T(8,128)(2,1)} %shard_map.155.packed_early, bf16[5,2,20,16,128]{4,3,2,1,0:T(8,128)(2,1)} %get-tuple-element.47.packed_late, ...), custom_call_target="tpu_custom_call" | custom-call | flops 1000000000 | bytes 1000000 | tf_op jit(solution)/shard_map/pallas_call | solution.py:133
  31.7 4.5 %all-to-all-start.1 = ((bf16[8,5,16,128]{3,2,1,0:T(8,128)(2,1)}), bf16[8,5,16,128]{3,2,1,0:T(8,128)(2,1)S(1)}, u32[]{:S(2)}, u32[]{:S(2)}) async-start(bf16[8,5,16,128]{3,2,1,0:T(8,128)(2,1)} %shard_map.158.after), calls=%async_computation.1 | async-start | bytes 327680 | tf_op jit(solution)/shard_map/all_to_all | solution.py:876
  36.2 0.0 collective-permute-done.3.near
  36.2 0.0 collective-permute-done.4.far
  36.2 5.9 %shard_map.159 = (f32[6,12,24,128]{3,2,1,0:T(8,128)S(1)}, bf16[128,256]{1,0:T(8,128)(2,1)S(1)}, bf16[128,128]{1,0:T(8,128)(2,1)S(1)}) custom-call(bf16[8,5,16,128]{3,2,1,0:T(8,128)(2,1)} %shard_map.158.after, bf16[3,12,24,128]{3,2,1,0:T(8,128)(2,1)S(1)} %collective-permute-done.3.near, bf16[3,12,24,128]{3,2,1,0:T(8,128)(2,1)S(1)} %collective-permute-done.4.far, ...), custom_call_target="tpu_custom_call" | custom-call | flops 6000000000 | bytes 1000000 | tf_op jit(solution)/shard_map/pallas_call | solution.py:133
  42.1 1.3 %all-to-all-done.1.line = bf16[8,5,16,128]{3,2,1,0:T(8,128)(2,1)S(1)} async-done(((bf16[8,5,16,128]{3,2,1,0:T(8,128)(2,1)}), bf16[8,5,16,128]{3,2,1,0:T(8,128)(2,1)S(1)}, u32[]{:S(2)}, u32[]{:S(2)}) %all-to-all-start.1) | async-done | bytes 163872 | tf_op jit(solution)/shard_map/all_to_all | solution.py:876
  43.4 0.4 shard_map.160
  43.8 1.0 %collective-permute-start.5 = (bf16[160,128]{1,0:T(8,128)(2,1)S(1)}, bf16[160,128]{1,0:T(8,128)(2,1)S(1)}, u32[]{:S(2)}, u32[]{:S(2)}) collective-permute-start(bf16[160,128]{1,0:T(8,128)(2,1)S(1)} %get-tuple-element.64), channel_id=1, source_target_pairs={{0,1},{1,2},{2,3},{3,0},{4,5},{5,6},{6,7},{7,4},{8,9},{9,10},{10,1... | collective-permute-start | bytes 122888 | tf_op jit(solution)/shard_map/ppermute | solution.py:748
  44.7 0.9 %collective-permute-start.6 = (bf16[160,128]{1,0:T(8,128)(2,1)S(1)}, bf16[160,128]{1,0:T(8,128)(2,1)S(1)}, u32[]{:S(2)}, u32[]{:S(2)}) collective-permute-start(bf16[160,128]{1,0:T(8,128)(2,1)S(1)} %get-tuple-element.65), channel_id=1, source_target_pairs={{0,2},{1,3},{2,0},{3,1},{4,6},{5,7},{6,4},{7,5},{8,10},{9,11},{10,... | collective-permute-start | bytes 122888 | tf_op jit(solution)/shard_map/ppermute | solution.py:748
  45.6 1.7 %collective-permute-start.7 = (bf16[160,128]{1,0:T(8,128)(2,1)S(1)}, bf16[160,128]{1,0:T(8,128)(2,1)S(1)}, u32[]{:S(2)}, u32[]{:S(2)}) collective-permute-start(bf16[160,128]{1,0:T(8,128)(2,1)S(1)} %get-tuple-element.66), channel_id=1, source_target_pairs={{0,3},{1,0},{2,1},{3,2},{4,7},{5,4},{6,5},{7,6},{8,11},{9,8},{10,9... | collective-permute-start | bytes 122888 | tf_op jit(solution)/shard_map/ppermute | solution.py:748
  47.2 2.2 %shard_map.161 = (bf16[4,16,24,128]{3,2,1,0:T(8,128)(2,1)S(1)}, bf16[20,8,32,128]{3,2,1,0:T(8,128)(2,1)S(1)}, bf16[320,512]{1,0:T(8,128)(2,1)S(1)}, bf16[512,512]{1,0:T(8,128)(2,1)S(1)}, bf16[128,1024]{1,0:T(8,128)(2,1)S(1)}) custom-call(bf16[160,128]{1,0:T(8,128)(2,1)S(1)} %get-tuple-element.56.after.own, f32[6,12,24,128]{3,2,1,0:T(8,128)S(1)} %get-tuple-element.57.second, ...), custom_call_target="tpu_custom_call" | custom-call | flops 3000000000 | bytes 1000000 | tf_op jit(solution)/shard_map/pallas_call | solution.py:133
  49.4 0.0 collective-permute-done.5.rest_0_
  49.4 0.0 collective-permute-done.6.rest_1_
  49.5 0.1 collective-permute-done.7.rest_2_
  49.6 2.7 %shard_map.162 = bf16[20,8,32,128]{3,2,1,0:T(8,128)(2,1)} custom-call(bf16[20,8,32,128]{3,2,1,0:T(8,128)(2,1)S(1)} %get-tuple-element.59.field, bf16[4,16,24,128]{3,2,1,0:T(8,128)(2,1)S(1)} %get-tuple-element.60.third, bf16[320,512]{1,0:T(8,128)(2,1)S(1)} %get-tuple-element.61.lift, bf16[512,512]{1,0:T(8,128)(2,1)S(1)} %get-tuple-element.62.regroup, ...), custom_call_target="tpu_custom_call" | custom-call | flops 1000000000 | bytes 1000000 | tf_op jit(solution)/shard_map/pallas_call | solution.py:133
Async XLA Ops:
  0.0 9.3 %copy-start = (bf16[3,27,20,20]{1,3,2,0:T(8,128)(2,1)S(1)}, bf16[3,27,20,20]{1,3,2,0:T(8,128)(2,1)}, u32[]{:S(2)}) copy-start(bf16[3,27,20,20]{1,3,2,0:T(8,128)(2,1)} %param.18) | copy-start | bytes 194404
  3.4 10.0 %collective-permute-start = (bf16[416,128]{1,0:T(8,128)(2,1)S(1)}, bf16[416,128]{1,0:T(8,128)(2,1)S(1)}, u32[]{:S(2)}, u32[]{:S(2)}) collective-permute-start(bf16[416,128]{1,0:T(8,128)(2,1)S(1)} %get-tuple-element.38), channel_id=1, source_target_pairs={{0,1},{1,2},{2,3},{3,0},{4,5},{5,6},{6,7},{7,4},{8,9},{9,10},{10,1... | collective-permute-start | bytes 319496 | tf_op jit(solution)/shard_map/ppermute | solution.py:748
  6.4 7.0 %collective-permute-start.1 = (bf16[416,128]{1,0:T(8,128)(2,1)S(1)}, bf16[416,128]{1,0:T(8,128)(2,1)S(1)}, u32[]{:S(2)}, u32[]{:S(2)}) collective-permute-start(bf16[416,128]{1,0:T(8,128)(2,1)S(1)} %get-tuple-element.39), channel_id=1, source_target_pairs={{0,3},{1,0},{2,1},{3,2},{4,7},{5,4},{6,5},{7,6},{8,11},{9,8},{10,9... | collective-permute-start | bytes 319496 | tf_op jit(solution)/shard_map/ppermute | solution.py:748
  7.4 6.0 %collective-permute-start.2 = (bf16[160,128]{1,0:T(8,128)(2,1)S(1)}, bf16[160,128]{1,0:T(8,128)(2,1)S(1)}, u32[]{:S(2)}, u32[]{:S(2)}) collective-permute-start(bf16[160,128]{1,0:T(8,128)(2,1)S(1)} %get-tuple-element.40), channel_id=1, source_target_pairs={{0,2},{1,3},{2,0},{3,1},{4,6},{5,7},{6,4},{7,5},{8,10},{9,11},{10,... | collective-permute-start | bytes 122888 | tf_op jit(solution)/shard_map/ppermute | solution.py:748
  12.5 0.8 %copy-start.1 = (bf16[20,20]{1,0:T(8,128)(2,1)S(1)}, bf16[20,20]{1,0:T(8,128)(2,1)}, u32[]{:S(2)}) copy-start(bf16[20,20]{1,0:T(8,128)(2,1)} %param.19) | copy-start | bytes 2404
  14.5 12.1 %all-to-all-start = ((bf16[8,5,16,128]{3,2,1,0:T(8,128)(2,1)}), bf16[8,5,16,128]{3,2,1,0:T(8,128)(2,1)S(1)}, u32[]{:S(2)}, u32[]{:S(2)}) async-start(bf16[8,5,16,128]{3,2,1,0:T(8,128)(2,1)} %get-tuple-element.44.after), calls=%async_computation | async-start | bytes 327680 | tf_op jit(solution)/shard_map/all_to_all | solution.py:818
  19.4 3.9 %copy-start.3 = (bf16[3,12,24,128]{3,2,1,0:T(8,128)(2,1)S(1)}, bf16[3,12,24,128]{3,2,1,0:T(8,128)(2,1)}, u32[]{:S(2)}) copy-start(bf16[3,12,24,128]{3,2,1,0:T(8,128)(2,1)} %get-tuple-element.52) | copy-start | bytes 663556
  19.4 4.5 %copy-start.2 = (bf16[3,12,24,128]{3,2,1,0:T(8,128)(2,1)S(1)}, bf16[3,12,24,128]{3,2,1,0:T(8,128)(2,1)}, u32[]{:S(2)}) copy-start(bf16[3,12,24,128]{3,2,1,0:T(8,128)(2,1)} %get-tuple-element.53) | copy-start | bytes 663556
  23.3 12.8 %collective-permute-start.3 = (bf16[3,12,24,128]{3,2,1,0:T(8,128)(2,1)S(1)}, bf16[3,12,24,128]{3,2,1,0:T(8,128)(2,1)S(1)}, u32[]{:S(2)}, u32[]{:S(2)}) collective-permute-start(bf16[3,12,24,128]{3,2,1,0:T(8,128)(2,1)S(1)} %copy-done.3), channel_id=1, source_target_pairs={{0,4},{4,0},{8,12},{12,8},{16,20},{20,16},{24,28},{28,24},{1,5},{5... | collective-permute-start | bytes 663560 | tf_op jit(solution)/shard_map/ppermute | solution.py:855
  23.9 12.3 %collective-permute-start.4 = (bf16[3,12,24,128]{3,2,1,0:T(8,128)(2,1)S(1)}, bf16[3,12,24,128]{3,2,1,0:T(8,128)(2,1)S(1)}, u32[]{:S(2)}, u32[]{:S(2)}) collective-permute-start(bf16[3,12,24,128]{3,2,1,0:T(8,128)(2,1)S(1)} %copy-done.2), channel_id=1, source_target_pairs={{4,8},{12,16},{20,24},{8,4},{16,12},{24,20},{5,9},{13,17},{21,25},... | collective-permute-start | bytes 663560 | tf_op jit(solution)/shard_map/ppermute | solution.py:857
  31.7 11.7 %all-to-all-start.1 = ((bf16[8,5,16,128]{3,2,1,0:T(8,128)(2,1)}), bf16[8,5,16,128]{3,2,1,0:T(8,128)(2,1)S(1)}, u32[]{:S(2)}, u32[]{:S(2)}) async-start(bf16[8,5,16,128]{3,2,1,0:T(8,128)(2,1)} %shard_map.158.after), calls=%async_computation.1 | async-start | bytes 327680 | tf_op jit(solution)/shard_map/all_to_all | solution.py:876
  43.8 5.7 %collective-permute-start.5 = (bf16[160,128]{1,0:T(8,128)(2,1)S(1)}, bf16[160,128]{1,0:T(8,128)(2,1)S(1)}, u32[]{:S(2)}, u32[]{:S(2)}) collective-permute-start(bf16[160,128]{1,0:T(8,128)(2,1)S(1)} %get-tuple-element.64), channel_id=1, source_target_pairs={{0,1},{1,2},{2,3},{3,0},{4,5},{5,6},{6,7},{7,4},{8,9},{9,10},{10,1... | collective-permute-start | bytes 122888 | tf_op jit(solution)/shard_map/ppermute | solution.py:748
  44.7 4.7 %collective-permute-start.6 = (bf16[160,128]{1,0:T(8,128)(2,1)S(1)}, bf16[160,128]{1,0:T(8,128)(2,1)S(1)}, u32[]{:S(2)}, u32[]{:S(2)}) collective-permute-start(bf16[160,128]{1,0:T(8,128)(2,1)S(1)} %get-tuple-element.65), channel_id=1, source_target_pairs={{0,2},{1,3},{2,0},{3,1},{4,6},{5,7},{6,4},{7,5},{8,10},{9,11},{10,... | collective-permute-start | bytes 122888 | tf_op jit(solution)/shard_map/ppermute | solution.py:748
  45.6 4.0 %collective-permute-start.7 = (bf16[160,128]{1,0:T(8,128)(2,1)S(1)}, bf16[160,128]{1,0:T(8,128)(2,1)S(1)}, u32[]{:S(2)}, u32[]{:S(2)}) collective-permute-start(bf16[160,128]{1,0:T(8,128)(2,1)S(1)} %get-tuple-element.66), channel_id=1, source_target_pairs={{0,3},{1,0},{2,1},{3,2},{4,7},{5,4},{6,5},{7,6},{8,11},{9,8},{10,9... | collective-permute-start | bytes 122888 | tf_op jit(solution)/shard_map/ppermute | solution.py:748

commit v6 on v5

--- a/solution.py
+++ b/solution.py
@@ -770,7 +770,7 @@
     outs = [chunk, message, message] + [chunk] * (devices_y - 3)
     outs += [shape((nx, ny, CP, cz), BF16)] + [shape(t.shape, BF16) for t in tables[4:]]
     if split:
-        early, late = channels // 6, channels // 4
+        early, late = channels // 10, 3 * channels // 10
         pack = lambda n: shape((n, 2, channels, plan.ky, LANES), BF16)
         hold = lambda n: [
             pltpu.VMEM((n, 2) + spectral_weight.shape[2:], F32), pltpu.SemaphoreType.DMA((n,))

time: 52.7 us -> 53 us (level)
  no operation moved by 1% of the time
where the time goes in v6:
time: 53 us; the launch traced here: 52.5 us
  Pallas kernels  27 us (51%)
  starting transfers between devices  20.3 us (38%)
  waiting for transfers between devices  3.49 us (7%)
  local copies, waits for them, and re-layouts  1.62 us (3%)
    pallas_call x9, Pallas kernels, call(): pl.pallas_call(body, out_shape=outs, in_specs=specs, out_specs=out_specs,...  27 us
    ppermute x6, starting transfers between devices, ring(): lax.ppermute(value, axis, [(i, (i + shift) % count) for i in range(count)])  9.43 us
    all_to_all x1, starting transfers between devices, on_device(): pencil = lax.all_to_all(y_spec, 'gx', 0, 0, tiled=True)  4.88 us
    all_to_all x1, starting transfers between devices, on_device(): line = lax.all_to_all(back, 'gx', 0, 0, tiled=True)  4.74 us
    all_to_all x1, waiting for transfers between devices, on_device(): pencil = lax.all_to_all(y_spec, 'gx', 0, 0, tiled=True)  1.8 us
    all_to_all x1, waiting for transfers between devices, on_device(): line = lax.all_to_all(back, 'gx', 0, 0, tiled=True)  1.27 us
  transfers between devices with their start and end apart: 10, of which 3 were waited for; matrix products, arithmetic and copies ran while one was open for 3% of the time, Pallas kernels for 37%

profile of v6, /device:TPU:0, one launch (start us, length us, event | category | flops | bytes accessed | tf_op | source)
XLA Modules:
  0.0 52.5 jit_solution(13627411601649577730)
XLA Ops:
  0.0 0.0 copy-start
  0.0 3.4 %shard_map.154 = (bf16[160,128]{1,0:T(8,128)(2,1)S(1)}, bf16[416,128]{1,0:T(8,128)(2,1)S(1)}, bf16[416,128]{1,0:T(8,128)(2,1)S(1)}, bf16[160,128]{1,0:T(8,128)(2...) custom-call(bf16[20,8,32,128]{3,2,1,0:T(8,128)(2,1)} %rest_0_.1, ...), custom_call_target="tpu_custom_call" | custom-call | flops 1000000000 | bytes 1000000 | tf_op jit(solution)/shard_map/pallas_call | solution.py:133
  3.4 3.0 %collective-permute-start = (bf16[416,128]{1,0:T(8,128)(2,1)S(1)}, bf16[416,128]{1,0:T(8,128)(2,1)S(1)}, u32[]{:S(2)}, u32[]{:S(2)}) collective-permute-start(bf16[416,128]{1,0:T(8,128)(2,1)S(1)} %get-tuple-element.38), channel_id=1, source_target_pairs={{0,1},{1,2},{2,3},{3,0},{4,5},{5,6},{6,7},{7,4},{8,9},{9,10},{10,1... | collective-permute-start | bytes 319496 | tf_op jit(solution)/shard_map/ppermute | solution.py:748
  6.4 1.0 %collective-permute-start.1 = (bf16[416,128]{1,0:T(8,128)(2,1)S(1)}, bf16[416,128]{1,0:T(8,128)(2,1)S(1)}, u32[]{:S(2)}, u32[]{:S(2)}) collective-permute-start(bf16[416,128]{1,0:T(8,128)(2,1)S(1)} %get-tuple-element.39), channel_id=1, source_target_pairs={{0,3},{1,0},{2,1},{3,2},{4,7},{5,4},{6,5},{7,6},{8,11},{9,8},{10,9... | collective-permute-start | bytes 319496 | tf_op jit(solution)/shard_map/ppermute | solution.py:748
  7.4 1.9 %collective-permute-start.2 = (bf16[160,128]{1,0:T(8,128)(2,1)S(1)}, bf16[160,128]{1,0:T(8,128)(2,1)S(1)}, u32[]{:S(2)}, u32[]{:S(2)}) collective-permute-start(bf16[160,128]{1,0:T(8,128)(2,1)S(1)} %get-tuple-element.40), channel_id=1, source_target_pairs={{0,2},{1,3},{2,0},{3,1},{4,6},{5,7},{6,4},{7,5},{8,10},{9,11},{10,... | collective-permute-start | bytes 122888 | tf_op jit(solution)/shard_map/ppermute | solution.py:748
  9.3 0.0 copy-done
  9.3 0.6 %copy.19 = bf16[3,27,20,20]{3,2,1,0:T(8,128)(2,1)S(1)} copy(bf16[3,27,20,20]{1,3,2,0:T(8,128)(2,1)S(1)} %copy-done) | data formatting | bytes 129600 | tf_op args[2]
  9.9 0.1 pad_bitcast_fusion
  10.1 2.1 %shard_map.155.packed_early = bf16[2,2,20,16,128]{4,3,2,1,0:T(8,128)(2,1)} custom-call(bf16[160,128]{1,0:T(8,128)(2,1)S(1)} %get-tuple-element.37.after.own, f32[2,20,20,2,16,64]{5,4,3,2,1,0:T(8,128)} %weight.5), custom_call_target="tpu_custom_call" | custom-call | flops 1000000000 | bytes 2000000 | tf_op jit(solution)/shard_map/pallas_call | solution.py:133
  12.2 0.0 copy-start.1
  12.2 0.2 copy.25
  12.4 0.6 %reshape.8.filters = bf16[3,72,216]{2,1,0:T(8,128)(2,1)S(1)} reshape(bf16[3,3,24,9,24]{4,3,2,1,0:T(8,128)(2,1)S(1)} %copy.25) | data formatting | bytes 186624 | tf_op jit(solution)/shard_map/reshape | solution.py:824
  13.0 0.0 copy-done.1
  13.0 0.1 copy.21
  13.1 0.0 collective-permute-done.2.rest_0_
  13.1 0.0 collective-permute-done.low_message
  13.1 0.0 collective-permute-done.1.high_message
  13.2 1.1 %shard_map.156 = (bf16[8,5,16,128]{3,2,1,0:T(8,128)(2,1)}, bf16[3,12,24,128]{3,2,1,0:T(8,128)(2,1)}, bf16[3,12,24,128]{3,2,1,0:T(8,128)(2,1)}, bf16[4,12,24,128]{3,2,1,0:T(8,128)(2,1)S(1)}) custom-call(bf16[160,128]{1,0:T(8,128)(2,1)S(1)} %get-tuple-element.37.after.own, bf16[416,128]{1,0:T(8,128)(2,1)S(1)} %collective-permute-done.low_message, ...), custom_call_target="tpu_custom_call" | custom-call | flops 1000000000 | bytes 1000000 | tf_op jit(solution)/shard_map/pallas_call | solution.py:133
  14.3 4.9 %all-to-all-start = ((bf16[8,5,16,128]{3,2,1,0:T(8,128)(2,1)}), bf16[8,5,16,128]{3,2,1,0:T(8,128)(2,1)S(1)}, u32[]{:S(2)}, u32[]{:S(2)}) async-start(bf16[8,5,16,128]{3,2,1,0:T(8,128)(2,1)} %get-tuple-element.44.after), calls=%async_computation | async-start | bytes 327680 | tf_op jit(solution)/shard_map/all_to_all | solution.py:818
  19.1 0.0 copy-start.3
  19.1 0.0 copy-start.2
  19.2 4.2 %shard_map.157 = (bf16[6,2,20,16,128]{4,3,2,1,0:T(8,128)(2,1)}, f32[4,72,1280]{2,1,0:T(8,128)}, bf16[320,512]{1,0:T(8,128)(2,1)}, bf16[1024,256]{1,0:T(8,128)(2,1)S(1)}, bf16[256,1024]{1,0:T(8,128)(2,1)S(1)}) custom-call(bf16[8,5,16,128]{3,2,1,0:T(8,128)(2,1)} %get-tuple-element.44.after, bf16[4,12,24,128]{3,2,1,0:T(8,128)(2,1)S(1)} %get-tuple-element.45.volume, ...), custom_call_target="tpu_custom_call" | custom-call | flops 4000000000 | bytes 8000000 | tf_op jit(solution)/shard_map/pallas_call | solution.py:133
  23.3 0.0 copy-done.3
  23.3 0.6 %collective-permute-start.3 = (bf16[3,12,24,128]{3,2,1,0:T(8,128)(2,1)S(1)}, bf16[3,12,24,128]{3,2,1,0:T(8,128)(2,1)S(1)}, u32[]{:S(2)}, u32[]{:S(2)}) collective-permute-start(bf16[3,12,24,128]{3,2,1,0:T(8,128)(2,1)S(1)} %copy-done.3), channel_id=1, source_target_pairs={{0,4},{4,0},{8,12},{12,8},{16,20},{20,16},{24,28},{28,24},{1,5},{5... | collective-permute-start | bytes 663560 | tf_op jit(solution)/shard_map/ppermute | solution.py:855
  23.9 0.0 copy-done.2
  23.9 0.7 %collective-permute-start.4 = (bf16[3,12,24,128]{3,2,1,0:T(8,128)(2,1)S(1)}, bf16[3,12,24,128]{3,2,1,0:T(8,128)(2,1)S(1)}, u32[]{:S(2)}, u32[]{:S(2)}) collective-permute-start(bf16[3,12,24,128]{3,2,1,0:T(8,128)(2,1)S(1)} %copy-done.2), channel_id=1, source_target_pairs={{4,8},{12,16},{20,24},{8,4},{16,12},{24,20},{5,9},{13,17},{21,25},... | collective-permute-start | bytes 663560 | tf_op jit(solution)/shard_map/ppermute | solution.py:857
  24.6 1.8 %all-to-all-done.pencil = bf16[8,5,16,128]{3,2,1,0:T(8,128)(2,1)S(1)} async-done(((bf16[8,5,16,128]{3,2,1,0:T(8,128)(2,1)}), bf16[8,5,16,128]{3,2,1,0:T(8,128)(2,1)S(1)}, u32[]{:S(2)}, u32[]{:S(2)}) %all-to-all-start) | async-done | bytes 163872 | tf_op jit(solution)/shard_map/all_to_all | solution.py:818
  26.4 5.0 %shard_map.158.after = bf16[8,5,16,128]{3,2,1,0:T(8,128)(2,1)} custom-call(bf16[8,5,16,128]{3,2,1,0:T(8,128)(2,1)S(1)} %all-to-all-done.pencil, bf16[1024,256]{1,0:T(8,128)(2,1)S(1)} %get-tuple-element.46.forward, bf16[2,2,20,16,128]{4,3,2,1,0:T(8,128)(2,1)} %shard_map.155.packed_early, bf16[6,2,20,16,128]{4,3,2,1,0:T(8,128)(2,1)} %get-tuple-element.47.packed_late, ...), custom_call_target="tpu_custom_call" | custom-call | flops 1000000000 | bytes 1000000 | tf_op jit(solution)/shard_map/pallas_call | solution.py:133
  31.4 4.7 %all-to-all-start.1 = ((bf16[8,5,16,128]{3,2,1,0:T(8,128)(2,1)}), bf16[8,5,16,128]{3,2,1,0:T(8,128)(2,1)S(1)}, u32[]{:S(2)}, u32[]{:S(2)}) async-start(bf16[8,5,16,128]{3,2,1,0:T(8,128)(2,1)} %shard_map.158.after), calls=%async_computation.1 | async-start | bytes 327680 | tf_op jit(solution)/shard_map/all_to_all | solution.py:876
  36.2 0.0 collective-permute-done.3.near
  36.2 0.0 collective-permute-done.4.far
  36.2 5.9 %shard_map.159 = (f32[6,12,24,128]{3,2,1,0:T(8,128)S(1)}, bf16[128,256]{1,0:T(8,128)(2,1)S(1)}, bf16[128,128]{1,0:T(8,128)(2,1)S(1)}) custom-call(bf16[8,5,16,128]{3,2,1,0:T(8,128)(2,1)} %shard_map.158.after, bf16[3,12,24,128]{3,2,1,0:T(8,128)(2,1)S(1)} %collective-permute-done.3.near, bf16[3,12,24,128]{3,2,1,0:T(8,128)(2,1)S(1)} %collective-permute-done.4.far, ...), custom_call_target="tpu_custom_call" | custom-call | flops 6000000000 | bytes 1000000 | tf_op jit(solution)/shard_map/pallas_call | solution.py:133
  42.1 1.3 %all-to-all-done.1.line = bf16[8,5,16,128]{3,2,1,0:T(8,128)(2,1)S(1)} async-done(((bf16[8,5,16,128]{3,2,1,0:T(8,128)(2,1)}), bf16[8,5,16,128]{3,2,1,0:T(8,128)(2,1)S(1)}, u32[]{:S(2)}, u32[]{:S(2)}) %all-to-all-start.1) | async-done | bytes 163872 | tf_op jit(solution)/shard_map/all_to_all | solution.py:876
  43.4 0.4 shard_map.160
  43.7 1.2 %collective-permute-start.5 = (bf16[160,128]{1,0:T(8,128)(2,1)S(1)}, bf16[160,128]{1,0:T(8,128)(2,1)S(1)}, u32[]{:S(2)}, u32[]{:S(2)}) collective-permute-start(bf16[160,128]{1,0:T(8,128)(2,1)S(1)} %get-tuple-element.64), channel_id=1, source_target_pairs={{0,1},{1,2},{2,3},{3,0},{4,5},{5,6},{6,7},{7,4},{8,9},{9,10},{10,1... | collective-permute-start | bytes 122888 | tf_op jit(solution)/shard_map/ppermute | solution.py:748
  45.0 0.9 %collective-permute-start.6 = (bf16[160,128]{1,0:T(8,128)(2,1)S(1)}, bf16[160,128]{1,0:T(8,128)(2,1)S(1)}, u32[]{:S(2)}, u32[]{:S(2)}) collective-permute-start(bf16[160,128]{1,0:T(8,128)(2,1)S(1)} %get-tuple-element.65), channel_id=1, source_target_pairs={{0,2},{1,3},{2,0},{3,1},{4,6},{5,7},{6,4},{7,5},{8,10},{9,11},{10,... | collective-permute-start | bytes 122888 | tf_op jit(solution)/shard_map/ppermute | solution.py:748
  45.8 1.4 %collective-permute-start.7 = (bf16[160,128]{1,0:T(8,128)(2,1)S(1)}, bf16[160,128]{1,0:T(8,128)(2,1)S(1)}, u32[]{:S(2)}, u32[]{:S(2)}) collective-permute-start(bf16[160,128]{1,0:T(8,128)(2,1)S(1)} %get-tuple-element.66), channel_id=1, source_target_pairs={{0,3},{1,0},{2,1},{3,2},{4,7},{5,4},{6,5},{7,6},{8,11},{9,8},{10,9... | collective-permute-start | bytes 122888 | tf_op jit(solution)/shard_map/ppermute | solution.py:748
  47.2 2.2 %shard_map.161 = (bf16[4,16,24,128]{3,2,1,0:T(8,128)(2,1)S(1)}, bf16[20,8,32,128]{3,2,1,0:T(8,128)(2,1)S(1)}, bf16[320,512]{1,0:T(8,128)(2,1)S(1)}, bf16[512,512]{1,0:T(8,128)(2,1)S(1)}, bf16[128,1024]{1,0:T(8,128)(2,1)S(1)}) custom-call(bf16[160,128]{1,0:T(8,128)(2,1)S(1)} %get-tuple-element.56.after.own, f32[6,12,24,128]{3,2,1,0:T(8,128)S(1)} %get-tuple-element.57.second, ...), custom_call_target="tpu_custom_call" | custom-call | flops 3000000000 | bytes 1000000 | tf_op jit(solution)/shard_map/pallas_call | solution.py:133
  49.4 0.0 collective-permute-done.5.rest_0_
  49.4 0.0 collective-permute-done.6.rest_1_
  49.4 0.4 collective-permute-done.7.rest_2_
  49.8 2.7 %shard_map.162 = bf16[20,8,32,128]{3,2,1,0:T(8,128)(2,1)} custom-call(bf16[20,8,32,128]{3,2,1,0:T(8,128)(2,1)S(1)} %get-tuple-element.59.field, bf16[4,16,24,128]{3,2,1,0:T(8,128)(2,1)S(1)} %get-tuple-element.60.third, bf16[320,512]{1,0:T(8,128)(2,1)S(1)} %get-tuple-element.61.lift, bf16[512,512]{1,0:T(8,128)(2,1)S(1)} %get-tuple-element.62.regroup, ...), custom_call_target="tpu_custom_call" | custom-call | flops 1000000000 | bytes 1000000 | tf_op jit(solution)/shard_map/pallas_call | solution.py:133
Async XLA Ops:
  0.0 9.3 %copy-start = (bf16[3,27,20,20]{1,3,2,0:T(8,128)(2,1)S(1)}, bf16[3,27,20,20]{1,3,2,0:T(8,128)(2,1)}, u32[]{:S(2)}) copy-start(bf16[3,27,20,20]{1,3,2,0:T(8,128)(2,1)} %param.18) | copy-start | bytes 194404
  3.4 9.7 %collective-permute-start = (bf16[416,128]{1,0:T(8,128)(2,1)S(1)}, bf16[416,128]{1,0:T(8,128)(2,1)S(1)}, u32[]{:S(2)}, u32[]{:S(2)}) collective-permute-start(bf16[416,128]{1,0:T(8,128)(2,1)S(1)} %get-tuple-element.38), channel_id=1, source_target_pairs={{0,1},{1,2},{2,3},{3,0},{4,5},{5,6},{6,7},{7,4},{8,9},{9,10},{10,1... | collective-permute-start | bytes 319496 | tf_op jit(solution)/shard_map/ppermute | solution.py:748
  6.4 6.8 %collective-permute-start.1 = (bf16[416,128]{1,0:T(8,128)(2,1)S(1)}, bf16[416,128]{1,0:T(8,128)(2,1)S(1)}, u32[]{:S(2)}, u32[]{:S(2)}) collective-permute-start(bf16[416,128]{1,0:T(8,128)(2,1)S(1)} %get-tuple-element.39), channel_id=1, source_target_pairs={{0,3},{1,0},{2,1},{3,2},{4,7},{5,4},{6,5},{7,6},{8,11},{9,8},{10,9... | collective-permute-start | bytes 319496 | tf_op jit(solution)/shard_map/ppermute | solution.py:748
  7.4 5.7 %collective-permute-start.2 = (bf16[160,128]{1,0:T(8,128)(2,1)S(1)}, bf16[160,128]{1,0:T(8,128)(2,1)S(1)}, u32[]{:S(2)}, u32[]{:S(2)}) collective-permute-start(bf16[160,128]{1,0:T(8,128)(2,1)S(1)} %get-tuple-element.40), channel_id=1, source_target_pairs={{0,2},{1,3},{2,0},{3,1},{4,6},{5,7},{6,4},{7,5},{8,10},{9,11},{10,... | collective-permute-start | bytes 122888 | tf_op jit(solution)/shard_map/ppermute | solution.py:748
  12.2 0.8 %copy-start.1 = (bf16[20,20]{1,0:T(8,128)(2,1)S(1)}, bf16[20,20]{1,0:T(8,128)(2,1)}, u32[]{:S(2)}) copy-start(bf16[20,20]{1,0:T(8,128)(2,1)} %param.19) | copy-start | bytes 2404
  14.3 12.1 %all-to-all-start = ((bf16[8,5,16,128]{3,2,1,0:T(8,128)(2,1)}), bf16[8,5,16,128]{3,2,1,0:T(8,128)(2,1)S(1)}, u32[]{:S(2)}, u32[]{:S(2)}) async-start(bf16[8,5,16,128]{3,2,1,0:T(8,128)(2,1)} %get-tuple-element.44.after), calls=%async_computation | async-start | bytes 327680 | tf_op jit(solution)/shard_map/all_to_all | solution.py:818
  19.1 4.2 %copy-start.3 = (bf16[3,12,24,128]{3,2,1,0:T(8,128)(2,1)S(1)}, bf16[3,12,24,128]{3,2,1,0:T(8,128)(2,1)}, u32[]{:S(2)}) copy-start(bf16[3,12,24,128]{3,2,1,0:T(8,128)(2,1)} %get-tuple-element.52) | copy-start | bytes 663556
  19.1 4.7 %copy-start.2 = (bf16[3,12,24,128]{3,2,1,0:T(8,128)(2,1)S(1)}, bf16[3,12,24,128]{3,2,1,0:T(8,128)(2,1)}, u32[]{:S(2)}) copy-start(bf16[3,12,24,128]{3,2,1,0:T(8,128)(2,1)} %get-tuple-element.53) | copy-start | bytes 663556
  23.3 12.8 %collective-permute-start.3 = (bf16[3,12,24,128]{3,2,1,0:T(8,128)(2,1)S(1)}, bf16[3,12,24,128]{3,2,1,0:T(8,128)(2,1)S(1)}, u32[]{:S(2)}, u32[]{:S(2)}) collective-permute-start(bf16[3,12,24,128]{3,2,1,0:T(8,128)(2,1)S(1)} %copy-done.3), channel_id=1, source_target_pairs={{0,4},{4,0},{8,12},{12,8},{16,20},{20,16},{24,28},{28,24},{1,5},{5... | collective-permute-start | bytes 663560 | tf_op jit(solution)/shard_map/ppermute | solution.py:855
  23.9 12.3 %collective-permute-start.4 = (bf16[3,12,24,128]{3,2,1,0:T(8,128)(2,1)S(1)}, bf16[3,12,24,128]{3,2,1,0:T(8,128)(2,1)S(1)}, u32[]{:S(2)}, u32[]{:S(2)}) collective-permute-start(bf16[3,12,24,128]{3,2,1,0:T(8,128)(2,1)S(1)} %copy-done.2), channel_id=1, source_target_pairs={{4,8},{12,16},{20,24},{8,4},{16,12},{24,20},{5,9},{13,17},{21,25},... | collective-permute-start | bytes 663560 | tf_op jit(solution)/shard_map/ppermute | solution.py:857
  31.4 12.0 %all-to-all-start.1 = ((bf16[8,5,16,128]{3,2,1,0:T(8,128)(2,1)}), bf16[8,5,16,128]{3,2,1,0:T(8,128)(2,1)S(1)}, u32[]{:S(2)}, u32[]{:S(2)}) async-start(bf16[8,5,16,128]{3,2,1,0:T(8,128)(2,1)} %shard_map.158.after), calls=%async_computation.1 | async-start | bytes 327680 | tf_op jit(solution)/shard_map/all_to_all | solution.py:876
  43.7 5.7 %collective-permute-start.5 = (bf16[160,128]{1,0:T(8,128)(2,1)S(1)}, bf16[160,128]{1,0:T(8,128)(2,1)S(1)}, u32[]{:S(2)}, u32[]{:S(2)}) collective-permute-start(bf16[160,128]{1,0:T(8,128)(2,1)S(1)} %get-tuple-element.64), channel_id=1, source_target_pairs={{0,1},{1,2},{2,3},{3,0},{4,5},{5,6},{6,7},{7,4},{8,9},{9,10},{10,1... | collective-permute-start | bytes 122888 | tf_op jit(solution)/shard_map/ppermute | solution.py:748
  45.0 4.5 %collective-permute-start.6 = (bf16[160,128]{1,0:T(8,128)(2,1)S(1)}, bf16[160,128]{1,0:T(8,128)(2,1)S(1)}, u32[]{:S(2)}, u32[]{:S(2)}) collective-permute-start(bf16[160,128]{1,0:T(8,128)(2,1)S(1)} %get-tuple-element.65), channel_id=1, source_target_pairs={{0,2},{1,3},{2,0},{3,1},{4,6},{5,7},{6,4},{7,5},{8,10},{9,11},{10,... | collective-permute-start | bytes 122888 | tf_op jit(solution)/shard_map/ppermute | solution.py:748
  45.8 4.0 %collective-permute-start.7 = (bf16[160,128]{1,0:T(8,128)(2,1)S(1)}, bf16[160,128]{1,0:T(8,128)(2,1)S(1)}, u32[]{:S(2)}, u32[]{:S(2)}) collective-permute-start(bf16[160,128]{1,0:T(8,128)(2,1)S(1)} %get-tuple-element.66), channel_id=1, source_target_pairs={{0,3},{1,0},{2,1},{3,2},{4,7},{5,4},{6,5},{7,6},{8,11},{9,8},{10,9... | collective-permute-start | bytes 122888 | tf_op jit(solution)/shard_map/ppermute | solution.py:748

commit v7 on v5

--- a/solution.py
+++ b/solution.py
@@ -416,7 +416,7 @@
 
     for copy in copies:
         copy.wait()
-    lax.fori_loop(0, plan.channels, step, 0, unroll=2)
+    lax.fori_loop(0, plan.channels, step, 0, unroll=4)
     lax.fori_loop(0, plan.channels - ready, streamed, 0)
     back = jnp.concatenate(
         [

time: 52.7 us -> 52.7 us (level)
  no operation moved by 1% of the time
where the time goes in v7:
time: 52.7 us; the launch traced here: 52.3 us
  Pallas kernels  27 us (51%)
  starting transfers between devices  20 us (38%)
  waiting for transfers between devices  3.46 us (7%)
  local copies, waits for them, and re-layouts  1.62 us (3%)
    pallas_call x9, Pallas kernels, call(): pl.pallas_call(body, out_shape=outs, in_specs=specs, out_specs=out_specs,...  27 us
    ppermute x6, starting transfers between devices, ring(): lax.ppermute(value, axis, [(i, (i + shift) % count) for i in range(count)])  9.43 us
    all_to_all x1, starting transfers between devices, on_device(): pencil = lax.all_to_all(y_spec, 'gx', 0, 0, tiled=True)  4.88 us
    all_to_all x1, starting transfers between devices, on_device(): line = lax.all_to_all(back, 'gx', 0, 0, tiled=True)  4.5 us
    all_to_all x1, waiting for transfers between devices, on_device(): pencil = lax.all_to_all(y_spec, 'gx', 0, 0, tiled=True)  2.05 us
    all_to_all x1, waiting for transfers between devices, on_device(): line = lax.all_to_all(back, 'gx', 0, 0, tiled=True)  1.28 us
  transfers between devices with their start and end apart: 10, of which 3 were waited for; matrix products, arithmetic and copies ran while one was open for 3% of the time, Pallas kernels for 37%

profile of v7, /device:TPU:0, one launch (start us, length us, event | category | flops | bytes accessed | tf_op | source)
XLA Modules:
  0.0 52.3 jit_solution(17063372871294740773)
XLA Ops:
  0.0 0.0 copy-start
  0.0 3.4 %shard_map.154 = (bf16[160,128]{1,0:T(8,128)(2,1)S(1)}, bf16[416,128]{1,0:T(8,128)(2,1)S(1)}, bf16[416,128]{1,0:T(8,128)(2,1)S(1)}, bf16[160,128]{1,0:T(8,128)(2...) custom-call(bf16[20,8,32,128]{3,2,1,0:T(8,128)(2,1)} %rest_0_.1, ...), custom_call_target="tpu_custom_call" | custom-call | flops 1000000000 | bytes 1000000 | tf_op jit(solution)/shard_map/pallas_call | solution.py:133
  3.4 3.0 %collective-permute-start = (bf16[416,128]{1,0:T(8,128)(2,1)S(1)}, bf16[416,128]{1,0:T(8,128)(2,1)S(1)}, u32[]{:S(2)}, u32[]{:S(2)}) collective-permute-start(bf16[416,128]{1,0:T(8,128)(2,1)S(1)} %get-tuple-element.38), channel_id=1, source_target_pairs={{0,1},{1,2},{2,3},{3,0},{4,5},{5,6},{6,7},{7,4},{8,9},{9,10},{10,1... | collective-permute-start | bytes 319496 | tf_op jit(solution)/shard_map/ppermute | solution.py:748
  6.4 1.0 %collective-permute-start.1 = (bf16[416,128]{1,0:T(8,128)(2,1)S(1)}, bf16[416,128]{1,0:T(8,128)(2,1)S(1)}, u32[]{:S(2)}, u32[]{:S(2)}) collective-permute-start(bf16[416,128]{1,0:T(8,128)(2,1)S(1)} %get-tuple-element.39), channel_id=1, source_target_pairs={{0,3},{1,0},{2,1},{3,2},{4,7},{5,4},{6,5},{7,6},{8,11},{9,8},{10,9... | collective-permute-start | bytes 319496 | tf_op jit(solution)/shard_map/ppermute | solution.py:748
  7.4 1.9 %collective-permute-start.2 = (bf16[160,128]{1,0:T(8,128)(2,1)S(1)}, bf16[160,128]{1,0:T(8,128)(2,1)S(1)}, u32[]{:S(2)}, u32[]{:S(2)}) collective-permute-start(bf16[160,128]{1,0:T(8,128)(2,1)S(1)} %get-tuple-element.40), channel_id=1, source_target_pairs={{0,2},{1,3},{2,0},{3,1},{4,6},{5,7},{6,4},{7,5},{8,10},{9,11},{10,... | collective-permute-start | bytes 122888 | tf_op jit(solution)/shard_map/ppermute | solution.py:748
  9.3 0.0 copy-done
  9.3 0.6 %copy.19 = bf16[3,27,20,20]{3,2,1,0:T(8,128)(2,1)S(1)} copy(bf16[3,27,20,20]{1,3,2,0:T(8,128)(2,1)S(1)} %copy-done) | data formatting | bytes 129600 | tf_op args[2]
  9.9 0.1 pad_bitcast_fusion
  10.1 2.4 %shard_map.155.packed_early = bf16[3,2,20,16,128]{4,3,2,1,0:T(8,128)(2,1)} custom-call(bf16[160,128]{1,0:T(8,128)(2,1)S(1)} %get-tuple-element.37.after.own, f32[2,20,20,2,16,64]{5,4,3,2,1,0:T(8,128)} %weight.5), custom_call_target="tpu_custom_call" | custom-call | flops 1000000000 | bytes 2000000 | tf_op jit(solution)/shard_map/pallas_call | solution.py:133
  12.5 0.0 copy-start.1
  12.5 0.2 copy.25
  12.7 0.6 %reshape.8.filters = bf16[3,72,216]{2,1,0:T(8,128)(2,1)S(1)} reshape(bf16[3,3,24,9,24]{4,3,2,1,0:T(8,128)(2,1)S(1)} %copy.25) | data formatting | bytes 186624 | tf_op jit(solution)/shard_map/reshape | solution.py:824
  13.3 0.0 copy-done.1
  13.3 0.1 copy.21
  13.4 0.0 collective-permute-done.2.rest_0_
  13.4 0.0 collective-permute-done.low_message
  13.4 0.0 collective-permute-done.1.high_message
  13.4 1.1 %shard_map.156 = (bf16[8,5,16,128]{3,2,1,0:T(8,128)(2,1)}, bf16[3,12,24,128]{3,2,1,0:T(8,128)(2,1)}, bf16[3,12,24,128]{3,2,1,0:T(8,128)(2,1)}, bf16[4,12,24,128]{3,2,1,0:T(8,128)(2,1)S(1)}) custom-call(bf16[160,128]{1,0:T(8,128)(2,1)S(1)} %get-tuple-element.37.after.own, bf16[416,128]{1,0:T(8,128)(2,1)S(1)} %collective-permute-done.low_message, ...), custom_call_target="tpu_custom_call" | custom-call | flops 1000000000 | bytes 1000000 | tf_op jit(solution)/shard_map/pallas_call | solution.py:133
  14.5 4.9 %all-to-all-start = ((bf16[8,5,16,128]{3,2,1,0:T(8,128)(2,1)}), bf16[8,5,16,128]{3,2,1,0:T(8,128)(2,1)S(1)}, u32[]{:S(2)}, u32[]{:S(2)}) async-start(bf16[8,5,16,128]{3,2,1,0:T(8,128)(2,1)} %get-tuple-element.44.after), calls=%async_computation | async-start | bytes 327680 | tf_op jit(solution)/shard_map/all_to_all | solution.py:818
  19.4 0.0 copy-start.3
  19.4 0.0 copy-start.2
  19.4 3.9 %shard_map.157 = (bf16[5,2,20,16,128]{4,3,2,1,0:T(8,128)(2,1)}, f32[4,72,1280]{2,1,0:T(8,128)}, bf16[320,512]{1,0:T(8,128)(2,1)}, bf16[1024,256]{1,0:T(8,128)(2,1)S(1)}, bf16[256,1024]{1,0:T(8,128)(2,1)S(1)}) custom-call(bf16[8,5,16,128]{3,2,1,0:T(8,128)(2,1)} %get-tuple-element.44.after, bf16[4,12,24,128]{3,2,1,0:T(8,128)(2,1)S(1)} %get-tuple-element.45.volume, ...), custom_call_target="tpu_custom_call" | custom-call | flops 4000000000 | bytes 8000000 | tf_op jit(solution)/shard_map/pallas_call | solution.py:133
  23.3 0.0 copy-done.3
  23.3 0.6 %collective-permute-start.3 = (bf16[3,12,24,128]{3,2,1,0:T(8,128)(2,1)S(1)}, bf16[3,12,24,128]{3,2,1,0:T(8,128)(2,1)S(1)}, u32[]{:S(2)}, u32[]{:S(2)}) collective-permute-start(bf16[3,12,24,128]{3,2,1,0:T(8,128)(2,1)S(1)} %copy-done.3), channel_id=1, source_target_pairs={{0,4},{4,0},{8,12},{12,8},{16,20},{20,16},{24,28},{28,24},{1,5},{5... | collective-permute-start | bytes 663560 | tf_op jit(solution)/shard_map/ppermute | solution.py:855
  23.9 0.0 copy-done.2
  23.9 0.7 %collective-permute-start.4 = (bf16[3,12,24,128]{3,2,1,0:T(8,128)(2,1)S(1)}, bf16[3,12,24,128]{3,2,1,0:T(8,128)(2,1)S(1)}, u32[]{:S(2)}, u32[]{:S(2)}) collective-permute-start(bf16[3,12,24,128]{3,2,1,0:T(8,128)(2,1)S(1)} %copy-done.2), channel_id=1, source_target_pairs={{4,8},{12,16},{20,24},{8,4},{16,12},{24,20},{5,9},{13,17},{21,25},... | collective-permute-start | bytes 663560 | tf_op jit(solution)/shard_map/ppermute | solution.py:857
  24.6 2.0 %all-to-all-done.pencil = bf16[8,5,16,128]{3,2,1,0:T(8,128)(2,1)S(1)} async-done(((bf16[8,5,16,128]{3,2,1,0:T(8,128)(2,1)}), bf16[8,5,16,128]{3,2,1,0:T(8,128)(2,1)S(1)}, u32[]{:S(2)}, u32[]{:S(2)}) %all-to-all-start) | async-done | bytes 163872 | tf_op jit(solution)/shard_map/all_to_all | solution.py:818
  26.6 5.0 %shard_map.158.after = bf16[8,5,16,128]{3,2,1,0:T(8,128)(2,1)} custom-call(bf16[8,5,16,128]{3,2,1,0:T(8,128)(2,1)S(1)} %all-to-all-done.pencil, bf16[1024,256]{1,0:T(8,128)(2,1)S(1)} %get-tuple-element.46.forward, bf16[3,2,20,16,128]{4,3,2,1,0:T(8,128)(2,1)} %shard_map.155.packed_early, bf16[5,2,20,16,128]{4,3,2,1,0:T(8,128)(2,1)} %get-tuple-element.47.packed_late, ...), custom_call_target="tpu_custom_call" | custom-call | flops 1000000000 | bytes 1000000 | tf_op jit(solution)/shard_map/pallas_call | solution.py:133
  31.7 4.5 %all-to-all-start.1 = ((bf16[8,5,16,128]{3,2,1,0:T(8,128)(2,1)}), bf16[8,5,16,128]{3,2,1,0:T(8,128)(2,1)S(1)}, u32[]{:S(2)}, u32[]{:S(2)}) async-start(bf16[8,5,16,128]{3,2,1,0:T(8,128)(2,1)} %shard_map.158.after), calls=%async_computation.1 | async-start | bytes 327680 | tf_op jit(solution)/shard_map/all_to_all | solution.py:876
  36.2 0.0 collective-permute-done.3.near
  36.2 0.0 collective-permute-done.4.far
  36.2 5.9 %shard_map.159 = (f32[6,12,24,128]{3,2,1,0:T(8,128)S(1)}, bf16[128,256]{1,0:T(8,128)(2,1)S(1)}, bf16[128,128]{1,0:T(8,128)(2,1)S(1)}) custom-call(bf16[8,5,16,128]{3,2,1,0:T(8,128)(2,1)} %shard_map.158.after, bf16[3,12,24,128]{3,2,1,0:T(8,128)(2,1)S(1)} %collective-permute-done.3.near, bf16[3,12,24,128]{3,2,1,0:T(8,128)(2,1)S(1)} %collective-permute-done.4.far, ...), custom_call_target="tpu_custom_call" | custom-call | flops 6000000000 | bytes 1000000 | tf_op jit(solution)/shard_map/pallas_call | solution.py:133
  42.1 1.3 %all-to-all-done.1.line = bf16[8,5,16,128]{3,2,1,0:T(8,128)(2,1)S(1)} async-done(((bf16[8,5,16,128]{3,2,1,0:T(8,128)(2,1)}), bf16[8,5,16,128]{3,2,1,0:T(8,128)(2,1)S(1)}, u32[]{:S(2)}, u32[]{:S(2)}) %all-to-all-start.1) | async-done | bytes 163872 | tf_op jit(solution)/shard_map/all_to_all | solution.py:876
  43.4 0.4 shard_map.160
  43.8 1.0 %collective-permute-start.5 = (bf16[160,128]{1,0:T(8,128)(2,1)S(1)}, bf16[160,128]{1,0:T(8,128)(2,1)S(1)}, u32[]{:S(2)}, u32[]{:S(2)}) collective-permute-start(bf16[160,128]{1,0:T(8,128)(2,1)S(1)} %get-tuple-element.64), channel_id=1, source_target_pairs={{0,1},{1,2},{2,3},{3,0},{4,5},{5,6},{6,7},{7,4},{8,9},{9,10},{10,1... | collective-permute-start | bytes 122888 | tf_op jit(solution)/shard_map/ppermute | solution.py:748
  44.7 0.9 %collective-permute-start.6 = (bf16[160,128]{1,0:T(8,128)(2,1)S(1)}, bf16[160,128]{1,0:T(8,128)(2,1)S(1)}, u32[]{:S(2)}, u32[]{:S(2)}) collective-permute-start(bf16[160,128]{1,0:T(8,128)(2,1)S(1)} %get-tuple-element.65), channel_id=1, source_target_pairs={{0,2},{1,3},{2,0},{3,1},{4,6},{5,7},{6,4},{7,5},{8,10},{9,11},{10,... | collective-permute-start | bytes 122888 | tf_op jit(solution)/shard_map/ppermute | solution.py:748
  45.6 1.7 %collective-permute-start.7 = (bf16[160,128]{1,0:T(8,128)(2,1)S(1)}, bf16[160,128]{1,0:T(8,128)(2,1)S(1)}, u32[]{:S(2)}, u32[]{:S(2)}) collective-permute-start(bf16[160,128]{1,0:T(8,128)(2,1)S(1)} %get-tuple-element.66), channel_id=1, source_target_pairs={{0,3},{1,0},{2,1},{3,2},{4,7},{5,4},{6,5},{7,6},{8,11},{9,8},{10,9... | collective-permute-start | bytes 122888 | tf_op jit(solution)/shard_map/ppermute | solution.py:748
  47.2 2.2 %shard_map.161 = (bf16[4,16,24,128]{3,2,1,0:T(8,128)(2,1)S(1)}, bf16[20,8,32,128]{3,2,1,0:T(8,128)(2,1)S(1)}, bf16[320,512]{1,0:T(8,128)(2,1)S(1)}, bf16[512,512]{1,0:T(8,128)(2,1)S(1)}, bf16[128,1024]{1,0:T(8,128)(2,1)S(1)}) custom-call(bf16[160,128]{1,0:T(8,128)(2,1)S(1)} %get-tuple-element.56.after.own, f32[6,12,24,128]{3,2,1,0:T(8,128)S(1)} %get-tuple-element.57.second, ...), custom_call_target="tpu_custom_call" | custom-call | flops 3000000000 | bytes 1000000 | tf_op jit(solution)/shard_map/pallas_call | solution.py:133
  49.4 0.0 collective-permute-done.5.rest_0_
  49.4 0.0 collective-permute-done.6.rest_1_
  49.5 0.1 collective-permute-done.7.rest_2_
  49.6 2.7 %shard_map.162 = bf16[20,8,32,128]{3,2,1,0:T(8,128)(2,1)} custom-call(bf16[20,8,32,128]{3,2,1,0:T(8,128)(2,1)S(1)} %get-tuple-element.59.field, bf16[4,16,24,128]{3,2,1,0:T(8,128)(2,1)S(1)} %get-tuple-element.60.third, bf16[320,512]{1,0:T(8,128)(2,1)S(1)} %get-tuple-element.61.lift, bf16[512,512]{1,0:T(8,128)(2,1)S(1)} %get-tuple-element.62.regroup, ...), custom_call_target="tpu_custom_call" | custom-call | flops 1000000000 | bytes 1000000 | tf_op jit(solution)/shard_map/pallas_call | solution.py:133
Async XLA Ops:
  0.0 9.3 %copy-start = (bf16[3,27,20,20]{1,3,2,0:T(8,128)(2,1)S(1)}, bf16[3,27,20,20]{1,3,2,0:T(8,128)(2,1)}, u32[]{:S(2)}) copy-start(bf16[3,27,20,20]{1,3,2,0:T(8,128)(2,1)} %param.18) | copy-start | bytes 194404
  3.4 10.0 %collective-permute-start = (bf16[416,128]{1,0:T(8,128)(2,1)S(1)}, bf16[416,128]{1,0:T(8,128)(2,1)S(1)}, u32[]{:S(2)}, u32[]{:S(2)}) collective-permute-start(bf16[416,128]{1,0:T(8,128)(2,1)S(1)} %get-tuple-element.38), channel_id=1, source_target_pairs={{0,1},{1,2},{2,3},{3,0},{4,5},{5,6},{6,7},{7,4},{8,9},{9,10},{10,1... | collective-permute-start | bytes 319496 | tf_op jit(solution)/shard_map/ppermute | solution.py:748
  6.4 7.0 %collective-permute-start.1 = (bf16[416,128]{1,0:T(8,128)(2,1)S(1)}, bf16[416,128]{1,0:T(8,128)(2,1)S(1)}, u32[]{:S(2)}, u32[]{:S(2)}) collective-permute-start(bf16[416,128]{1,0:T(8,128)(2,1)S(1)} %get-tuple-element.39), channel_id=1, source_target_pairs={{0,3},{1,0},{2,1},{3,2},{4,7},{5,4},{6,5},{7,6},{8,11},{9,8},{10,9... | collective-permute-start | bytes 319496 | tf_op jit(solution)/shard_map/ppermute | solution.py:748
  7.4 6.0 %collective-permute-start.2 = (bf16[160,128]{1,0:T(8,128)(2,1)S(1)}, bf16[160,128]{1,0:T(8,128)(2,1)S(1)}, u32[]{:S(2)}, u32[]{:S(2)}) collective-permute-start(bf16[160,128]{1,0:T(8,128)(2,1)S(1)} %get-tuple-element.40), channel_id=1, source_target_pairs={{0,2},{1,3},{2,0},{3,1},{4,6},{5,7},{6,4},{7,5},{8,10},{9,11},{10,... | collective-permute-start | bytes 122888 | tf_op jit(solution)/shard_map/ppermute | solution.py:748
  12.5 0.8 %copy-start.1 = (bf16[20,20]{1,0:T(8,128)(2,1)S(1)}, bf16[20,20]{1,0:T(8,128)(2,1)}, u32[]{:S(2)}) copy-start(bf16[20,20]{1,0:T(8,128)(2,1)} %param.19) | copy-start | bytes 2404
  14.5 12.1 %all-to-all-start = ((bf16[8,5,16,128]{3,2,1,0:T(8,128)(2,1)}), bf16[8,5,16,128]{3,2,1,0:T(8,128)(2,1)S(1)}, u32[]{:S(2)}, u32[]{:S(2)}) async-start(bf16[8,5,16,128]{3,2,1,0:T(8,128)(2,1)} %get-tuple-element.44.after), calls=%async_computation | async-start | bytes 327680 | tf_op jit(solution)/shard_map/all_to_all | solution.py:818
  19.4 3.9 %copy-start.3 = (bf16[3,12,24,128]{3,2,1,0:T(8,128)(2,1)S(1)}, bf16[3,12,24,128]{3,2,1,0:T(8,128)(2,1)}, u32[]{:S(2)}) copy-start(bf16[3,12,24,128]{3,2,1,0:T(8,128)(2,1)} %get-tuple-element.52) | copy-start | bytes 663556
  19.4 4.5 %copy-start.2 = (bf16[3,12,24,128]{3,2,1,0:T(8,128)(2,1)S(1)}, bf16[3,12,24,128]{3,2,1,0:T(8,128)(2,1)}, u32[]{:S(2)}) copy-start(bf16[3,12,24,128]{3,2,1,0:T(8,128)(2,1)} %get-tuple-element.53) | copy-start | bytes 663556
  23.3 12.8 %collective-permute-start.3 = (bf16[3,12,24,128]{3,2,1,0:T(8,128)(2,1)S(1)}, bf16[3,12,24,128]{3,2,1,0:T(8,128)(2,1)S(1)}, u32[]{:S(2)}, u32[]{:S(2)}) collective-permute-start(bf16[3,12,24,128]{3,2,1,0:T(8,128)(2,1)S(1)} %copy-done.3), channel_id=1, source_target_pairs={{0,4},{4,0},{8,12},{12,8},{16,20},{20,16},{24,28},{28,24},{1,5},{5... | collective-permute-start | bytes 663560 | tf_op jit(solution)/shard_map/ppermute | solution.py:855
  23.9 12.3 %collective-permute-start.4 = (bf16[3,12,24,128]{3,2,1,0:T(8,128)(2,1)S(1)}, bf16[3,12,24,128]{3,2,1,0:T(8,128)(2,1)S(1)}, u32[]{:S(2)}, u32[]{:S(2)}) collective-permute-start(bf16[3,12,24,128]{3,2,1,0:T(8,128)(2,1)S(1)} %copy-done.2), channel_id=1, source_target_pairs={{4,8},{12,16},{20,24},{8,4},{16,12},{24,20},{5,9},{13,17},{21,25},... | collective-permute-start | bytes 663560 | tf_op jit(solution)/shard_map/ppermute | solution.py:857
  31.7 11.7 %all-to-all-start.1 = ((bf16[8,5,16,128]{3,2,1,0:T(8,128)(2,1)}), bf16[8,5,16,128]{3,2,1,0:T(8,128)(2,1)S(1)}, u32[]{:S(2)}, u32[]{:S(2)}) async-start(bf16[8,5,16,128]{3,2,1,0:T(8,128)(2,1)} %shard_map.158.after), calls=%async_computation.1 | async-start | bytes 327680 | tf_op jit(solution)/shard_map/all_to_all | solution.py:876
  43.8 5.7 %collective-permute-start.5 = (bf16[160,128]{1,0:T(8,128)(2,1)S(1)}, bf16[160,128]{1,0:T(8,128)(2,1)S(1)}, u32[]{:S(2)}, u32[]{:S(2)}) collective-permute-start(bf16[160,128]{1,0:T(8,128)(2,1)S(1)} %get-tuple-element.64), channel_id=1, source_target_pairs={{0,1},{1,2},{2,3},{3,0},{4,5},{5,6},{6,7},{7,4},{8,9},{9,10},{10,1... | collective-permute-start | bytes 122888 | tf_op jit(solution)/shard_map/ppermute | solution.py:748
  44.7 4.7 %collective-permute-start.6 = (bf16[160,128]{1,0:T(8,128)(2,1)S(1)}, bf16[160,128]{1,0:T(8,128)(2,1)S(1)}, u32[]{:S(2)}, u32[]{:S(2)}) collective-permute-start(bf16[160,128]{1,0:T(8,128)(2,1)S(1)} %get-tuple-element.65), channel_id=1, source_target_pairs={{0,2},{1,3},{2,0},{3,1},{4,6},{5,7},{6,4},{7,5},{8,10},{9,11},{10,... | collective-permute-start | bytes 122888 | tf_op jit(solution)/shard_map/ppermute | solution.py:748
  45.6 4.0 %collective-permute-start.7 = (bf16[160,128]{1,0:T(8,128)(2,1)S(1)}, bf16[160,128]{1,0:T(8,128)(2,1)S(1)}, u32[]{:S(2)}, u32[]{:S(2)}) collective-permute-start(bf16[160,128]{1,0:T(8,128)(2,1)S(1)} %get-tuple-element.66), channel_id=1, source_target_pairs={{0,3},{1,0},{2,1},{3,2},{4,7},{5,4},{6,5},{7,6},{8,11},{9,8},{10,9... | collective-permute-start | bytes 122888 | tf_op jit(solution)/shard_map/ppermute | solution.py:748
